TPU v7x, 32 devices: a whole 2x2x4 slice. The times are simulated.
32 devices in a mesh: row: 8 (over z, x), col: 4 (over y, core).
Axes of the slice: x: 2, y: 2, z: 4, core: 2. Of those that a mesh axis runs over, the one named last changes fastest.
Arguments:
- recorded: float32 [2, 2, 4096, 4096], P(None, None, 'row', 'col'), may hold values from -1.1 to 1.1, as said below
Outputs:
- multiples: float32 [2, 2, 4096, 4096], P(None, None, 'row', 'col')
Inputs may be any that keep to these rules, and one draw needn't show every extreme that they name: Every frequency slice is reciprocal: recorded[c, f, s, r] = recorded[c, f, r, s] for both parts c.
All inputs are finite; a program needn't handle non-finite values.
Results may differ from a plain program's by a relative error of at most 0.00011.
Values sent between devices are 32-bit elements; how exact they have to be, the bound alone decides.
No kernel may reach another device: no remote copies, remote signals or barrier semaphores. Data moves between devices by JAX's collectives and lax.ppermute only.
A program may use at most 192 MiB of HBM per device.

v0:
```python
import jax
import jax.numpy as jnp
from jax import lax
from jax.sharding import PartitionSpec as P


def product(left, right):
    return jnp.einsum(
        "fik,fkj->fij",
        left,
        right,
        precision=lax.Precision.HIGHEST,
        preferred_element_type=jnp.float32,
    )


def body(recorded):
    panel_rows = lax.all_gather(recorded, "col", axis=3, tiled=True)
    pieces = lax.all_gather(recorded, "row", axis=2, tiled=True)
    real_part = product(panel_rows[0], pieces[0]) - product(panel_rows[1], pieces[1])
    imag_part = product(panel_rows[0], pieces[1]) + product(panel_rows[1], pieces[0])
    real_part, imag_part = (real_part, imag_part)
    return -jnp.stack([real_part, imag_part])


def solution(mesh):
    in_specs = (P(None, None, "row", "col"),)
    out_specs = P(None, None, "row", "col")
    return jax.shard_map(body, mesh=mesh, in_specs=in_specs, out_specs=out_specs, check_vma=False)
```

profile of v0, /device:TPU:16, one launch (start us, length us, event | category | flops | bytes accessed | tf_op | source)
XLA Modules:
  0.0 1743.3 jit_solution(15805430828804374967)
XLA Ops:
  6.5 0.0 all-gather.3.cloned.1.call-start
  6.5 0.7 all-gather.3.cloned.1.call-update
  7.3 0.0 all-gather.5.cloned.1.call-start
  7.3 0.7 all-gather.5.cloned.1.call-update
  8.0 203.6 %all-gather.3.cloned.1.call-done = f32[2,2,512,4096]{3,2,1,0:T(8,128)} async-done(((f32[2,2,512,1024]{3,2,1,0:T(8,128)}), f32[2,2,512,4096]{3,2,1,0:T(8,128)}) %all-gather.3.cloned.1.call-update) | async-done | bytes 33554448 | tf_op jit(solution)/shard_map/all_gather | solution.py:18
  211.6 1268.5 %all-gather.5.cloned.1.call-done = f32[2,2,4096,1024]{3,2,1,0:T(8,128)} async-done(((f32[2,2,512,1024]{3,2,1,0:T(8,128)}), f32[2,2,4096,1024]{3,2,1,0:T(8,128)}) %all-gather.5.cloned.1.call-update) | async-done | bytes 67108880 | tf_op jit(solution)/shard_map/all_gather | solution.py:19
  1480.0 59.4 %fusion = f32[2,512,1024]{2,1,0:T(8,128)} fusion(f32[2,2,4096,1024]{3,2,1,0:T(8,128)} %all-gather.5.cloned.1.call-done, f32[2,2,512,4096]{3,2,1,0:T(8,128)} %all-gather.3.cloned.1.call-done), kind=kOutput, calls=%fused_computation.2 | convolution fusion | flops 51539607552 | bytes 54525952 | tf_op jit(solution)/shard_map/fik,fkj->fij/dot_general | solution.py:8
  1539.5 59.5 %fusion.1 = f32[2,512,1024]{2,1,0:T(8,128)} fusion(f32[2,2,4096,1024]{3,2,1,0:T(8,128)} %all-gather.5.cloned.1.call-done, f32[2,2,512,4096]{3,2,1,0:T(8,128)} %all-gather.3.cloned.1.call-done), kind=kOutput, calls=%fused_computation.3 | convolution fusion | flops 51539607552 | bytes 54525952 | tf_op jit(solution)/shard_map/fik,fkj->fij/dot_general | solution.py:8
  1598.9 64.3 %add_bitcast_fusion = f32[1,2,512,1024]{3,2,1,0:T(8,128)} fusion(f32[2,512,1024]{2,1,0:T(8,128)} %fusion, f32[2,2,4096,1024]{3,2,1,0:T(8,128)} %all-gather.5.cloned.1.call-done, f32[2,2,512,4096]{3,2,1,0:T(8,128)} %all-gather.3.cloned.1.call-done), kind=kOutput, calls=%fused_computation.9 | convolution fusion | flops 51540656128 | bytes 58720256 | tf_op jit(solution)/shard_map/fik,fkj->fij/dot_general | solution.py:8
  1663.2 64.4 %subtract_bitcast_fusion = f32[1,2,512,1024]{3,2,1,0:T(8,128)} fusion(f32[2,512,1024]{2,1,0:T(8,128)} %fusion.1, f32[2,2,4096,1024]{3,2,1,0:T(8,128)} %all-gather.5.cloned.1.call-done, f32[2,2,512,4096]{3,2,1,0:T(8,128)} %all-gather.3.cloned.1.call-done), kind=kOutput, calls=%fused_computation.10 | convolution fusion | flops 51540656128 | bytes 58720256 | tf_op jit(solution)/shard_map/fik,fkj->fij/dot_general | solution.py:8
  1727.6 8.8 maximum_negate_fusion
Async XLA Ops:
  6.5 205.0 %all-gather.3.cloned.1.call-start = ((), (), s32[]{:S(2)}) async-start(), calls=%async_computation | async-start | bytes 41943040 | tf_op jit(solution)/shard_map/all_gather | solution.py:18
  7.3 1472.8 %all-gather.5.cloned.1.call-start = ((), (), s32[]{:S(2)}) async-start(), calls=%async_computation.1 | async-start | bytes 75497472 | tf_op jit(solution)/shard_map/all_gather | solution.py:19
Sparse Core Ops, SparseCore 0:
  8.9 202.5 all-gather.2
  213.1 1266.8 all-gather.4
where the time goes:
time: 1750 us; the launch traced here: 1740 us
  waiting for transfers between devices  1470 us (84%)
  matrix products  248 us (14%)
    all_gather x1, waiting for transfers between devices, body(): pieces = lax.all_gather(recorded, 'row', axis=2, tiled=True)  1270 us
    dot_general x4, matrix products, product(): jnp.einsum('fik,fkj->fij', left, right, precision=lax.Precision.HIGHEST,...  248 us
    all_gather x1, waiting for transfers between devices, body(): panel_rows = lax.all_gather(recorded, 'col', axis=3, tiled=True)  204 us
  transfers between devices with their start and end apart: 2, of which 2 were waited for; matrix products, arithmetic and copies ran while one was open for 0% of the time, Pallas kernels for 0%

commit v1 on v0

v1 whole, which is shorter than its diff:
```python
import functools

import jax
import jax.numpy as jnp
from jax import lax
from jax.experimental import pallas as pl
from jax.experimental.pallas import tpu as pltpu
from jax.sharding import PartitionSpec as P

AXES = ("row", "col")
CHUNKS = 4


def dot(left, right):
    return jnp.dot(left, right, precision=lax.Precision.HIGH, preferred_element_type=jnp.float32)


def multiply(left, right):
    rr, ii = dot(left[0], right[0]), dot(left[1], right[1])
    ss = dot(left[0] + left[1], right[0] + right[1])
    return jnp.stack([rr - ii, ss - rr - ii])


def gathered(recorded):
    rows = lax.all_gather(recorded, "col", axis=3, tiled=True)
    columns = lax.all_gather(recorded, "row", axis=2, tiled=True)
    out = [multiply(rows[:, f], columns[:, f]) for f in range(recorded.shape[1])]
    return -jnp.stack(out, axis=1)


def split(value):
    high = value.astype(jnp.bfloat16)
    return high, (value - high.astype(jnp.float32)).astype(jnp.bfloat16)


def split_into(out, at, block, rows=slice(None)):
    k = block[0].shape[1]
    for c in range(3):
        v = block[c] if c < 2 else block[0] + block[1]
        out[2 * c, rows, at : at + k], out[2 * c + 1, rows, at : at + k] = split(v)


def split_kernel(*refs):
    at = 0
    for ref in refs[:-1]:
        split_into(refs[-1], at, ref)
        at += ref.shape[2]


def split_blocks(blocks):
    rows, ks = blocks[0].shape[1], [v.shape[2] for v in blocks]
    mb = rows // CHUNKS
    return pl.pallas_call(
        split_kernel,
        grid=(rows // mb,),
        in_specs=[pl.BlockSpec((2, mb, k), lambda i: (0, i, 0)) for k in ks],
        out_specs=pl.BlockSpec((6, mb, sum(ks)), lambda i: (0, i, 0)),
        out_shape=jax.ShapeDtypeStruct((6, rows, sum(ks)), jnp.bfloat16),
        compiler_params=pltpu.CompilerParams(vmem_limit_bytes=56 * 2**20),
        cost_estimate=pl.CostEstimate(flops=1000, bytes_accessed=1000, transcendentals=0),
    )(*blocks)


def product_kernel(role_ref, *refs, picks, lefts, rights, more, halves, fetch):
    left, candidates, rest = refs[:lefts], refs[lefts : lefts + rights], refs[lefts + rights :]
    base, rest = (rest[0], rest[1:]) if more else (None, rest)
    outs, rest = rest[:halves], rest[halves:]
    scratch = rest[0]
    j, i = pl.program_id(0), pl.program_id(1)
    for role, steps in picks.items():
        for step, pieces in enumerate(steps):

            @pl.when((role_ref[0] == role) & (i == 0) & (j == step))
            def _():
                if fetch:
                    staged, sems = rest[-2:]
                    at, copies = 0, []
                    for which, start, size, _, _, _ in pieces:
                        source = candidates[which].at[:, pl.ds(start, size), :]
                        copies.append(
                            pltpu.make_async_copy(source, staged.at[:, pl.ds(at, size), :], sems.at[len(copies)])
                        )
                        copies[-1].start()
                        at += size
                    at = 0
                for number, (which, start, size, flip, row, col) in enumerate(pieces):
                    if fetch:
                        copies[number].wait()
                        block = [staged[c, at : at + size, :] for c in range(2)]
                        at += size
                    else:
                        block = [candidates[which][c, start : start + size, :] for c in range(2)]
                    if flip:
                        block = [v.T for v in block]
                    split_into(scratch, col, block, slice(row, row + block[0].shape[0]))

    @pl.when(functools.reduce(jnp.logical_or, [role_ref[0] == role for role in picks]))
    def _():
        if lefts == 1:
            parts = multiply_split(left[0], slice(None), scratch)
        else:
            held = rest[1]
            mb = left[0].shape[1]
            rows = pl.ds(pl.multiple_of(i * mb, mb), mb)

            @pl.when(j == 0)
            def _():
                at = 0
                for ref in left:
                    split_into(held, at, ref, rows)
                    at += ref.shape[2]

            parts = multiply_split(held, rows, scratch)
        for h, out in enumerate(outs):

            @pl.when(i * halves // pl.num_programs(1) == h)
            def _():
                for c in range(2):
                    out[c] = parts[c] if base is None else parts[c] + base[c]


def multiply_split(left, rows, right):
    parts = []
    for c in range(3):
        high, low = left[2 * c, rows, :], left[2 * c + 1, rows, :]
        total = jnp.dot(high, right[2 * c], preferred_element_type=jnp.float32)
        total += jnp.dot(high, right[2 * c + 1], preferred_element_type=jnp.float32)
        total += jnp.dot(low, right[2 * c], preferred_element_type=jnp.float32)
        parts.append(total)
    rr, ii, ss = parts
    return rr - ii, ss - rr - ii


def product(role, left, rights, picks, columns, base=None, half=None, halves=1, fetch=False):
    split_left = not isinstance(left, list)
    lefts = [left] if split_left else left
    rows = lefts[0].shape[1]
    depth = sum(v.shape[2] for v in lefts) // (1 if half is None else 2)
    mb, nb = rows // CHUNKS, min(columns, rows // 2)
    once = pl.Buffered(1)

    def on(r):
        return functools.reduce(jnp.maximum, [jnp.where(r[0] == role_, 1, 0) for role_ in picks])

    if split_left:
        in_specs = [pl.BlockSpec((6, mb, depth), lambda j, i, r: (0, i * on(r), half or 0))]
    else:
        last = rows // mb - 1
        in_specs = [
            pl.BlockSpec((2, mb, v.shape[2]), lambda j, i, r: (0, jnp.where(j == 0, i, last) * on(r), 0)) for v in lefts
        ]
    arrays = []
    for v in rights:
        if fetch:
            arrays.append(v)
            spec = pl.BlockSpec(memory_space=pl.ANY)
        elif isinstance(v, tuple):
            arrays.append(v[0])
            spec = pl.BlockSpec((2, nb, v[0].shape[2]), lambda j, i, r: (0, j * on(r), 0), pipeline_mode=once)
        else:
            arrays.append(v)
            spec = pl.BlockSpec(v.shape, lambda j, i, r: (0, 0, 0), pipeline_mode=once)
        in_specs.append(spec)
    args = lefts + arrays
    if base is not None:
        in_specs.append(pl.BlockSpec((2, mb, nb), lambda j, i, r: (0, i * on(r), j * on(r))))
        args.append(base)
    scratch = [pltpu.VMEM((6, depth, nb), jnp.bfloat16)]
    if not split_left:
        scratch.append(pltpu.VMEM((6, rows, depth), jnp.bfloat16))
    if fetch:
        every = [pieces for steps in picks.values() for pieces in steps]
        scratch.append(pltpu.VMEM((2, max(sum(e[2] for e in v) for v in every), nb), jnp.float32))
        scratch.append(pltpu.SemaphoreType.DMA((max(len(v) for v in every),)))
    body = functools.partial(
        product_kernel, picks=picks, lefts=len(lefts), rights=len(rights), more=base is not None, halves=halves, fetch=fetch
    )
    steps = rows // mb // halves
    out_specs = [
        pl.BlockSpec((2, mb, nb), lambda j, i, r, h=h: (0, jnp.clip(i - h * steps, 0, steps - 1) * on(r), j * on(r)))
        for h in range(halves)
    ]
    out_shape = [jax.ShapeDtypeStruct((2, rows // halves, columns), jnp.float32)] * halves
    result = pl.pallas_call(
        body,
        grid_spec=pltpu.PrefetchScalarGridSpec(
            num_scalar_prefetch=1,
            grid=(columns // nb, rows // mb),
            in_specs=in_specs,
            out_specs=out_specs,
            scratch_shapes=scratch,
        ),
        out_shape=out_shape,
        compiler_params=pltpu.CompilerParams(vmem_limit_bytes=58 * 2**20),
        cost_estimate=pl.CostEstimate(flops=1000, bytes_accessed=1000, transcendentals=0),
    )(role, *args)
    return result[0] if halves == 1 else tuple(result)


def place_kernel(role_ref, *refs):
    (totals, gots, tops, crossed), out = (refs[:2], refs[2:4], refs[4:8], refs[8:12]), refs[12]
    f, j = pl.program_id(0), pl.program_id(1)
    kept = role_ref[1] == f
    for sources, flag in ((totals, kept), (gots, jnp.logical_not(kept))):
        for role, ref in enumerate(sources):

            @pl.when(flag & (role_ref[0] == role))
            def _():
                out[:, 0] = -ref[...]

    for sources, flag in ((tops, kept), (crossed, jnp.logical_not(kept))):
        for step, ref in enumerate(sources):

            @pl.when(flag & (role_ref[0] >= 2) & (j == step))
            def _():
                out[:, 0] = -ref[...]


def place(role, totals, gots, tops, crossed):
    _, rows, columns = totals[0].shape
    w = columns // CHUNKS
    in_specs = [
        pl.BlockSpec((2, rows, w), lambda f, j, r, k=k: (0, 0, j * jnp.where(r[0] == k, 1, 0))) for k in (0, 1, 0, 1)
    ] + [pl.BlockSpec((2, rows, w), lambda f, j, r: (0, 0, 0))] * 8
    return pl.pallas_call(
        place_kernel,
        grid_spec=pltpu.PrefetchScalarGridSpec(
            num_scalar_prefetch=1,
            grid=(2, CHUNKS),
            in_specs=in_specs,
            out_specs=pl.BlockSpec((2, 1, rows, w), lambda f, j, r: (0, f, 0, (j + 2 * f) % CHUNKS)),
        ),
        out_shape=jax.ShapeDtypeStruct((2, 2, rows, columns), jnp.float32),
        compiler_params=pltpu.CompilerParams(vmem_limit_bytes=56 * 2**20),
        cost_estimate=pl.CostEstimate(flops=1000, bytes_accessed=1000, transcendentals=0),
    )(role, *totals, *gots, *tops, *crossed)


def blocked(recorded):
    row, col = lax.axis_index("row"), lax.axis_index("col")
    z, x, y, c = row // 2, row % 2, col // 2, col % 2
    half, p = z // 2, z % 2
    diag, first, lane = y == half, c == p, c == half
    at_end = (z == 0) | (z == 3)
    role = jnp.where(diag, jnp.where(first, 0, 1), jnp.where(lane, 3, 2)).astype(jnp.int32)
    roles = jnp.reshape(role, (1,))
    part, width = recorded.shape[2], recorded.shape[3]
    w, n = width // CHUNKS, width

    def send(value, *moves):
        pairs = []
        for zz in range(4):
            for xx in range(2):
                for yy in range(2):
                    for cc in range(2):
                        for move in moves:
                            to = move(zz, xx, yy, cc)
                            if to is not None:
                                a, b, d, e = to
                                pairs.append((((zz * 2 + xx) * 2 + yy) * 2 + cc, ((a * 2 + b) * 2 + d) * 2 + e))
        return lax.ppermute(value, AXES, pairs)

    def on_diag(zz, yy):
        return yy == zz // 2

    swap_x = lambda a, b, d, e: (a, 1 - b, d, e)
    swap_y = lambda a, b, d, e: (a, b, 1 - d, e)
    swap_core = lambda a, b, d, e: (a, b, d, 1 - e)
    swap_core_diag = lambda a, b, d, e: (a, b, d, 1 - e) if on_diag(a, d) else None
    to_diag = lambda a, b, d, e: None if on_diag(a, d) else (a, b, 1 - d, e)
    to_off = lambda a, b, d, e: (a, b, 1 - d, e) if on_diag(a, d) else None
    swap_slab = lambda a, b, d, e: (a ^ 1, b, d, e) if on_diag(a, d) else None
    first_to_slab = lambda a, b, d, e: (a ^ 1, b, d, e) if on_diag(a, d) and e == a % 2 else None
    over_middle = lambda a, b, d, e: (3 - a, b, d, e) if on_diag(a, d) and a in (1, 2) else None
    middle_second = lambda a, b, d, e: (3 - a, b, d, e) if on_diag(a, d) and a in (1, 2) and e != a % 2 else None
    outward = lambda a, b, d, e: {1: (0, b, d, e), 2: (3, b, d, e)}.get(a) if not on_diag(a, d) else None
    outward_second = lambda a, b, d, e: outward(a, b, d, e) if e != a // 2 else None
    x_first = lambda a, b, d, e: (a, 1 - b, d, e) if on_diag(a, d) and e == a % 2 else None
    x_second = lambda a, b, d, e: (a, 1 - b, d, e) if on_diag(a, d) and e != a % 2 else None
    x_off = lambda a, b, d, e: None if on_diag(a, d) else (a, 1 - b, d, e)

    pick = jnp.where
    sync = lambda *values: lax.optimization_barrier(values)
    mid_off = jnp.logical_not(diag | at_end)

    def cut(f, j):
        start = (j * w + f * part) % width
        return lax.dynamic_slice(recorded, (0, f, 0, start), (2, 1, part, 2 * w))[:, 0]

    def chunk(value, j):
        return value[:, :, j * w : (j + 1) * w]

    mine, give = [cut(x, 0), cut(x, 2)], [cut(1 - x, 0), cut(1 - x, 2)]
    got = send(give[0], swap_x)
    own01 = jnp.concatenate([mine[0], got], 1)
    own = [chunk(own01, 0), chunk(own01, 1)]
    lows = jnp.concatenate([own[0], own[1][:, w:]], 1)
    own01, own[0], own[1], lows, give[1] = sync(own01, own[0], own[1], lows, give[1])

    right, there, seen, cores, seen_cores = [None] * 4, [None] * 4, [None] * 4, [None] * 4, [None] * 4
    got = send(give[1], swap_x)
    right[0] = send(own[0], to_diag, over_middle)
    low01 = send(lows, first_to_slab)
    core01 = send(own01, swap_core)
    own23 = jnp.concatenate([mine[1], got], 1)
    own += [chunk(own23, 0), chunk(own23, 1)]
    lows23 = jnp.concatenate([own[2][:, 2 * w :], own[3][:, 3 * w :]], 1)
    mixed = pick(diag & first, jnp.concatenate([own[1][:, w:], own[3][:, 3 * w :]], 1), own[1])
    own23, own[2], own[3], lows23, mixed, right[0], low01, core01 = sync(
        own23, own[2], own[3], lows23, mixed, right[0], low01, core01
    )
    core23 = send(own23, swap_core)
    core23, own[3], lows23, mixed, right[0] = sync(core23, own[3], lows23, mixed, right[0])

    def whole(which, k, row, transposed=False):
        return (which, 0, k, transposed, row, 0)

    def lower(sources, j, row, col):
        out = [(sources[i][0], sources[i][1] + (j - i) * w, w, True, row + i * w, col) for i in range(j)]
        return out + [(sources[j][0], sources[j][1], n - j * w, False, row + j * w, col)]

    there[0] = send(right[0], swap_slab, outward)
    right[1] = send(mixed, to_diag, over_middle)
    low23 = send(lows23, first_to_slab)
    cores[0] = send(right[0], swap_core_diag)
    left = split_blocks([own01, own23, core01, core23])
    both = [[whole(0, n // 2, 0, True), whole(1, n // 2, n // 2, True)]] * 2
    total = product(
        roles,
        left,
        [(core01, "rows"), (core23, "rows"), own01, own23],
        {0: both, 1: [[whole(2, n, 0)], [whole(3, n, 0)]]},
        n,
        half=1,
    )
    mixed = pick(diag & first, chunk(core23, 1), own[2])
    seen[0] = pick(mid_off, right[0], there[0])
    there[0], right[1], low01, low23, cores[0], left, total, mixed, seen[0] = sync(
        there[0], right[1], low01, low23, cores[0], left, total, mixed, seen[0]
    )

    def share(j):
        r, t = right[j], there[j]
        return product(
            roles, left, [r, t], {0: [[whole(0, n, 0), whole(1, n, n)]], 1: [[whole(1, n, 0), whole(0, n, n)]]}, w, fetch=True
        )

    def add_rights(total, j, role_, halves=1):
        these = [right[j], right[j + 1], cores[j], cores[j + 1]]
        others = [there[j], there[j + 1], seen_cores[j], seen_cores[j + 1]] if role_ else these
        pieces = [whole(i, n // 2, i * w, True) for i in range(4)]
        return product(roles, these, [(v, "rows") for v in others], {role_: [pieces, pieces]}, n, base=total, halves=halves)

    shares, shared = [None] * 4, [None] * 4
    there[1] = send(right[1], swap_slab, outward)
    right[2] = send(mixed, to_diag, over_middle)
    cores[1] = send(right[1], swap_core_diag)
    seen_cores[0] = send(seen[0], swap_core)
    shares[0] = share(0)
    low_sources = [(2, 0), (2, n), (3, 0), (3, 2 * w)]
    total = product(
        roles,
        left,
        [(own01, "rows"), (own23, "rows"), low01, low23],
        {
            0: both,
            1: [lower(low_sources, 2 * j, 0, 0) + lower(low_sources, 2 * j + 1, 0, w) for j in range(2)],
        },
        n,
        base=total,
        half=0,
    )
    mixed = pick(diag, shares[0], own[3])
    seen[1] = pick(mid_off, right[1], there[1])
    there[1], right[2], low01, low23, cores[1], seen_cores[0], total, mixed, seen[1] = sync(
        there[1], right[2], low01, low23, cores[1], seen_cores[0], total, mixed, seen[1]
    )

    there[2] = send(right[2], swap_slab, outward)
    right[3] = send(mixed, swap_y)
    near3 = send(low01, middle_second)
    cores[2] = send(right[2], swap_core_diag)
    seen_cores[1] = send(seen[1], swap_core)
    shares[1] = share(1)
    total_first = add_rights(total, 0, 0)
    seen[2] = pick(mid_off, right[2], there[2])
    mixed = pick(diag & first, lows23, low23)
    swapped = pick(diag, right[3], seen[2])
    there[2], right[3], near3, cores[2], seen_cores[1], shares[1], total_first, swapped, mixed = sync(
        there[2], right[3], near3, cores[2], seen_cores[1], shares[1], total_first, swapped, mixed
    )
    shared[0] = right[3]

    there[3] = send(right[3], swap_slab)
    shared[1] = send(shares[1], to_off)
    near4 = send(mixed, over_middle)
    far3 = send(near3, outward_second)
    swapped = send(swapped, swap_core)
    shares[2] = share(2)
    shares[2], total_first, swapped = sync(shares[2], total_first, swapped)
    cores[3] = swapped
    keep_first, to_first = add_rights(total_first, 2, 0, 2)
    to_first, total = sync(to_first, total)
    total_second = add_rights(total, 0, 1)
    far3 = pick(at_end, far3, near3)
    there[3], shared[1], near4, far3, swapped, shares[2], keep_first, to_first, total_second = sync(
        there[3], shared[1], near4, far3, swapped, shares[2], keep_first, to_first, total_second
    )

    def rest(j, base):
        rights = seen[:3] + seen_cores[:2] + [swapped, far3, far4]
        lane_low = [(0, 0), (1, 0), (7, 0), (1, 3 * w)]
        other_low = [(6, 0), (6, n), (7, 0), (7, 2 * w)]
        picks = {
            2: lower(other_low, j, 0, 0) + [whole((0, 1, 2, 5)[j], n, n)],
            3: lower(lane_low, j, 0, 0) + [(v, j * w, w, True, n + k * w, 0) for k, v in enumerate((3, 4, 5, 2))],
        }
        used = sorted({entry[0] for pieces in picks.values() for entry in pieces})
        picks = {r: [[(used.index(e[0]),) + e[1:] for e in v]] for r, v in picks.items()}
        return product(roles, left, [rights[i] for i in used], picks, w, base=base, halves=2, fetch=True)

    tops, downs, crossed = [None] * 4, [None] * 4, [None] * 4
    shared[2] = send(shares[2], to_off)
    far4 = send(near4, outward)
    seen_cores[2] = send(there[2], swap_core_diag)
    seen_cores[3] = send(there[3], swap_core_diag)
    got_first = send(to_first, x_first)
    shares[3] = share(3)
    shares[3], shared[0], seen_cores[2], seen_cores[3] = sync(shares[3], shared[0], seen_cores[2], seen_cores[3])
    shared[3] = send(shares[3], to_off)
    tops[0], downs[0] = rest(0, shared[0])
    downs[0], shared[1] = sync(downs[0], shared[1])
    crossed[0] = send(downs[0], x_off)
    tops[1], downs[1] = rest(1, shared[1])
    downs[1], total_second = sync(downs[1], total_second)
    crossed[1] = send(downs[1], x_off)
    keep_second, to_second = add_rights(total_second, 2, 1, 2)
    far4 = pick(at_end, far4, near4)
    to_second, shared[2], far4, crossed[0] = sync(to_second, shared[2], far4, crossed[0])
    got_second = send(to_second, x_second)
    tops[2], downs[2] = rest(2, shared[2])
    downs[2], shared[3], crossed[1], got_first = sync(downs[2], shared[3], crossed[1], got_first)
    crossed[2] = send(downs[2], x_off)
    tops[3], downs[3] = rest(3, shared[3])
    downs[3], crossed[2] = sync(downs[3], crossed[2])
    crossed[3] = send(downs[3], x_off)

    flags = jnp.stack([role, x.astype(jnp.int32)])
    return place(flags, [keep_first, keep_second], [got_first, got_second], tops, crossed)


def solution(mesh):
    rows, cols = mesh.shape["row"], mesh.shape["col"]

    def body(recorded):
        frequencies = recorded.shape[1]
        if frequencies == 2 and cols == 4 and rows == frequencies * cols:
            return blocked(recorded)
        return gathered(recorded)

    spec = P(None, None, "row", "col")
    return jax.shard_map(body, mesh=mesh, in_specs=(spec,), out_specs=spec, check_vma=False)
```

time: 1750 us -> 583 us (0.33)
  the two profiles are of different devices: /device:TPU:16 before, /device:TPU:12 now
where the time goes in v1:
time: 583 us; the launch traced here: 578 us
  waiting for transfers between devices  272 us (47%)
  Pallas kernels  149 us (26%)
  starting transfers between devices  101 us (17%)
  other arithmetic  42 us (7%)
  local copies, waits for them, and re-layouts  13.3 us (2%)
    ppermute x35, waiting for transfers between devices, send(): return lax.ppermute(value, AXES, pairs)  272 us
    pallas_call x14, Pallas kernels, product(): pl.pallas_call(body, grid_spec=pltpu.PrefetchScalarGridSpec(num_scalar_pr...  123 us
    ppermute x35, starting transfers between devices, send(): return lax.ppermute(value, AXES, pairs)  101 us
    pallas_call x1, Pallas kernels, split_blocks(): pl.pallas_call(split_kernel, grid=(rows // mb,), in_specs=[pl.BlockSpec((...  16.1 us
  transfers between devices with their start and end apart: 35, of which 17 were waited for; matrix products, arithmetic and copies ran while one was open for 6% of the time, Pallas kernels for 24%

profile of v1, /device:TPU:12, one launch (start us, length us, event | category | flops | bytes accessed | tf_op | source)
XLA Modules:
  0.0 577.7 jit_solution(18031114813673686429)
XLA Ops:
  0.0 6.8 %dynamic-slice_bitcast_fusion.3 = (f32[2,512,512]{2,1,0:T(8,128)}, f32[2,512,512]{2,1,0:T(8,128)S(1)}, f32[2,512,512]{2,1,0:T(8,128)}, f32[2,512,512]{2,1,0:T(8,128)S(1)}) fusion(f32[2,2,512,1024]{3,2,1,0:T(8,128)} %param.1, s32[]{:T(128)S(6)} %select_n.139, s32[]{:T(128)S(6)} %select_n.141, s32[]{:T(128)S(6)} %select_n.143, s32[]{:T(128)S(6)} %select_n.144, ...), kind=kLoop, calls=%fused_computation.22 | loop fusion | bytes 16777240 | tf_op jit(solution)/shard_map/squeeze | solution.py:288
  8.3 45.9 %collective-permute-done = f32[2,512,512]{2,1,0:T(8,128)S(1)} collective-permute-done((f32[2,512,512]{2,1,0:T(8,128)S(1)}, f32[2,512,512]{2,1,0:T(8,128)S(1)}, u32[]{:S(2)}, u32[]{:S(2)}) %collective-permute-start) | collective-permute-done | bytes 2097184 | tf_op jit(solution)/shard_map/ppermute | solution.py:261
  54.4 2.3 fusion.3
  56.7 3.7 pad_maximum_fusion.2
  60.4 2.6 pad_maximum_fusion.refs_0_.refs_3_.refs_1_
  63.0 2.4 collective-permute-start.3
  70.5 43.4 %collective-permute-done.1 = f32[2,512,512]{2,1,0:T(8,128)} collective-permute-done((f32[2,512,512]{2,1,0:T(8,128)}, f32[2,512,512]{2,1,0:T(8,128)}, u32[]{:S(2)}, u32[]{:S(2)}) %collective-permute-start.1) | collective-permute-done | bytes 2097184 | tf_op jit(solution)/shard_map/ppermute | solution.py:261
  117.7 2.2 pad_maximum_fusion.1.refs_1_.refs_4_.refs_2_
  119.9 6.0 %fusion.1 = (f32[2,1024,256]{2,1,0:T(8,128)}, f32[2,1024,256]{2,1,0:T(8,128)}, f32[2,1024,256]{2,1,0:T(8,128)}) fusion(f32[2,512,512]{2,1,0:T(8,128)S(1)} %copy-done.8, f32[2,512,512]{2,1,0:T(8,128)} %collective-permute-done.1, f32[2,1024,256]{2,1,0:T(8,128)S(1)} %copy-done.9, f32[2,256,256]{2,1,0:T(8,128)S(1)} %slice.53, f32[2,768,256]{2,1,0:T(8,128)S(1)} %slice.40, ...), kind=kLoop, calls=%fused_computation.14 | loop fusion | flops 2097152 | bytes 14680065 | tf_op jit(solution)/shard_map/concatenate | solution.py:305
  126.0 7.1 %collective-permute-done.5.refs_3_.refs_2_ = f32[2,1024,512]{2,1,0:T(8,128)S(1)} collective-permute-done((f32[2,1024,512]{2,1,0:T(8,128)S(1)}, f32[2,1024,512]{2,1,0:T(8,128)S(1)}, u32[]{:S(2)}, u32[]{:S(2)}) %collective-permute-start.5) | collective-permute-done | bytes 4194336 | tf_op jit(solution)/shard_map/ppermute | solution.py:261
  133.1 3.7 collective-permute-start.6
  138.7 2.1 collective-permute-start.9
  140.8 2.2 collective-permute-start.8
  143.0 16.1 %shard_map.17.refs_0_ = bf16[6,1024,2048]{2,1,0:T(8,128)(2,1)} custom-call(f32[2,1024,512]{2,1,0:T(8,128)} %pad_maximum_fusion.refs_0_.refs_3_.refs_1_, f32[2,1024,512]{2,1,0:T(8,128)} %copy-done.2, f32[2,1024,512]{2,1,0:T(8,128)} %collective-permute-done.4.refs_2_.refs_1_, f32[2,1024,512]{2,1,0:T(8,128)} %copy-done.7), custom_call_target="tpu_custom_call" | custom-call | flops 1000 | bytes 1000 | tf_op jit(solution)/shard_map/pallas_call | solution.py:53
  159.1 6.7 %shard_map.18.refs_5_ = f32[2,1024,1024]{2,1,0:T(8,128)} custom-call(s32[1]{0:T(128)} %bitcast.role_ref, bf16[6,1024,2048]{2,1,0:T(8,128)(2,1)} %shard_map.17.refs_0_, f32[2,1024,512]{2,1,0:T(8,128)} %collective-permute-done.4.refs_2_.refs_1_, f32[2,1024,512]{2,1,0:T(8,128)} %copy-done.7, f32[2,1024,512]{2,1,0:T(8,128)} %pad_maximum_fusion.refs_0_.refs_3_.refs_1_, ...), custom_call_target="tpu_custom_call" | custom-call | flops 1000 | bytes 1000 | tf_op jit(solution)/shard_map/pallas_call | solution.py:184
  165.8 3.2 slice_select_fusion
  169.0 11.6 %collective-permute-done.6.refs_2_.refs_4_ = f32[2,1024,256]{2,1,0:T(8,128)} collective-permute-done((f32[2,1024,256]{2,1,0:T(8,128)S(1)}, f32[2,1024,256]{2,1,0:T(8,128)}, u32[]{:S(2)}, u32[]{:S(2)}) %collective-permute-start.6) | collective-permute-done | bytes 2097184 | tf_op jit(solution)/shard_map/ppermute | solution.py:261
  180.9 5.4 collective-permute-done.7.refs_1_.refs_5_
  186.4 2.6 collective-permute-start.10
  190.9 19.9 %collective-permute-start.11 = (f32[2,1024,256]{2,1,0:T(8,128)}, f32[2,1024,256]{2,1,0:T(8,128)}, u32[]{:S(2)}, u32[]{:S(2)}) collective-permute-start(f32[2,1024,256]{2,1,0:T(8,128)} %slice_select_fusion), channel_id=1, source_target_pairs={{2,0},{3,1},{6,4},{7,5},{8,16},{9,17},{10,8},{11,9},{12,20},{13,21... | collective-permute-start | bytes 6291464 | tf_op jit(solution)/shard_map/ppermute | solution.py:261
  211.2 3.6 shard_map.20
  214.8 6.2 %shard_map.19.refs_8_ = f32[2,1024,1024]{2,1,0:T(8,128)} custom-call(s32[1]{0:T(128)} %bitcast.role_ref, bf16[6,1024,2048]{2,1,0:T(8,128)(2,1)} %shard_map.17.refs_0_, f32[2,1024,512]{2,1,0:T(8,128)} %pad_maximum_fusion.refs_0_.refs_3_.refs_1_, f32[2,1024,512]{2,1,0:T(8,128)} %copy-done.2, f32[2,1792,256]{2,1,0:T(8,128)} %collective-permute-done.3.refs_3_, ...), custom_call_target="tpu_custom_call" | custom-call | flops 1000 | bytes 1000 | tf_op jit(solution)/shard_map/pallas_call | solution.py:184
  220.9 3.2 broadcast_select_fusion.2
  224.2 8.1 %collective-permute-done.10.refs_2_.refs_5_ = f32[2,1024,256]{2,1,0:T(8,128)} collective-permute-done((f32[2,1024,256]{2,1,0:T(8,128)}, f32[2,1024,256]{2,1,0:T(8,128)}, u32[]{:S(2)}, u32[]{:S(2)}) %collective-permute-start.10) | collective-permute-done | bytes 2097184 | tf_op jit(solution)/shard_map/ppermute | solution.py:261
  232.3 3.2 broadcast_select_fusion.4.refs_2_
  235.4 20.8 %collective-permute-done.11.refs_1_.refs_0_.refs_4_ = f32[2,1024,256]{2,1,0:T(8,128)} collective-permute-done((f32[2,1024,256]{2,1,0:T(8,128)}, f32[2,1024,256]{2,1,0:T(8,128)}, u32[]{:S(2)}, u32[]{:S(2)}) %collective-permute-start.11) | collective-permute-done | bytes 2097184 | tf_op jit(solution)/shard_map/ppermute | solution.py:261
  256.2 2.5 collective-permute-start.16
  258.8 3.3 collective-permute-start.14
  262.0 14.1 %collective-permute-start.15 = (f32[2,1024,256]{2,1,0:T(8,128)}, f32[2,1024,256]{2,1,0:T(8,128)S(1)}, u32[]{:S(2)}, u32[]{:S(2)}) collective-permute-start(f32[2,1024,256]{2,1,0:T(8,128)} %broadcast_select_fusion.2), channel_id=1, source_target_pairs={{0,2},{1,3},{2,0},{3,1},{4,6},{5,7},{6,4},{7,5},{8,10},{9,11},{10,... | collective-permute-start | bytes 6291464 | tf_op jit(solution)/shard_map/ppermute | solution.py:261
  276.2 2.0 collective-permute-start.17
  278.1 3.6 shard_map.21
  281.8 4.2 shard_map.22.refs_8_
  286.0 2.8 broadcast_select_fusion.7
  288.8 16.9 %collective-permute-done.14.refs_2_.refs_4_ = f32[2,1024,256]{2,1,0:T(8,128)} collective-permute-done((f32[2,1024,256]{2,1,0:T(8,128)}, f32[2,1024,256]{2,1,0:T(8,128)}, u32[]{:S(2)}, u32[]{:S(2)}) %collective-permute-start.14) | collective-permute-done | bytes 2097184 | tf_op jit(solution)/shard_map/ppermute | solution.py:261
  305.7 15.2 %collective-permute-done.15.refs_1_.refs_5_.refs_7_ = f32[2,1024,256]{2,1,0:T(8,128)S(1)} collective-permute-done((f32[2,1024,256]{2,1,0:T(8,128)}, f32[2,1024,256]{2,1,0:T(8,128)S(1)}, u32[]{:S(2)}, u32[]{:S(2)}) %collective-permute-start.15) | collective-permute-done | bytes 2097184 | tf_op jit(solution)/shard_map/ppermute | solution.py:261
  320.9 4.8 broadcast_select_fusion.1
  327.0 2.4 collective-permute-start.22
  330.0 2.0 collective-permute-start.19
  334.6 3.9 shard_map.23
  338.5 2.0 collective-permute-start.24
  340.5 4.7 shard_map.24
  345.2 4.2 shard_map.25.refs_8_
  349.4 4.3 broadcast_select_fusion.refs_6_.refs_7_
  353.7 30.3 %collective-permute-done.21 = f32[2,768,256]{2,1,0:T(8,128)S(1)} collective-permute-done((f32[2,768,256]{2,1,0:T(8,128)}, f32[2,768,256]{2,1,0:T(8,128)S(1)}, u32[]{:S(2)}, u32[]{:S(2)}) %collective-permute-start.21) | collective-permute-done | bytes 1572896 | tf_op jit(solution)/shard_map/ppermute | solution.py:261
  384.0 10.7 %collective-permute-done.20.refs_8_ = f32[2,1024,256]{2,1,0:T(8,128)} collective-permute-done((f32[2,1024,256]{2,1,0:T(8,128)}, f32[2,1024,256]{2,1,0:T(8,128)}, u32[]{:S(2)}, u32[]{:S(2)}) %collective-permute-start.20) | collective-permute-done | bytes 2097184 | tf_op jit(solution)/shard_map/ppermute | solution.py:261
  398.9 3.4 collective-permute-start.27
  402.2 4.0 shard_map.26
  406.3 19.3 %shard_map.27 = (f32[2,512,256]{2,1,0:T(8,128)}, f32[2,512,256]{2,1,0:T(8,128)}) custom-call(s32[1]{0:T(128)} %bitcast.role_ref, bf16[6,1024,2048]{2,1,0:T(8,128)(2,1)} %shard_map.17.refs_0_, f32[2,1024,256]{2,1,0:T(8,128)} %copy-done.4, f32[2,1024,256]{2,1,0:T(8,128)} %get-tuple-element.184.refs_2_.refs_3_, f32[2,1024,256]{2,1,0:T(8,128)} %copy-done.5, ...), custom_call_target="tpu_custom_call" | custom-call | flops 1000 | bytes 1000 | tf_op jit(solution)/shard_map/pallas_call | solution.py:184
  425.5 3.4 collective-permute-start.28
  429.0 5.8 %collective-permute-done.27 = f32[2,768,256]{2,1,0:T(8,128)} collective-permute-done((f32[2,768,256]{2,1,0:T(8,128)S(1)}, f32[2,768,256]{2,1,0:T(8,128)}, u32[]{:S(2)}, u32[]{:S(2)}) %collective-permute-start.27) | collective-permute-done | bytes 1572896 | tf_op jit(solution)/shard_map/ppermute | solution.py:261
  436.2 19.3 %shard_map.28 = (f32[2,512,256]{2,1,0:T(8,128)}, f32[2,512,256]{2,1,0:T(8,128)}) custom-call(s32[1]{0:T(128)} %bitcast.role_ref, bf16[6,1024,2048]{2,1,0:T(8,128)(2,1)} %shard_map.17.refs_0_, f32[2,1024,256]{2,1,0:T(8,128)} %copy-done.4, f32[2,1024,256]{2,1,0:T(8,128)} %broadcast_select_fusion.4.refs_2_, f32[2,1024,256]{2,1,0:T(8,128)} %get-tuple-element.184.refs_2_.refs_3_, ...), custom_call_target="tpu_custom_call" | custom-call | flops 1000 | bytes 1000 | tf_op jit(solution)/shard_map/pallas_call | solution.py:184
  456.7 4.7 shard_map.29
  461.4 4.3 collective-permute-done.26.refs_9_
  465.7 2.7 collective-permute-start.32
  468.4 4.5 collective-permute-start.30
  472.9 19.2 %shard_map.30 = (f32[2,512,256]{2,1,0:T(8,128)}, f32[2,512,256]{2,1,0:T(8,128)}) custom-call(s32[1]{0:T(128)} %bitcast.role_ref, bf16[6,1024,2048]{2,1,0:T(8,128)(2,1)} %shard_map.17.refs_0_, f32[2,1024,256]{2,1,0:T(8,128)} %copy-done.4, f32[2,1024,256]{2,1,0:T(8,128)} %broadcast_select_fusion.4.refs_2_, f32[2,1024,256]{2,1,0:T(8,128)} %get-tuple-element.184.refs_2_.refs_3_, ...), custom_call_target="tpu_custom_call" | custom-call | flops 1000 | bytes 1000 | tf_op jit(solution)/shard_map/pallas_call | solution.py:184
  492.1 4.5 collective-permute-done.30.refs_9_
  496.6 14.0 %collective-permute-done.29.refs_9_ = f32[2,1024,256]{2,1,0:T(8,128)} collective-permute-done((f32[2,1024,256]{2,1,0:T(8,128)}, f32[2,1024,256]{2,1,0:T(8,128)}, u32[]{:S(2)}, u32[]{:S(2)}) %collective-permute-start.29) | collective-permute-done | bytes 2097184 | tf_op jit(solution)/shard_map/ppermute | solution.py:261
  510.7 4.5 collective-permute-start.33
  515.2 19.0 %shard_map.31 = (f32[2,512,256]{2,1,0:T(8,128)}, f32[2,512,256]{2,1,0:T(8,128)}) custom-call(s32[1]{0:T(128)} %bitcast.role_ref, bf16[6,1024,2048]{2,1,0:T(8,128)(2,1)} %shard_map.17.refs_0_, f32[2,1024,256]{2,1,0:T(8,128)} %copy-done.4, f32[2,1024,256]{2,1,0:T(8,128)} %broadcast_select_fusion.4.refs_2_, f32[2,1024,256]{2,1,0:T(8,128)} %get-tuple-element.184.refs_2_.refs_3_, ...), custom_call_target="tpu_custom_call" | custom-call | flops 1000 | bytes 1000 | tf_op jit(solution)/shard_map/pallas_call | solution.py:184
  534.2 5.1 collective-permute-done.33.refs_10_
  539.3 3.4 collective-permute-start.34
  543.3 23.1 %collective-permute-done.34.refs_11_ = f32[2,512,256]{2,1,0:T(8,128)S(1)} collective-permute-done((f32[2,512,256]{2,1,0:T(8,128)}, f32[2,512,256]{2,1,0:T(8,128)S(1)}, u32[]{:S(2)}, u32[]{:S(2)}) %collective-permute-start.34) | collective-permute-done | bytes 1048608 | tf_op jit(solution)/shard_map/ppermute | solution.py:261
  567.5 10.0 %shard_map.32 = f32[2,2,512,1024]{3,2,1,0:T(8,128)} custom-call(s32[2]{0:T(128)} %pad_add_fusion.role_ref, f32[2,512,1024]{2,1,0:T(8,128)} %get-tuple-element.146.refs_0_, f32[2,512,1024]{2,1,0:T(8,128)} %get-tuple-element.159.refs_1_, f32[2,512,1024]{2,1,0:T(8,128)} %copy-done.11, f32[2,512,1024]{2,1,0:T(8,128)} %collective-permute-done.32.refs_3_, ...), custom_call_target="tpu_custom_call" | custom-call | flops 1000 | bytes 1000 | tf_op jit(solution)/shard_map/pallas_call | solution.py:225
  (70 shorter events, 27.9 us)
Async XLA Ops:
  6.8 47.4 %collective-permute-start = (f32[2,512,512]{2,1,0:T(8,128)S(1)}, f32[2,512,512]{2,1,0:T(8,128)S(1)}, u32[]{:S(2)}, u32[]{:S(2)}) collective-permute-start(f32[2,512,512]{2,1,0:T(8,128)S(1)} %get-tuple-element.188), channel_id=1, source_target_pairs={{0,4},{1,5},{2,6},{3,7},{4,0},{5,1},{6,2},{7,3},{8,12},{9,13},{10,... | collective-permute-start | bytes 6291464 | tf_op jit(solution)/shard_map/ppermute | solution.py:261
  63.0 62.8 %collective-permute-start.4 = (f32[2,1024,512]{2,1,0:T(8,128)}, f32[2,1024,512]{2,1,0:T(8,128)}, u32[]{:S(2)}, u32[]{:S(2)}) collective-permute-start(f32[2,1024,512]{2,1,0:T(8,128)} %pad_maximum_fusion.refs_0_.refs_3_.refs_1_), channel_id=1, source_target_pairs={{0,1},{1,0},{2,3},{3,2},{4,5},{5,4},{6,7},{7,6},{8,9},{9,8},{10,11... | collective-permute-start | bytes 12582920 | tf_op jit(solution)/shard_map/ppermute | solution.py:261
  63.0 62.8 %collective-permute-start.3 = (f32[2,1792,256]{2,1,0:T(8,128)}, f32[2,1792,256]{2,1,0:T(8,128)}, u32[]{:S(2)}, u32[]{:S(2)}) collective-permute-start(f32[2,1792,256]{2,1,0:T(8,128)} %pad_maximum_fusion.2), channel_id=1, source_target_pairs={{0,8},{4,12},{9,1},{13,5},{18,26},{22,30},{27,19},{31,23}} | collective-permute-start | bytes 11010056 | tf_op jit(solution)/shard_map/ppermute | solution.py:261
  65.5 48.4 %collective-permute-start.1 = (f32[2,512,512]{2,1,0:T(8,128)}, f32[2,512,512]{2,1,0:T(8,128)}, u32[]{:S(2)}, u32[]{:S(2)}) collective-permute-start(f32[2,512,512]{2,1,0:T(8,128)} %get-tuple-element.94), channel_id=1, source_target_pairs={{0,4},{1,5},{2,6},{3,7},{4,0},{5,1},{6,2},{7,3},{8,12},{9,13},{10,... | collective-permute-start | bytes 6291464 | tf_op jit(solution)/shard_map/ppermute | solution.py:261
  67.0 58.9 %collective-permute-start.2 = (f32[2,1024,256]{2,1,0:T(8,128)}, f32[2,1024,256]{2,1,0:T(8,128)S(1)}, u32[]{:S(2)}, u32[]{:S(2)}) collective-permute-start(f32[2,1024,256]{2,1,0:T(8,128)} %get-tuple-element.96), channel_id=1, source_target_pairs={{2,0},{3,1},{6,4},{7,5},{8,16},{9,17},{10,8},{11,9},{12,20},{13,21... | collective-permute-start | bytes 6291464 | tf_op jit(solution)/shard_map/ppermute | solution.py:261
  115.1 2.5 copy-start.8
  117.7 2.2 copy-start.9
  119.9 6.0 %copy-start.2 = (f32[2,1024,512]{2,1,0:T(8,128)}, f32[2,1024,512]{2,1,0:T(8,128)S(1)}, u32[]{:S(2)}) copy-start(f32[2,1024,512]{2,1,0:T(8,128)S(1)} %pad_maximum_fusion.1.refs_1_.refs_4_.refs_2_) | copy-start | bytes 12582916
  125.8 54.8 %copy-start.3 = (f32[2,1024,256]{2,1,0:T(8,128)}, f32[2,1024,256]{2,1,0:T(8,128)S(1)}, u32[]{:S(2)}) copy-start(f32[2,1024,256]{2,1,0:T(8,128)S(1)} %collective-permute-done.2.refs_1_.refs_0_.refs_4_) | copy-start | bytes 6291460
  125.9 7.2 %collective-permute-start.5 = (f32[2,1024,512]{2,1,0:T(8,128)S(1)}, f32[2,1024,512]{2,1,0:T(8,128)S(1)}, u32[]{:S(2)}, u32[]{:S(2)}) collective-permute-start(f32[2,1024,512]{2,1,0:T(8,128)S(1)} %pad_maximum_fusion.1.refs_1_.refs_4_.refs_2_), channel_id=1, source_target_pairs={{0,1},{1,0},{2,3},{3,2},{4,5},{5,4},{6,7},{7,6},{8,9},{9,8},{10,11... | collective-permute-start | bytes 12582920 | tf_op jit(solution)/shard_map/ppermute | solution.py:261
  133.1 3.7 copy-start.7
  133.1 47.5 %collective-permute-start.6 = (f32[2,1024,256]{2,1,0:T(8,128)S(1)}, f32[2,1024,256]{2,1,0:T(8,128)}, u32[]{:S(2)}, u32[]{:S(2)}) collective-permute-start(f32[2,1024,256]{2,1,0:T(8,128)S(1)} %collective-permute-done.2.refs_1_.refs_0_.refs_4_), channel_id=1, source_target_pairs={{0,8},{1,9},{4,12},{5,13},{8,0},{9,1},{10,2},{11,3},{12,4},{13,5},... | collective-permute-start | bytes 6291464 | tf_op jit(solution)/shard_map/ppermute | solution.py:261
  136.8 49.6 %collective-permute-start.7 = (f32[2,1024,256]{2,1,0:T(8,128)}, f32[2,1024,256]{2,1,0:T(8,128)}, u32[]{:S(2)}, u32[]{:S(2)}) collective-permute-start(f32[2,1024,256]{2,1,0:T(8,128)} %get-tuple-element.105), channel_id=1, source_target_pairs={{2,0},{3,1},{6,4},{7,5},{8,16},{9,17},{10,8},{11,9},{12,20},{13,21... | collective-permute-start | bytes 6291464 | tf_op jit(solution)/shard_map/ppermute | solution.py:261
  138.7 47.7 %collective-permute-start.9 = (f32[2,1024,256]{2,1,0:T(8,128)S(1)}, f32[2,1024,256]{2,1,0:T(8,128)}, u32[]{:S(2)}, u32[]{:S(2)}) collective-permute-start(f32[2,1024,256]{2,1,0:T(8,128)S(1)} %collective-permute-done.2.refs_1_.refs_0_.refs_4_), channel_id=1, source_target_pairs={{0,1},{1,0},{4,5},{5,4},{8,9},{9,8},{12,13},{13,12},{18,19},{19,18... | collective-permute-start | bytes 6291464 | tf_op jit(solution)/shard_map/ppermute | solution.py:261
  140.8 40.2 %collective-permute-start.8 = (f32[2,768,256]{2,1,0:T(8,128)}, f32[2,768,256]{2,1,0:T(8,128)}, u32[]{:S(2)}, u32[]{:S(2)}) collective-permute-start(f32[2,768,256]{2,1,0:T(8,128)} %pad_maximum_fusion.3), channel_id=1, source_target_pairs={{0,8},{4,12},{9,1},{13,5},{18,26},{22,30},{27,19},{31,23}} | collective-permute-start | bytes 4718600 | tf_op jit(solution)/shard_map/ppermute | solution.py:261
  159.1 6.7 %copy-start.10 = (f32[2,1024,256]{2,1,0:T(8,128)S(1)}, f32[2,1024,256]{2,1,0:T(8,128)}, u32[]{:S(2)}) copy-start(f32[2,1024,256]{2,1,0:T(8,128)} %get-tuple-element.110) | copy-start | bytes 6291460
  180.9 33.9 %copy-start.4 = (f32[2,1024,256]{2,1,0:T(8,128)}, f32[2,1024,256]{2,1,0:T(8,128)S(1)}, u32[]{:S(2)}) copy-start(f32[2,1024,256]{2,1,0:T(8,128)S(1)} %broadcast_select_fusion.5.refs_1_) | copy-start | bytes 6291460
  186.4 45.9 %collective-permute-start.10 = (f32[2,1024,256]{2,1,0:T(8,128)}, f32[2,1024,256]{2,1,0:T(8,128)}, u32[]{:S(2)}, u32[]{:S(2)}) collective-permute-start(f32[2,1024,256]{2,1,0:T(8,128)} %collective-permute-done.7.refs_1_.refs_5_), channel_id=1, source_target_pairs={{0,8},{1,9},{4,12},{5,13},{8,0},{9,1},{10,2},{11,3},{12,4},{13,5},... | collective-permute-start | bytes 6291464 | tf_op jit(solution)/shard_map/ppermute | solution.py:261
  189.0 67.2 %collective-permute-start.12 = (f32[2,1024,256]{2,1,0:T(8,128)}, f32[2,1024,256]{2,1,0:T(8,128)}, u32[]{:S(2)}, u32[]{:S(2)}) collective-permute-start(f32[2,1024,256]{2,1,0:T(8,128)} %collective-permute-done.7.refs_1_.refs_5_), channel_id=1, source_target_pairs={{0,1},{1,0},{4,5},{5,4},{8,9},{9,8},{12,13},{13,12},{18,19},{19,18... | collective-permute-start | bytes 6291464 | tf_op jit(solution)/shard_map/ppermute | solution.py:261
  190.9 65.2 %collective-permute-start.11 = (f32[2,1024,256]{2,1,0:T(8,128)}, f32[2,1024,256]{2,1,0:T(8,128)}, u32[]{:S(2)}, u32[]{:S(2)}) collective-permute-start(f32[2,1024,256]{2,1,0:T(8,128)} %slice_select_fusion), channel_id=1, source_target_pairs={{2,0},{3,1},{6,4},{7,5},{8,16},{9,17},{10,8},{11,9},{12,20},{13,21... | collective-permute-start | bytes 6291464 | tf_op jit(solution)/shard_map/ppermute | solution.py:261
  210.9 45.3 %collective-permute-start.13 = (f32[2,1024,256]{2,1,0:T(8,128)S(1)}, f32[2,1024,256]{2,1,0:T(8,128)S(1)}, u32[]{:S(2)}, u32[]{:S(2)}) collective-permute-start(f32[2,1024,256]{2,1,0:T(8,128)S(1)} %broadcast_select_fusion.5.refs_1_), channel_id=1, source_target_pairs={{0,1},{1,0},{2,3},{3,2},{4,5},{5,4},{6,7},{7,6},{8,9},{9,8},{10,11... | collective-permute-start | bytes 6291464 | tf_op jit(solution)/shard_map/ppermute | solution.py:261
  256.2 2.6 copy-start.5
  256.2 69.5 %collective-permute-start.16 = (f32[2,1792,256]{2,1,0:T(8,128)}, f32[2,1792,256]{2,1,0:T(8,128)}, u32[]{:S(2)}, u32[]{:S(2)}) collective-permute-start(f32[2,1792,256]{2,1,0:T(8,128)} %collective-permute-done.3.refs_3_), channel_id=1, source_target_pairs={{8,16},{12,20},{19,11},{23,15}} | collective-permute-start | bytes 11010056 | tf_op jit(solution)/shard_map/ppermute | solution.py:261
  258.8 47.0 %collective-permute-start.14 = (f32[2,1024,256]{2,1,0:T(8,128)}, f32[2,1024,256]{2,1,0:T(8,128)}, u32[]{:S(2)}, u32[]{:S(2)}) collective-permute-start(f32[2,1024,256]{2,1,0:T(8,128)} %collective-permute-done.11.refs_1_.refs_0_.refs_4_), channel_id=1, source_target_pairs={{0,8},{1,9},{4,12},{5,13},{8,0},{9,1},{10,2},{11,3},{12,4},{13,5},... | collective-permute-start | bytes 6291464 | tf_op jit(solution)/shard_map/ppermute | solution.py:261
  262.0 58.9 %collective-permute-start.15 = (f32[2,1024,256]{2,1,0:T(8,128)}, f32[2,1024,256]{2,1,0:T(8,128)S(1)}, u32[]{:S(2)}, u32[]{:S(2)}) collective-permute-start(f32[2,1024,256]{2,1,0:T(8,128)} %broadcast_select_fusion.2), channel_id=1, source_target_pairs={{0,2},{1,3},{2,0},{3,1},{4,6},{5,7},{6,4},{7,5},{8,10},{9,11},{10,... | collective-permute-start | bytes 6291464 | tf_op jit(solution)/shard_map/ppermute | solution.py:261
  276.2 49.5 %collective-permute-start.17 = (f32[2,1024,256]{2,1,0:T(8,128)}, f32[2,1024,256]{2,1,0:T(8,128)}, u32[]{:S(2)}, u32[]{:S(2)}) collective-permute-start(f32[2,1024,256]{2,1,0:T(8,128)} %collective-permute-done.11.refs_1_.refs_0_.refs_4_), channel_id=1, source_target_pairs={{0,1},{1,0},{4,5},{5,4},{8,9},{9,8},{12,13},{13,12},{18,19},{19,18... | collective-permute-start | bytes 6291464 | tf_op jit(solution)/shard_map/ppermute | solution.py:261
  278.1 47.5 %collective-permute-start.18 = (f32[2,1024,256]{2,1,0:T(8,128)}, f32[2,1024,256]{2,1,0:T(8,128)S(1)}, u32[]{:S(2)}, u32[]{:S(2)}) collective-permute-start(f32[2,1024,256]{2,1,0:T(8,128)} %broadcast_select_fusion.4.refs_2_), channel_id=1, source_target_pairs={{0,1},{1,0},{2,3},{3,2},{4,5},{5,4},{6,7},{7,6},{8,9},{9,8},{10,11... | collective-permute-start | bytes 6291464 | tf_op jit(solution)/shard_map/ppermute | solution.py:261
  320.9 9.1 %copy-start.1 = (f32[2,1024,256]{2,1,0:T(8,128)}, f32[2,1024,256]{2,1,0:T(8,128)S(1)}, u32[]{:S(2)}) copy-start(f32[2,1024,256]{2,1,0:T(8,128)S(1)} %collective-permute-done.15.refs_1_.refs_5_.refs_7_) | copy-start | bytes 6291460
  325.7 1.3 copy-start.6
  327.0 22.4 %collective-permute-start.22 = (f32[2,1792,256]{2,1,0:T(8,128)}, f32[2,1792,256]{2,1,0:T(8,128)}, u32[]{:S(2)}, u32[]{:S(2)}) collective-permute-start(f32[2,1792,256]{2,1,0:T(8,128)} %collective-permute-done.16), channel_id=1, source_target_pairs={{11,3},{15,7},{16,24},{20,28}} | collective-permute-start | bytes 11010056 | tf_op jit(solution)/shard_map/ppermute | solution.py:261
  329.4 9.0 %collective-permute-start.23 = (f32[2,1024,256]{2,1,0:T(8,128)}, f32[2,1024,256]{2,1,0:T(8,128)S(1)}, u32[]{:S(2)}, u32[]{:S(2)}) collective-permute-start(f32[2,1024,256]{2,1,0:T(8,128)} %get-tuple-element.135), channel_id=1, source_target_pairs={{0,1},{1,0},{2,3},{3,2},{4,5},{5,4},{6,7},{7,6},{8,9},{9,8},{10,11... | collective-permute-start | bytes 6291464 | tf_op jit(solution)/shard_map/ppermute | solution.py:261
  330.0 54.0 %collective-permute-start.19 = (f32[2,1024,256]{2,1,0:T(8,128)S(1)}, f32[2,1024,256]{2,1,0:T(8,128)}, u32[]{:S(2)}, u32[]{:S(2)}) collective-permute-start(f32[2,1024,256]{2,1,0:T(8,128)S(1)} %collective-permute-done.15.refs_1_.refs_5_.refs_7_), channel_id=1, source_target_pairs={{0,8},{1,9},{4,12},{5,13},{8,0},{9,1},{12,4},{13,5},{18,26},{19,27... | collective-permute-start | bytes 6291464 | tf_op jit(solution)/shard_map/ppermute | solution.py:261
  332.0 62.7 %collective-permute-start.20 = (f32[2,1024,256]{2,1,0:T(8,128)}, f32[2,1024,256]{2,1,0:T(8,128)}, u32[]{:S(2)}, u32[]{:S(2)}) collective-permute-start(f32[2,1024,256]{2,1,0:T(8,128)} %shard_map.21), channel_id=1, source_target_pairs={{0,2},{1,3},{4,6},{5,7},{8,10},{9,11},{12,14},{13,15},{18,16},{19,... | collective-permute-start | bytes 6291464 | tf_op jit(solution)/shard_map/ppermute | solution.py:261
  333.3 50.7 %collective-permute-start.21 = (f32[2,768,256]{2,1,0:T(8,128)}, f32[2,768,256]{2,1,0:T(8,128)S(1)}, u32[]{:S(2)}, u32[]{:S(2)}) collective-permute-start(f32[2,768,256]{2,1,0:T(8,128)} %broadcast_select_fusion.7), channel_id=1, source_target_pairs={{8,16},{9,17},{12,20},{13,21},{18,10},{19,11},{22,14},{23,15}} | collective-permute-start | bytes 4718600 | tf_op jit(solution)/shard_map/ppermute | solution.py:261
  338.5 2.0 copy-start
  338.5 67.8 %collective-permute-start.24 = (f32[2,1024,256]{2,1,0:T(8,128)}, f32[2,1024,256]{2,1,0:T(8,128)}, u32[]{:S(2)}, u32[]{:S(2)}) collective-permute-start(f32[2,1024,256]{2,1,0:T(8,128)} %collective-permute-done.14.refs_2_.refs_4_), channel_id=1, source_target_pairs={{0,1},{1,0},{4,5},{5,4},{8,9},{9,8},{12,13},{13,12},{18,19},{19,18... | collective-permute-start | bytes 6291464 | tf_op jit(solution)/shard_map/ppermute | solution.py:261
  394.7 11.6 %collective-permute-start.25 = (f32[2,1024,256]{2,1,0:T(8,128)}, f32[2,1024,256]{2,1,0:T(8,128)}, u32[]{:S(2)}, u32[]{:S(2)}) collective-permute-start(f32[2,1024,256]{2,1,0:T(8,128)} %collective-permute-done.19.refs_2_.refs_5_), channel_id=1, source_target_pairs={{0,1},{1,0},{4,5},{5,4},{8,9},{9,8},{12,13},{13,12},{18,19},{19,18... | collective-permute-start | bytes 6291464 | tf_op jit(solution)/shard_map/ppermute | solution.py:261
  396.6 114.0 %collective-permute-start.31 = (f32[2,512,1024]{2,1,0:T(8,128)}, f32[2,512,1024]{2,1,0:T(8,128)S(1)}, u32[]{:S(2)}, u32[]{:S(2)}) collective-permute-start(f32[2,512,1024]{2,1,0:T(8,128)} %get-tuple-element.169), channel_id=1, source_target_pairs={{0,4},{4,0},{9,13},{13,9},{18,22},{22,18},{27,31},{31,27}} | collective-permute-start | bytes 12582920 | tf_op jit(solution)/shard_map/ppermute | solution.py:261
  397.6 68.2 %collective-permute-start.26 = (f32[2,1024,256]{2,1,0:T(8,128)}, f32[2,1024,256]{2,1,0:T(8,128)}, u32[]{:S(2)}, u32[]{:S(2)}) collective-permute-start(f32[2,1024,256]{2,1,0:T(8,128)} %shard_map.23), channel_id=1, source_target_pairs={{0,2},{1,3},{4,6},{5,7},{8,10},{9,11},{12,14},{13,15},{18,16},{19,... | collective-permute-start | bytes 6291464 | tf_op jit(solution)/shard_map/ppermute | solution.py:261
  398.9 35.9 %collective-permute-start.27 = (f32[2,768,256]{2,1,0:T(8,128)S(1)}, f32[2,768,256]{2,1,0:T(8,128)}, u32[]{:S(2)}, u32[]{:S(2)}) collective-permute-start(f32[2,768,256]{2,1,0:T(8,128)S(1)} %collective-permute-done.21), channel_id=1, source_target_pairs={{10,2},{11,3},{14,6},{15,7},{16,24},{17,25},{20,28},{21,29}} | collective-permute-start | bytes 4718600 | tf_op jit(solution)/shard_map/ppermute | solution.py:261
  425.5 40.2 %collective-permute-start.28 = (f32[2,512,256]{2,1,0:T(8,128)}, f32[2,512,256]{2,1,0:T(8,128)}, u32[]{:S(2)}, u32[]{:S(2)}) collective-permute-start(f32[2,512,256]{2,1,0:T(8,128)} %get-tuple-element.163), channel_id=1, source_target_pairs={{2,6},{3,7},{6,2},{7,3},{10,14},{11,15},{14,10},{15,11},{16,20},{1... | collective-permute-start | bytes 3145736 | tf_op jit(solution)/shard_map/ppermute | solution.py:261
  455.4 55.2 %collective-permute-start.29 = (f32[2,1024,256]{2,1,0:T(8,128)}, f32[2,1024,256]{2,1,0:T(8,128)}, u32[]{:S(2)}, u32[]{:S(2)}) collective-permute-start(f32[2,1024,256]{2,1,0:T(8,128)} %shard_map.26), channel_id=1, source_target_pairs={{0,2},{1,3},{4,6},{5,7},{8,10},{9,11},{12,14},{13,15},{18,16},{19,... | collective-permute-start | bytes 6291464 | tf_op jit(solution)/shard_map/ppermute | solution.py:261
  465.7 100.7 %collective-permute-start.32 = (f32[2,512,1024]{2,1,0:T(8,128)}, f32[2,512,1024]{2,1,0:T(8,128)}, u32[]{:S(2)}, u32[]{:S(2)}) collective-permute-start(f32[2,512,1024]{2,1,0:T(8,128)} %get-tuple-element.171), channel_id=1, source_target_pairs={{1,5},{5,1},{8,12},{12,8},{19,23},{23,19},{26,30},{30,26}} | collective-permute-start | bytes 12582920 | tf_op jit(solution)/shard_map/ppermute | solution.py:261
  468.4 28.2 %collective-permute-start.30 = (f32[2,512,256]{2,1,0:T(8,128)}, f32[2,512,256]{2,1,0:T(8,128)S(1)}, u32[]{:S(2)}, u32[]{:S(2)}) collective-permute-start(f32[2,512,256]{2,1,0:T(8,128)} %get-tuple-element.168), channel_id=1, source_target_pairs={{2,6},{3,7},{6,2},{7,3},{10,14},{11,15},{14,10},{15,11},{16,20},{1... | collective-permute-start | bytes 3145736 | tf_op jit(solution)/shard_map/ppermute | solution.py:261
  496.6 37.6 %copy-start.12 = (f32[2,512,256]{2,1,0:T(8,128)}, f32[2,512,256]{2,1,0:T(8,128)S(1)}, u32[]{:S(2)}) copy-start(f32[2,512,256]{2,1,0:T(8,128)S(1)} %collective-permute-done.30.refs_9_) | copy-start | bytes 3145732
  510.7 23.5 %copy-start.11 = (f32[2,512,1024]{2,1,0:T(8,128)}, f32[2,512,1024]{2,1,0:T(8,128)S(1)}, u32[]{:S(2)}) copy-start(f32[2,512,1024]{2,1,0:T(8,128)S(1)} %collective-permute-done.31.refs_2_) | copy-start | bytes 12582916
  510.7 28.7 %collective-permute-start.33 = (f32[2,512,256]{2,1,0:T(8,128)}, f32[2,512,256]{2,1,0:T(8,128)}, u32[]{:S(2)}, u32[]{:S(2)}) collective-permute-start(f32[2,512,256]{2,1,0:T(8,128)} %get-tuple-element.180), channel_id=1, source_target_pairs={{2,6},{3,7},{6,2},{7,3},{10,14},{11,15},{14,10},{15,11},{16,20},{1... | collective-permute-start | bytes 3145736 | tf_op jit(solution)/shard_map/ppermute | solution.py:261
  539.3 27.1 %collective-permute-start.34 = (f32[2,512,256]{2,1,0:T(8,128)}, f32[2,512,256]{2,1,0:T(8,128)S(1)}, u32[]{:S(2)}, u32[]{:S(2)}) collective-permute-start(f32[2,512,256]{2,1,0:T(8,128)} %get-tuple-element.182), channel_id=1, source_target_pairs={{2,6},{3,7},{6,2},{7,3},{10,14},{11,15},{14,10},{15,11},{16,20},{1... | collective-permute-start | bytes 3145736 | tf_op jit(solution)/shard_map/ppermute | solution.py:261
  566.5 1.0 copy-start.13

commit v2 on v1

--- a/solution.py
+++ b/solution.py
@@ -40,31 +40,11 @@
         out[2 * c, rows, at : at + k], out[2 * c + 1, rows, at : at + k] = split(v)
 
 
-def split_kernel(*refs):
-    at = 0
-    for ref in refs[:-1]:
-        split_into(refs[-1], at, ref)
-        at += ref.shape[2]
-
-
-def split_blocks(blocks):
-    rows, ks = blocks[0].shape[1], [v.shape[2] for v in blocks]
-    mb = rows // CHUNKS
-    return pl.pallas_call(
-        split_kernel,
-        grid=(rows // mb,),
-        in_specs=[pl.BlockSpec((2, mb, k), lambda i: (0, i, 0)) for k in ks],
-        out_specs=pl.BlockSpec((6, mb, sum(ks)), lambda i: (0, i, 0)),
-        out_shape=jax.ShapeDtypeStruct((6, rows, sum(ks)), jnp.bfloat16),
-        compiler_params=pltpu.CompilerParams(vmem_limit_bytes=56 * 2**20),
-        cost_estimate=pl.CostEstimate(flops=1000, bytes_accessed=1000, transcendentals=0),
-    )(*blocks)
-
-
-def product_kernel(role_ref, *refs, picks, lefts, rights, more, halves, fetch):
+def product_kernel(role_ref, *refs, picks, lefts, rights, more, halves, fetch, depth, keep):
     left, candidates, rest = refs[:lefts], refs[lefts : lefts + rights], refs[lefts + rights :]
     base, rest = (rest[0], rest[1:]) if more else (None, rest)
     outs, rest = rest[:halves], rest[halves:]
+    kept, rest = (rest[0], rest[1:]) if keep else (None, rest)
     scratch = rest[0]
     j, i = pl.program_id(0), pl.program_id(1)
     for role, steps in picks.items():
@@ -77,16 +57,17 @@
                     at, copies = 0, []
                     for which, start, size, _, _, _ in pieces:
                         source = candidates[which].at[:, pl.ds(start, size), :]
-                        copies.append(
-                            pltpu.make_async_copy(source, staged.at[:, pl.ds(at, size), :], sems.at[len(copies)])
-                        )
+                        k = source.shape[2]
+                        target = staged.at[:, pl.ds(at, size), pl.ds(0, k)]
+                        copies.append(pltpu.make_async_copy(source, target, sems.at[len(copies)]))
                         copies[-1].start()
                         at += size
                     at = 0
                 for number, (which, start, size, flip, row, col) in enumerate(pieces):
                     if fetch:
                         copies[number].wait()
-                        block = [staged[c, at : at + size, :] for c in range(2)]
+                        k = candidates[which].shape[2]
+                        block = [staged[c, at : at + size, :k] for c in range(2)]
                         at += size
                     else:
                         block = [candidates[which][c, start : start + size, :] for c in range(2)]
@@ -94,23 +75,24 @@
                         block = [v.T for v in block]
                     split_into(scratch, col, block, slice(row, row + block[0].shape[0]))
 
+    def split_left(held):
+        at = 0
+        for ref in left:
+            split_into(held, at, ref)
+            at += ref.shape[2]
+
+    if keep:
+        split_left(kept)
+
     @pl.when(functools.reduce(jnp.logical_or, [role_ref[0] == role for role in picks]))
     def _():
-        if lefts == 1:
+        if keep:
+            parts = multiply_split(kept, slice(kept.shape[2] - depth, None), scratch)
+        elif lefts == 1:
             parts = multiply_split(left[0], slice(None), scratch)
         else:
-            held = rest[1]
-            mb = left[0].shape[1]
-            rows = pl.ds(pl.multiple_of(i * mb, mb), mb)
-
-            @pl.when(j == 0)
-            def _():
-                at = 0
-                for ref in left:
-                    split_into(held, at, ref, rows)
-                    at += ref.shape[2]
-
-            parts = multiply_split(held, rows, scratch)
+            split_left(rest[1])
+            parts = multiply_split(rest[1], slice(None), scratch)
         for h, out in enumerate(outs):
 
             @pl.when(i * halves // pl.num_programs(1) == h)
@@ -119,10 +101,10 @@
                     out[c] = parts[c] if base is None else parts[c] + base[c]
 
 
-def multiply_split(left, rows, right):
+def multiply_split(left, columns, right):
     parts = []
     for c in range(3):
-        high, low = left[2 * c, rows, :], left[2 * c + 1, rows, :]
+        high, low = left[2 * c, :, columns], left[2 * c + 1, :, columns]
         total = jnp.dot(high, right[2 * c], preferred_element_type=jnp.float32)
         total += jnp.dot(high, right[2 * c + 1], preferred_element_type=jnp.float32)
         total += jnp.dot(low, right[2 * c], preferred_element_type=jnp.float32)
@@ -131,12 +113,13 @@
     return rr - ii, ss - rr - ii
 
 
-def product(role, left, rights, picks, columns, base=None, half=None, halves=1, fetch=False):
+def product(role, left, rights, picks, columns, base=None, half=None, halves=1, fetch=False, keep=False):
     split_left = not isinstance(left, list)
     lefts = [left] if split_left else left
     rows = lefts[0].shape[1]
-    depth = sum(v.shape[2] for v in lefts) // (1 if half is None else 2)
-    mb, nb = rows // CHUNKS, min(columns, rows // 2)
+    total = sum(v.shape[2] for v in lefts)
+    depth = total // (1 if half is None and not keep else 2)
+    mb, nb = rows // CHUNKS, columns
     once = pl.Buffered(1)
 
     def on(r):
@@ -145,9 +128,8 @@
     if split_left:
         in_specs = [pl.BlockSpec((6, mb, depth), lambda j, i, r: (0, i * on(r), half or 0))]
     else:
-        last = rows // mb - 1
         in_specs = [
-            pl.BlockSpec((2, mb, v.shape[2]), lambda j, i, r: (0, jnp.where(j == 0, i, last) * on(r), 0)) for v in lefts
+            pl.BlockSpec((2, mb, v.shape[2]), lambda j, i, r: (0, i * (1 if keep else on(r)), 0)) for v in lefts
         ]
     arrays = []
     for v in rights:
@@ -166,14 +148,16 @@
         in_specs.append(pl.BlockSpec((2, mb, nb), lambda j, i, r: (0, i * on(r), j * on(r))))
         args.append(base)
     scratch = [pltpu.VMEM((6, depth, nb), jnp.bfloat16)]
-    if not split_left:
-        scratch.append(pltpu.VMEM((6, rows, depth), jnp.bfloat16))
+    if not split_left and not keep:
+        scratch.append(pltpu.VMEM((6, mb, depth), jnp.bfloat16))
     if fetch:
         every = [pieces for steps in picks.values() for pieces in steps]
-        scratch.append(pltpu.VMEM((2, max(sum(e[2] for e in v) for v in every), nb), jnp.float32))
+        wide = max(v.shape[2] for v in rights)
+        scratch.append(pltpu.VMEM((2, max(sum(e[2] for e in v) for v in every), wide), jnp.float32))
         scratch.append(pltpu.SemaphoreType.DMA((max(len(v) for v in every),)))
     body = functools.partial(
-        product_kernel, picks=picks, lefts=len(lefts), rights=len(rights), more=base is not None, halves=halves, fetch=fetch
+        product_kernel, picks=picks, lefts=len(lefts), rights=len(rights), more=base is not None, halves=halves, fetch=fetch,
+        depth=depth, keep=keep,
     )
     steps = rows // mb // halves
     out_specs = [
@@ -181,6 +165,9 @@
         for h in range(halves)
     ]
     out_shape = [jax.ShapeDtypeStruct((2, rows // halves, columns), jnp.float32)] * halves
+    if keep:
+        out_specs.append(pl.BlockSpec((6, mb, total), lambda j, i, r: (0, i, 0)))
+        out_shape.append(jax.ShapeDtypeStruct((6, rows, total), jnp.bfloat16))
     result = pl.pallas_call(
         body,
         grid_spec=pltpu.PrefetchScalarGridSpec(
@@ -194,7 +181,7 @@
         compiler_params=pltpu.CompilerParams(vmem_limit_bytes=58 * 2**20),
         cost_estimate=pl.CostEstimate(flops=1000, bytes_accessed=1000, transcendentals=0),
     )(role, *args)
-    return result[0] if halves == 1 else tuple(result)
+    return tuple(result) if len(result) > 1 else result[0]
 
 
 def place_kernel(role_ref, *refs):
@@ -242,7 +229,7 @@
     half, p = z // 2, z % 2
     diag, first, lane = y == half, c == p, c == half
     at_end = (z == 0) | (z == 3)
-    role = jnp.where(diag, jnp.where(first, 0, 1), jnp.where(lane, 3, 2)).astype(jnp.int32)
+    role = jnp.where(diag, jnp.where(first, 0, 1), jnp.where(lane, 3, 2) + jnp.where(at_end, 0, 2)).astype(jnp.int32)
     roles = jnp.reshape(role, (1,))
     part, width = recorded.shape[2], recorded.shape[3]
     w, n = width // CHUNKS, width
@@ -310,7 +297,6 @@
         own23, own[2], own[3], lows23, mixed, right[0], low01, core01
     )
     core23 = send(own23, swap_core)
-    core23, own[3], lows23, mixed, right[0] = sync(core23, own[3], lows23, mixed, right[0])
 
     def whole(which, k, row, transposed=False):
         return (which, 0, k, transposed, row, 0)
@@ -323,20 +309,21 @@
     right[1] = send(mixed, to_diag, over_middle)
     low23 = send(lows23, first_to_slab)
     cores[0] = send(right[0], swap_core_diag)
-    left = split_blocks([own01, own23, core01, core23])
-    both = [[whole(0, n // 2, 0, True), whole(1, n // 2, n // 2, True)]] * 2
-    total = product(
+    both = [whole(0, n, 0, True), whole(1, n, n // 2, True)]
+    total, left = product(
         roles,
-        left,
-        [(core01, "rows"), (core23, "rows"), own01, own23],
-        {0: both, 1: [[whole(2, n, 0)], [whole(3, n, 0)]]},
+        [own01, own23, core01, core23],
+        [core01, core23, own01, own23],
+        {0: [both], 1: [[whole(2, n, 0), (3, 0, n, False, 0, n // 2)]]},
         n,
-        half=1,
-    )
+        fetch=True,
+        keep=True,
+    )
+    there[0], right[1], total, left = sync(there[0], right[1], total, left)
     mixed = pick(diag & first, chunk(core23, 1), own[2])
     seen[0] = pick(mid_off, right[0], there[0])
-    there[0], right[1], low01, low23, cores[0], left, total, mixed, seen[0] = sync(
-        there[0], right[1], low01, low23, cores[0], left, total, mixed, seen[0]
+    there[0], right[1], low01, low23, cores[0], left, total, mixed, seen[0], own[3] = sync(
+        there[0], right[1], low01, low23, cores[0], left, total, mixed, seen[0], own[3]
     )
 
     def share(j):
@@ -345,11 +332,14 @@
             roles, left, [r, t], {0: [[whole(0, n, 0), whole(1, n, n)]], 1: [[whole(1, n, 0), whole(0, n, n)]]}, w, fetch=True
         )
 
-    def add_rights(total, j, role_, halves=1):
-        these = [right[j], right[j + 1], cores[j], cores[j + 1]]
-        others = [there[j], there[j + 1], seen_cores[j], seen_cores[j + 1]] if role_ else these
-        pieces = [whole(i, n // 2, i * w, True) for i in range(4)]
-        return product(roles, these, [(v, "rows") for v in others], {role_: [pieces, pieces]}, n, base=total, halves=halves)
+    def add_rights(total, js, active, halves=1):
+        these = [right[j] for j in js] + [cores[j] for j in js]
+        others = [there[j] for j in js] + [seen_cores[j] for j in js]
+        k = len(these)
+        rights = (these if 0 in active else []) + (others if 1 in active else [])
+        first_of = {0: 0, 1: len(rights) - k}
+        picks = {v: [[whole(first_of[v] + i, n, i * w, True) for i in range(k)]] for v in active}
+        return product(roles, these, rights, picks, n, base=total, halves=halves, fetch=True)
 
     shares, shared = [None] * 4, [None] * 4
     there[1] = send(right[1], swap_slab, outward)
@@ -361,14 +351,12 @@
     total = product(
         roles,
         left,
-        [(own01, "rows"), (own23, "rows"), low01, low23],
-        {
-            0: both,
-            1: [lower(low_sources, 2 * j, 0, 0) + lower(low_sources, 2 * j + 1, 0, w) for j in range(2)],
-        },
+        [own01, own23, low01, low23],
+        {0: [both], 1: [sum([lower(low_sources, j, 0, j * w) for j in range(4)], [])]},
         n,
         base=total,
         half=0,
+        fetch=True,
     )
     mixed = pick(diag, shares[0], own[3])
     seen[1] = pick(mid_off, right[1], there[1])
@@ -382,12 +370,13 @@
     cores[2] = send(right[2], swap_core_diag)
     seen_cores[1] = send(seen[1], swap_core)
     shares[1] = share(1)
-    total_first = add_rights(total, 0, 0)
+    shares[1], seen_cores[1], cores[1], total = sync(shares[1], seen_cores[1], cores[1], total)
+    total = add_rights(total, (0, 1), (0, 1))
     seen[2] = pick(mid_off, right[2], there[2])
     mixed = pick(diag & first, lows23, low23)
     swapped = pick(diag, right[3], seen[2])
-    there[2], right[3], near3, cores[2], seen_cores[1], shares[1], total_first, swapped, mixed = sync(
-        there[2], right[3], near3, cores[2], seen_cores[1], shares[1], total_first, swapped, mixed
+    there[2], right[3], near3, cores[2], shares[1], total, swapped, mixed = sync(
+        there[2], right[3], near3, cores[2], shares[1], total, swapped, mixed
     )
     shared[0] = right[3]
 
@@ -397,24 +386,22 @@
     far3 = send(near3, outward_second)
     swapped = send(swapped, swap_core)
     shares[2] = share(2)
-    shares[2], total_first, swapped = sync(shares[2], total_first, swapped)
+    shares[2], total, swapped = sync(shares[2], total, swapped)
     cores[3] = swapped
-    keep_first, to_first = add_rights(total_first, 2, 0, 2)
-    to_first, total = sync(to_first, total)
-    total_second = add_rights(total, 0, 1)
-    far3 = pick(at_end, far3, near3)
-    there[3], shared[1], near4, far3, swapped, shares[2], keep_first, to_first, total_second = sync(
-        there[3], shared[1], near4, far3, swapped, shares[2], keep_first, to_first, total_second
+    keep_first, to_first = add_rights(total, (2, 3), (0,), 2)
+    there[3], shared[1], near4, far3, swapped, shares[2], keep_first, to_first, total = sync(
+        there[3], shared[1], near4, far3, swapped, shares[2], keep_first, to_first, total
     )
 
     def rest(j, base):
-        rights = seen[:3] + seen_cores[:2] + [swapped, far3, far4]
-        lane_low = [(0, 0), (1, 0), (7, 0), (1, 3 * w)]
-        other_low = [(6, 0), (6, n), (7, 0), (7, 2 * w)]
-        picks = {
-            2: lower(other_low, j, 0, 0) + [whole((0, 1, 2, 5)[j], n, n)],
-            3: lower(lane_low, j, 0, 0) + [(v, j * w, w, True, n + k * w, 0) for k, v in enumerate((3, 4, 5, 2))],
-        }
+        rights = seen[:3] + seen_cores[:2] + [swapped, far3, far4, near3, near4]
+        picks = {}
+        for k, last in ((2, 6), (4, 8)):
+            lane_low = [(0, 0), (1, 0), (last + 1, 0), (1, 3 * w)]
+            other_low = [(last, 0), (last, n), (last + 1, 0), (last + 1, 2 * w)]
+            picks[k] = lower(other_low, j, 0, 0) + [whole((0, 1, 2, 5)[j], n, n)]
+            picks[k + 1] = lower(lane_low, j, 0, 0)
+            picks[k + 1] += [(v, j * w, w, True, n + i * w, 0) for i, v in enumerate((3, 4, 5, 2))]
         used = sorted({entry[0] for pieces in picks.values() for entry in pieces})
         picks = {r: [[(used.index(e[0]),) + e[1:] for e in v]] for r, v in picks.items()}
         return product(roles, left, [rights[i] for i in used], picks, w, base=base, halves=2, fetch=True)
@@ -432,10 +419,9 @@
     downs[0], shared[1] = sync(downs[0], shared[1])
     crossed[0] = send(downs[0], x_off)
     tops[1], downs[1] = rest(1, shared[1])
-    downs[1], total_second = sync(downs[1], total_second)
+    downs[1], total = sync(downs[1], total)
     crossed[1] = send(downs[1], x_off)
-    keep_second, to_second = add_rights(total_second, 2, 1, 2)
-    far4 = pick(at_end, far4, near4)
+    keep_second, to_second = add_rights(total, (2, 3), (1,), 2)
     to_second, shared[2], far4, crossed[0] = sync(to_second, shared[2], far4, crossed[0])
     got_second = send(to_second, x_second)
     tops[2], downs[2] = rest(2, shared[2])

time: 583 us -> 559 us (0.959)
  the two profiles are of different devices: /device:TPU:12 before, /device:TPU:16 now
where the time goes in v2:
time: 559 us; the launch traced here: 549 us
  waiting for transfers between devices  267 us (48%)
  Pallas kernels  136 us (24%)
  starting transfers between devices  90.8 us (16%)
  other arithmetic  37.3 us (7%)
  local copies, waits for them, and re-layouts  17.1 us (3%)
    ppermute x35, waiting for transfers between devices, send(): return lax.ppermute(value, AXES, pairs)  267 us
    pallas_call x13, Pallas kernels, product(): pl.pallas_call(body, grid_spec=pltpu.PrefetchScalarGridSpec(num_scalar_pr...  126 us
    ppermute x35, starting transfers between devices, send(): return lax.ppermute(value, AXES, pairs)  90.8 us
  transfers between devices with their start and end apart: 35, of which 15 were waited for; matrix products, arithmetic and copies ran while one was open for 6% of the time, Pallas kernels for 23%

profile of v2, /device:TPU:16, one launch (start us, length us, event | category | flops | bytes accessed | tf_op | source)
XLA Modules:
  0.0 548.9 jit_solution(9239699613431046841)
XLA Ops:
  0.0 6.8 %dynamic-slice_bitcast_fusion.3 = (f32[2,512,512]{2,1,0:T(8,128)}, f32[2,512,512]{2,1,0:T(8,128)S(1)}, f32[2,512,512]{2,1,0:T(8,128)}, f32[2,512,512]{2,1,0:T(8,128)S(1)}) fusion(f32[2,2,512,1024]{3,2,1,0:T(8,128)} %param.1, s32[]{:T(128)S(6)} %select_n.129, s32[]{:T(128)S(6)} %select_n.131, s32[]{:T(128)S(6)} %select_n.133, s32[]{:T(128)S(6)} %select_n.134, ...), kind=kLoop, calls=%fused_computation.22 | loop fusion | bytes 16777240 | tf_op jit(solution)/shard_map/squeeze | solution.py:275
  6.8 1.5 collective-permute-start
  8.3 45.9 %collective-permute-done = f32[2,512,512]{2,1,0:T(8,128)S(1)} collective-permute-done((f32[2,512,512]{2,1,0:T(8,128)S(1)}, f32[2,512,512]{2,1,0:T(8,128)S(1)}, u32[]{:S(2)}, u32[]{:S(2)}) %collective-permute-start) | collective-permute-done | bytes 2097184 | tf_op jit(solution)/shard_map/ppermute | solution.py:248
  54.4 2.3 fusion.3
  56.7 3.7 pad_maximum_fusion.2
  60.4 2.6 pad_maximum_fusion.refs_0_.refs_6_.refs_1_
  63.0 2.4 collective-permute-start.3
  66.9 6.2 %collective-permute-start.2 = (f32[2,1024,256]{2,1,0:T(8,128)}, f32[2,1024,256]{2,1,0:T(8,128)S(1)}, u32[]{:S(2)}, u32[]{:S(2)}) collective-permute-start(f32[2,1024,256]{2,1,0:T(8,128)} %get-tuple-element.99), channel_id=1, source_target_pairs={{2,0},{3,1},{6,4},{7,5},{8,16},{9,17},{10,8},{11,9},{12,20},{13,21... | collective-permute-start | bytes 6291464 | tf_op jit(solution)/shard_map/ppermute | solution.py:248
  73.2 1.5 slice.40
  74.8 39.0 %collective-permute-done.1 = f32[2,512,512]{2,1,0:T(8,128)} collective-permute-done((f32[2,512,512]{2,1,0:T(8,128)}, f32[2,512,512]{2,1,0:T(8,128)}, u32[]{:S(2)}, u32[]{:S(2)}) %collective-permute-start.1) | collective-permute-done | bytes 2097184 | tf_op jit(solution)/shard_map/ppermute | solution.py:248
  117.6 4.2 pad_maximum_fusion.1.refs_1_.refs_7_.refs_2_
  121.7 4.4 fusion.1
  126.3 4.8 collective-permute-start.5
  131.1 1.9 collective-permute-start.6
  133.0 2.0 collective-permute-start.9
  134.9 2.0 collective-permute-start.8
  137.0 16.9 %shard_map.17 = (f32[2,1024,1024]{2,1,0:T(8,128)}, bf16[6,1024,2048]{2,1,0:T(8,128)(2,1)}) custom-call(s32[1]{0:T(128)} %bitcast.role_ref, f32[2,1024,512]{2,1,0:T(8,128)} %pad_maximum_fusion.refs_0_.refs_6_.refs_1_, f32[2,1024,512]{2,1,0:T(8,128)} %pad_maximum_fusion.1.refs_1_.refs_7_.refs_2_, f32[2,1024,512]{2,1,0:T(8,128)} %collective-permute-done.4.refs_2_.refs_4_, ...), custom_call_target="tpu_custom_call" | custom-call | flops 1000 | bytes 1000 | tf_op jit(solution)/shard_map/pallas_call | solution.py:171
  153.8 21.4 %collective-permute-done.5.refs_2_.refs_8_ = f32[2,1024,256]{2,1,0:T(8,128)} collective-permute-done((f32[2,1024,256]{2,1,0:T(8,128)S(1)}, f32[2,1024,256]{2,1,0:T(8,128)}, u32[]{:S(2)}, u32[]{:S(2)}) %collective-permute-start.5) | collective-permute-done | bytes 2097184 | tf_op jit(solution)/shard_map/ppermute | solution.py:248
  175.3 5.7 %collective-permute-done.6.refs_1_.refs_5_ = f32[2,1024,256]{2,1,0:T(8,128)} collective-permute-done((f32[2,1024,256]{2,1,0:T(8,128)}, f32[2,1024,256]{2,1,0:T(8,128)}, u32[]{:S(2)}, u32[]{:S(2)}) %collective-permute-start.6) | collective-permute-done | bytes 2097184 | tf_op jit(solution)/shard_map/ppermute | solution.py:248
  182.6 3.9 slice_select_fusion
  186.5 2.7 collective-permute-start.10
  189.2 2.0 collective-permute-start.12
  191.2 10.1 %collective-permute-start.11 = (f32[2,1024,256]{2,1,0:T(8,128)}, f32[2,1024,256]{2,1,0:T(8,128)}, u32[]{:S(2)}, u32[]{:S(2)}) collective-permute-start(f32[2,1024,256]{2,1,0:T(8,128)} %slice_select_fusion), channel_id=1, source_target_pairs={{2,0},{3,1},{6,4},{7,5},{8,16},{9,17},{10,8},{11,9},{12,20},{13,21... | collective-permute-start | bytes 6291464 | tf_op jit(solution)/shard_map/ppermute | solution.py:248
  201.6 3.6 shard_map.19
  205.2 4.0 shard_map.18.refs_12_
  209.2 3.2 broadcast_select_fusion.1
  212.3 20.5 %collective-permute-done.10.refs_2_.refs_9_ = f32[2,1024,256]{2,1,0:T(8,128)} collective-permute-done((f32[2,1024,256]{2,1,0:T(8,128)}, f32[2,1024,256]{2,1,0:T(8,128)}, u32[]{:S(2)}, u32[]{:S(2)}) %collective-permute-start.10) | collective-permute-done | bytes 2097184 | tf_op jit(solution)/shard_map/ppermute | solution.py:248
  232.8 3.2 broadcast_select_fusion.3.refs_2_
  236.0 10.7 %collective-permute-done.11.refs_1_.refs_0_.refs_4_ = f32[2,1024,256]{2,1,0:T(8,128)} collective-permute-done((f32[2,1024,256]{2,1,0:T(8,128)}, f32[2,1024,256]{2,1,0:T(8,128)}, u32[]{:S(2)}, u32[]{:S(2)}) %collective-permute-start.11) | collective-permute-done | bytes 2097184 | tf_op jit(solution)/shard_map/ppermute | solution.py:248
  248.9 3.5 collective-permute-start.14
  252.5 10.2 %collective-permute-start.15 = (f32[2,1024,256]{2,1,0:T(8,128)}, f32[2,1024,256]{2,1,0:T(8,128)S(1)}, u32[]{:S(2)}, u32[]{:S(2)}) collective-permute-start(f32[2,1024,256]{2,1,0:T(8,128)} %broadcast_select_fusion.1), channel_id=1, source_target_pairs={{0,2},{1,3},{2,0},{3,1},{4,6},{5,7},{6,4},{7,5},{8,10},{9,11},{10,... | collective-permute-start | bytes 6291464 | tf_op jit(solution)/shard_map/ppermute | solution.py:248
  262.7 2.0 collective-permute-start.17
  264.7 3.8 shard_map.20
  268.5 2.8 broadcast_select_fusion.5
  272.6 3.6 shard_map.21.refs_8_
  276.2 20.8 %collective-permute-done.14.refs_2_.refs_4_ = f32[2,1024,256]{2,1,0:T(8,128)} collective-permute-done((f32[2,1024,256]{2,1,0:T(8,128)}, f32[2,1024,256]{2,1,0:T(8,128)}, u32[]{:S(2)}, u32[]{:S(2)}) %collective-permute-start.14) | collective-permute-done | bytes 2097184 | tf_op jit(solution)/shard_map/ppermute | solution.py:248
  297.0 12.2 %collective-permute-done.15.refs_1_.refs_5_.refs_8_ = f32[2,1024,256]{2,1,0:T(8,128)S(1)} collective-permute-done((f32[2,1024,256]{2,1,0:T(8,128)}, f32[2,1024,256]{2,1,0:T(8,128)S(1)}, u32[]{:S(2)}, u32[]{:S(2)}) %collective-permute-start.15) | collective-permute-done | bytes 2097184 | tf_op jit(solution)/shard_map/ppermute | solution.py:248
  309.2 4.8 broadcast_select_fusion
  314.0 5.5 %collective-permute-start.22 = (f32[2,1792,256]{2,1,0:T(8,128)}, f32[2,1792,256]{2,1,0:T(8,128)}, u32[]{:S(2)}, u32[]{:S(2)}) collective-permute-start(f32[2,1792,256]{2,1,0:T(8,128)} %collective-permute-done.16.refs_7_.refs_8_.refs_9_), channel_id=1, source_target_pairs={{11,3},{15,7},{16,24},{20,28}} | collective-permute-start | bytes 11010056 | tf_op jit(solution)/shard_map/ppermute | solution.py:248
  319.5 2.0 collective-permute-start.19
  324.1 4.0 shard_map.22
  328.2 2.0 collective-permute-start.24
  330.2 4.3 shard_map.23
  334.5 30.9 %collective-permute-done.21.refs_10_ = f32[2,768,256]{2,1,0:T(8,128)S(1)} collective-permute-done((f32[2,768,256]{2,1,0:T(8,128)}, f32[2,768,256]{2,1,0:T(8,128)S(1)}, u32[]{:S(2)}, u32[]{:S(2)}) %collective-permute-start.21) | collective-permute-done | bytes 1572896 | tf_op jit(solution)/shard_map/ppermute | solution.py:248
  365.4 11.4 %collective-permute-done.20.refs_9_ = f32[2,1024,256]{2,1,0:T(8,128)} collective-permute-done((f32[2,1024,256]{2,1,0:T(8,128)}, f32[2,1024,256]{2,1,0:T(8,128)}, u32[]{:S(2)}, u32[]{:S(2)}) %collective-permute-start.20) | collective-permute-done | bytes 2097184 | tf_op jit(solution)/shard_map/ppermute | solution.py:248
  376.8 2.0 collective-permute-start.25
  378.8 2.6 collective-permute-start.31
  382.7 2.3 collective-permute-start.27
  385.0 3.8 shard_map.24
  388.9 19.1 %shard_map.25 = (f32[2,512,256]{2,1,0:T(8,128)}, f32[2,512,256]{2,1,0:T(8,128)}) custom-call(s32[1]{0:T(128)} %bitcast.role_ref, bf16[6,1024,2048]{2,1,0:T(8,128)(2,1)} %get-tuple-element.121.refs_0_, f32[2,1024,256]{2,1,0:T(8,128)} %copy-done.2, f32[2,1024,256]{2,1,0:T(8,128)} %get-tuple-element.190.refs_2_.refs_3_, f32[2,1024,256]{2,1,0:T(8,128)} %copy-done.3, ...), custom_call_target="tpu_custom_call" | custom-call | flops 1000 | bytes 1000 | tf_op jit(solution)/shard_map/pallas_call | solution.py:171
  407.9 3.4 collective-permute-start.28
  411.3 19.3 %shard_map.26 = (f32[2,512,256]{2,1,0:T(8,128)}, f32[2,512,256]{2,1,0:T(8,128)}) custom-call(s32[1]{0:T(128)} %bitcast.role_ref, bf16[6,1024,2048]{2,1,0:T(8,128)(2,1)} %get-tuple-element.121.refs_0_, f32[2,1024,256]{2,1,0:T(8,128)} %copy-done.2, f32[2,1024,256]{2,1,0:T(8,128)} %broadcast_select_fusion.3.refs_2_, ...), custom_call_target="tpu_custom_call" | custom-call | flops 1000 | bytes 1000 | tf_op jit(solution)/shard_map/pallas_call | solution.py:171
  431.9 4.6 shard_map.27
  436.5 2.3 collective-permute-done.26.refs_11_
  441.0 2.4 collective-permute-start.30
  443.5 19.5 %shard_map.28 = (f32[2,512,256]{2,1,0:T(8,128)}, f32[2,512,256]{2,1,0:T(8,128)}) custom-call(s32[1]{0:T(128)} %bitcast.role_ref, bf16[6,1024,2048]{2,1,0:T(8,128)(2,1)} %get-tuple-element.121.refs_0_, f32[2,1024,256]{2,1,0:T(8,128)} %copy-done.2, f32[2,1024,256]{2,1,0:T(8,128)} %broadcast_select_fusion.3.refs_2_, ...), custom_call_target="tpu_custom_call" | custom-call | flops 1000 | bytes 1000 | tf_op jit(solution)/shard_map/pallas_call | solution.py:171
  463.0 4.1 collective-permute-done.30.refs_9_
  467.1 15.7 %collective-permute-done.29.refs_11_ = f32[2,1024,256]{2,1,0:T(8,128)} collective-permute-done((f32[2,1024,256]{2,1,0:T(8,128)}, f32[2,1024,256]{2,1,0:T(8,128)}, u32[]{:S(2)}, u32[]{:S(2)}) %collective-permute-start.29) | collective-permute-done | bytes 2097184 | tf_op jit(solution)/shard_map/ppermute | solution.py:248
  482.8 3.4 collective-permute-start.33
  486.2 19.2 %shard_map.29 = (f32[2,512,256]{2,1,0:T(8,128)}, f32[2,512,256]{2,1,0:T(8,128)}) custom-call(s32[1]{0:T(128)} %bitcast.role_ref, bf16[6,1024,2048]{2,1,0:T(8,128)(2,1)} %get-tuple-element.121.refs_0_, f32[2,1024,256]{2,1,0:T(8,128)} %copy-done.2, f32[2,1024,256]{2,1,0:T(8,128)} %broadcast_select_fusion.3.refs_2_, ...), custom_call_target="tpu_custom_call" | custom-call | flops 1000 | bytes 1000 | tf_op jit(solution)/shard_map/pallas_call | solution.py:171
  505.5 4.4 collective-permute-done.33.refs_10_
  509.8 3.6 collective-permute-start.34
  514.0 22.2 %collective-permute-done.34.refs_11_ = f32[2,512,256]{2,1,0:T(8,128)S(1)} collective-permute-done((f32[2,512,256]{2,1,0:T(8,128)}, f32[2,512,256]{2,1,0:T(8,128)S(1)}, u32[]{:S(2)}, u32[]{:S(2)}) %collective-permute-start.34) | collective-permute-done | bytes 1048608 | tf_op jit(solution)/shard_map/ppermute | solution.py:248
  538.5 10.1 %shard_map.30 = f32[2,2,512,1024]{3,2,1,0:T(8,128)} custom-call(s32[2]{0:T(128)} %pad_add_fusion.role_ref, f32[2,512,1024]{2,1,0:T(8,128)} %get-tuple-element.152.refs_0_, f32[2,512,1024]{2,1,0:T(8,128)} %get-tuple-element.165.refs_1_, f32[2,512,1024]{2,1,0:T(8,128)} %collective-permute-done.31.refs_2_, f32[2,512,1024]{2,1,0:T(8,128)} %copy-done.11, ...), custom_call_target="tpu_custom_call" | custom-call | flops 1000 | bytes 1000 | tf_op jit(solution)/shard_map/pallas_call | solution.py:212
  (68 shorter events, 21.3 us)
Async XLA Ops:
  6.8 47.4 %collective-permute-start = (f32[2,512,512]{2,1,0:T(8,128)S(1)}, f32[2,512,512]{2,1,0:T(8,128)S(1)}, u32[]{:S(2)}, u32[]{:S(2)}) collective-permute-start(f32[2,512,512]{2,1,0:T(8,128)S(1)} %get-tuple-element.194), channel_id=1, source_target_pairs={{0,4},{1,5},{2,6},{3,7},{4,0},{5,1},{6,2},{7,3},{8,12},{9,13},{10,... | collective-permute-start | bytes 6291464 | tf_op jit(solution)/shard_map/ppermute | solution.py:248
  63.0 63.2 %collective-permute-start.4 = (f32[2,1024,512]{2,1,0:T(8,128)}, f32[2,1024,512]{2,1,0:T(8,128)}, u32[]{:S(2)}, u32[]{:S(2)}) collective-permute-start(f32[2,1024,512]{2,1,0:T(8,128)} %pad_maximum_fusion.refs_0_.refs_6_.refs_1_), channel_id=1, source_target_pairs={{0,1},{1,0},{2,3},{3,2},{4,5},{5,4},{6,7},{7,6},{8,9},{9,8},{10,11... | collective-permute-start | bytes 12582920 | tf_op jit(solution)/shard_map/ppermute | solution.py:248
  63.0 63.2 %collective-permute-start.3 = (f32[2,1792,256]{2,1,0:T(8,128)}, f32[2,1792,256]{2,1,0:T(8,128)}, u32[]{:S(2)}, u32[]{:S(2)}) collective-permute-start(f32[2,1792,256]{2,1,0:T(8,128)} %pad_maximum_fusion.2), channel_id=1, source_target_pairs={{0,8},{4,12},{9,1},{13,5},{18,26},{22,30},{27,19},{31,23}} | collective-permute-start | bytes 11010056 | tf_op jit(solution)/shard_map/ppermute | solution.py:248
  65.4 48.4 %collective-permute-start.1 = (f32[2,512,512]{2,1,0:T(8,128)}, f32[2,512,512]{2,1,0:T(8,128)}, u32[]{:S(2)}, u32[]{:S(2)}) collective-permute-start(f32[2,512,512]{2,1,0:T(8,128)} %get-tuple-element.97), channel_id=1, source_target_pairs={{0,4},{1,5},{2,6},{3,7},{4,0},{5,1},{6,2},{7,3},{8,12},{9,13},{10,... | collective-permute-start | bytes 6291464 | tf_op jit(solution)/shard_map/ppermute | solution.py:248
  66.9 59.2 %collective-permute-start.2 = (f32[2,1024,256]{2,1,0:T(8,128)}, f32[2,1024,256]{2,1,0:T(8,128)S(1)}, u32[]{:S(2)}, u32[]{:S(2)}) collective-permute-start(f32[2,1024,256]{2,1,0:T(8,128)} %get-tuple-element.99), channel_id=1, source_target_pairs={{2,0},{3,1},{6,4},{7,5},{8,16},{9,17},{10,8},{11,9},{12,20},{13,21... | collective-permute-start | bytes 6291464 | tf_op jit(solution)/shard_map/ppermute | solution.py:248
  115.1 2.5 copy-start.6
  117.6 4.2 copy-start.7
  126.2 54.8 %copy-start.5 = (f32[2,1024,256]{2,1,0:T(8,128)}, f32[2,1024,256]{2,1,0:T(8,128)S(1)}, u32[]{:S(2)}) copy-start(f32[2,1024,256]{2,1,0:T(8,128)S(1)} %collective-permute-done.2.refs_1_.refs_0_.refs_4_) | copy-start | bytes 6291460
  126.2 10.8 %collective-permute-start.7 = (f32[2,1024,512]{2,1,0:T(8,128)}, f32[2,1024,512]{2,1,0:T(8,128)}, u32[]{:S(2)}, u32[]{:S(2)}) collective-permute-start(f32[2,1024,512]{2,1,0:T(8,128)} %pad_maximum_fusion.1.refs_1_.refs_7_.refs_2_), channel_id=1, source_target_pairs={{0,1},{1,0},{2,3},{3,2},{4,5},{5,4},{6,7},{7,6},{8,9},{9,8},{10,11... | collective-permute-start | bytes 12582920 | tf_op jit(solution)/shard_map/ppermute | solution.py:248
  126.3 49.0 %collective-permute-start.5 = (f32[2,1024,256]{2,1,0:T(8,128)S(1)}, f32[2,1024,256]{2,1,0:T(8,128)}, u32[]{:S(2)}, u32[]{:S(2)}) collective-permute-start(f32[2,1024,256]{2,1,0:T(8,128)S(1)} %collective-permute-done.2.refs_1_.refs_0_.refs_4_), channel_id=1, source_target_pairs={{0,8},{1,9},{4,12},{5,13},{8,0},{9,1},{10,2},{11,3},{12,4},{13,5},... | collective-permute-start | bytes 6291464 | tf_op jit(solution)/shard_map/ppermute | solution.py:248
  131.1 49.9 %collective-permute-start.6 = (f32[2,1024,256]{2,1,0:T(8,128)}, f32[2,1024,256]{2,1,0:T(8,128)}, u32[]{:S(2)}, u32[]{:S(2)}) collective-permute-start(f32[2,1024,256]{2,1,0:T(8,128)} %get-tuple-element.103), channel_id=1, source_target_pairs={{2,0},{3,1},{6,4},{7,5},{8,16},{9,17},{10,8},{11,9},{12,20},{13,21... | collective-permute-start | bytes 6291464 | tf_op jit(solution)/shard_map/ppermute | solution.py:248
  133.0 53.6 %collective-permute-start.9 = (f32[2,1024,256]{2,1,0:T(8,128)S(1)}, f32[2,1024,256]{2,1,0:T(8,128)}, u32[]{:S(2)}, u32[]{:S(2)}) collective-permute-start(f32[2,1024,256]{2,1,0:T(8,128)S(1)} %collective-permute-done.2.refs_1_.refs_0_.refs_4_), channel_id=1, source_target_pairs={{0,1},{1,0},{4,5},{5,4},{8,9},{9,8},{12,13},{13,12},{18,19},{19,18... | collective-permute-start | bytes 6291464 | tf_op jit(solution)/shard_map/ppermute | solution.py:248
  134.9 51.6 %collective-permute-start.8 = (f32[2,768,256]{2,1,0:T(8,128)}, f32[2,768,256]{2,1,0:T(8,128)}, u32[]{:S(2)}, u32[]{:S(2)}) collective-permute-start(f32[2,768,256]{2,1,0:T(8,128)} %pad_maximum_fusion.3), channel_id=1, source_target_pairs={{0,8},{4,12},{9,1},{13,5},{18,26},{22,30},{27,19},{31,23}} | collective-permute-start | bytes 4718600 | tf_op jit(solution)/shard_map/ppermute | solution.py:248
  181.0 1.6 copy-start.8
  182.6 18.7 %copy-start.2 = (f32[2,1024,256]{2,1,0:T(8,128)}, f32[2,1024,256]{2,1,0:T(8,128)S(1)}, u32[]{:S(2)}) copy-start(f32[2,1024,256]{2,1,0:T(8,128)S(1)} %broadcast_select_fusion.4.refs_1_) | copy-start | bytes 6291460
  186.5 46.3 %collective-permute-start.10 = (f32[2,1024,256]{2,1,0:T(8,128)}, f32[2,1024,256]{2,1,0:T(8,128)}, u32[]{:S(2)}, u32[]{:S(2)}) collective-permute-start(f32[2,1024,256]{2,1,0:T(8,128)} %collective-permute-done.6.refs_1_.refs_5_), channel_id=1, source_target_pairs={{0,8},{1,9},{4,12},{5,13},{8,0},{9,1},{10,2},{11,3},{12,4},{13,5},... | collective-permute-start | bytes 6291464 | tf_op jit(solution)/shard_map/ppermute | solution.py:248
  189.2 57.5 %collective-permute-start.12 = (f32[2,1024,256]{2,1,0:T(8,128)}, f32[2,1024,256]{2,1,0:T(8,128)}, u32[]{:S(2)}, u32[]{:S(2)}) collective-permute-start(f32[2,1024,256]{2,1,0:T(8,128)} %collective-permute-done.6.refs_1_.refs_5_), channel_id=1, source_target_pairs={{0,1},{1,0},{4,5},{5,4},{8,9},{9,8},{12,13},{13,12},{18,19},{19,18... | collective-permute-start | bytes 6291464 | tf_op jit(solution)/shard_map/ppermute | solution.py:248
  191.2 55.5 %collective-permute-start.11 = (f32[2,1024,256]{2,1,0:T(8,128)}, f32[2,1024,256]{2,1,0:T(8,128)}, u32[]{:S(2)}, u32[]{:S(2)}) collective-permute-start(f32[2,1024,256]{2,1,0:T(8,128)} %slice_select_fusion), channel_id=1, source_target_pairs={{2,0},{3,1},{6,4},{7,5},{8,16},{9,17},{10,8},{11,9},{12,20},{13,21... | collective-permute-start | bytes 6291464 | tf_op jit(solution)/shard_map/ppermute | solution.py:248
  201.3 45.4 %collective-permute-start.13 = (f32[2,1024,256]{2,1,0:T(8,128)S(1)}, f32[2,1024,256]{2,1,0:T(8,128)S(1)}, u32[]{:S(2)}, u32[]{:S(2)}) collective-permute-start(f32[2,1024,256]{2,1,0:T(8,128)S(1)} %broadcast_select_fusion.4.refs_1_), channel_id=1, source_target_pairs={{0,1},{1,0},{2,3},{3,2},{4,5},{5,4},{6,7},{7,6},{8,9},{9,8},{10,11... | collective-permute-start | bytes 6291464 | tf_op jit(solution)/shard_map/ppermute | solution.py:248
  246.7 2.2 copy-start.3
  246.7 67.2 %collective-permute-start.16 = (f32[2,1792,256]{2,1,0:T(8,128)}, f32[2,1792,256]{2,1,0:T(8,128)}, u32[]{:S(2)}, u32[]{:S(2)}) collective-permute-start(f32[2,1792,256]{2,1,0:T(8,128)} %collective-permute-done.3.refs_3_), channel_id=1, source_target_pairs={{8,16},{12,20},{19,11},{23,15}} | collective-permute-start | bytes 11010056 | tf_op jit(solution)/shard_map/ppermute | solution.py:248
  248.0 23.2 %collective-permute-start.18 = (f32[2,1024,256]{2,1,0:T(8,128)}, f32[2,1024,256]{2,1,0:T(8,128)S(1)}, u32[]{:S(2)}, u32[]{:S(2)}) collective-permute-start(f32[2,1024,256]{2,1,0:T(8,128)} %broadcast_select_fusion.3.refs_2_), channel_id=1, source_target_pairs={{0,1},{1,0},{2,3},{3,2},{4,5},{5,4},{6,7},{7,6},{8,9},{9,8},{10,11... | collective-permute-start | bytes 6291464 | tf_op jit(solution)/shard_map/ppermute | solution.py:248
  248.9 48.1 %collective-permute-start.14 = (f32[2,1024,256]{2,1,0:T(8,128)}, f32[2,1024,256]{2,1,0:T(8,128)}, u32[]{:S(2)}, u32[]{:S(2)}) collective-permute-start(f32[2,1024,256]{2,1,0:T(8,128)} %collective-permute-done.11.refs_1_.refs_0_.refs_4_), channel_id=1, source_target_pairs={{0,8},{1,9},{4,12},{5,13},{8,0},{9,1},{10,2},{11,3},{12,4},{13,5},... | collective-permute-start | bytes 6291464 | tf_op jit(solution)/shard_map/ppermute | solution.py:248
  252.5 56.7 %collective-permute-start.15 = (f32[2,1024,256]{2,1,0:T(8,128)}, f32[2,1024,256]{2,1,0:T(8,128)S(1)}, u32[]{:S(2)}, u32[]{:S(2)}) collective-permute-start(f32[2,1024,256]{2,1,0:T(8,128)} %broadcast_select_fusion.1), channel_id=1, source_target_pairs={{0,2},{1,3},{2,0},{3,1},{4,6},{5,7},{6,4},{7,5},{8,10},{9,11},{10,... | collective-permute-start | bytes 6291464 | tf_op jit(solution)/shard_map/ppermute | solution.py:248
  262.7 51.3 %collective-permute-start.17 = (f32[2,1024,256]{2,1,0:T(8,128)}, f32[2,1024,256]{2,1,0:T(8,128)}, u32[]{:S(2)}, u32[]{:S(2)}) collective-permute-start(f32[2,1024,256]{2,1,0:T(8,128)} %collective-permute-done.11.refs_1_.refs_0_.refs_4_), channel_id=1, source_target_pairs={{0,1},{1,0},{4,5},{5,4},{8,9},{9,8},{12,13},{13,12},{18,19},{19,18... | collective-permute-start | bytes 6291464 | tf_op jit(solution)/shard_map/ppermute | solution.py:248
  271.3 1.3 copy-start.4
  309.2 10.3 %copy-start.1 = (f32[2,1024,256]{2,1,0:T(8,128)}, f32[2,1024,256]{2,1,0:T(8,128)S(1)}, u32[]{:S(2)}) copy-start(f32[2,1024,256]{2,1,0:T(8,128)S(1)} %collective-permute-done.15.refs_1_.refs_5_.refs_8_) | copy-start | bytes 6291460
  314.0 62.8 %collective-permute-start.22 = (f32[2,1792,256]{2,1,0:T(8,128)}, f32[2,1792,256]{2,1,0:T(8,128)}, u32[]{:S(2)}, u32[]{:S(2)}) collective-permute-start(f32[2,1792,256]{2,1,0:T(8,128)} %collective-permute-done.16.refs_7_.refs_8_.refs_9_), channel_id=1, source_target_pairs={{11,3},{15,7},{16,24},{20,28}} | collective-permute-start | bytes 11010056 | tf_op jit(solution)/shard_map/ppermute | solution.py:248
  319.5 8.7 %collective-permute-start.23 = (f32[2,1024,256]{2,1,0:T(8,128)}, f32[2,1024,256]{2,1,0:T(8,128)S(1)}, u32[]{:S(2)}, u32[]{:S(2)}) collective-permute-start(f32[2,1024,256]{2,1,0:T(8,128)} %get-tuple-element.145), channel_id=1, source_target_pairs={{0,1},{1,0},{2,3},{3,2},{4,5},{5,4},{6,7},{7,6},{8,9},{9,8},{10,11... | collective-permute-start | bytes 6291464 | tf_op jit(solution)/shard_map/ppermute | solution.py:248
  319.5 45.9 %collective-permute-start.19 = (f32[2,1024,256]{2,1,0:T(8,128)S(1)}, f32[2,1024,256]{2,1,0:T(8,128)}, u32[]{:S(2)}, u32[]{:S(2)}) collective-permute-start(f32[2,1024,256]{2,1,0:T(8,128)S(1)} %collective-permute-done.15.refs_1_.refs_5_.refs_8_), channel_id=1, source_target_pairs={{0,8},{1,9},{4,12},{5,13},{8,0},{9,1},{12,4},{13,5},{18,26},{19,27... | collective-permute-start | bytes 6291464 | tf_op jit(solution)/shard_map/ppermute | solution.py:248
  321.5 55.3 %collective-permute-start.20 = (f32[2,1024,256]{2,1,0:T(8,128)}, f32[2,1024,256]{2,1,0:T(8,128)}, u32[]{:S(2)}, u32[]{:S(2)}) collective-permute-start(f32[2,1024,256]{2,1,0:T(8,128)} %shard_map.20), channel_id=1, source_target_pairs={{0,2},{1,3},{4,6},{5,7},{8,10},{9,11},{12,14},{13,15},{18,16},{19,... | collective-permute-start | bytes 6291464 | tf_op jit(solution)/shard_map/ppermute | solution.py:248
  322.8 42.6 %collective-permute-start.21 = (f32[2,768,256]{2,1,0:T(8,128)}, f32[2,768,256]{2,1,0:T(8,128)S(1)}, u32[]{:S(2)}, u32[]{:S(2)}) collective-permute-start(f32[2,768,256]{2,1,0:T(8,128)} %broadcast_select_fusion.5), channel_id=1, source_target_pairs={{8,16},{9,17},{12,20},{13,21},{18,10},{19,11},{22,14},{23,15}} | collective-permute-start | bytes 4718600 | tf_op jit(solution)/shard_map/ppermute | solution.py:248
  328.2 2.0 copy-start
  328.2 60.6 %collective-permute-start.24 = (f32[2,1024,256]{2,1,0:T(8,128)}, f32[2,1024,256]{2,1,0:T(8,128)}, u32[]{:S(2)}, u32[]{:S(2)}) collective-permute-start(f32[2,1024,256]{2,1,0:T(8,128)} %collective-permute-done.14.refs_2_.refs_4_), channel_id=1, source_target_pairs={{0,1},{1,0},{4,5},{5,4},{8,9},{9,8},{12,13},{13,12},{18,19},{19,18... | collective-permute-start | bytes 6291464 | tf_op jit(solution)/shard_map/ppermute | solution.py:248
  365.4 23.4 %copy-start.9 = (f32[2,768,256]{2,1,0:T(8,128)}, f32[2,768,256]{2,1,0:T(8,128)S(1)}, u32[]{:S(2)}) copy-start(f32[2,768,256]{2,1,0:T(8,128)S(1)} %collective-permute-done.21.refs_10_) | copy-start | bytes 4718596
  376.8 12.0 %collective-permute-start.25 = (f32[2,1024,256]{2,1,0:T(8,128)}, f32[2,1024,256]{2,1,0:T(8,128)}, u32[]{:S(2)}, u32[]{:S(2)}) collective-permute-start(f32[2,1024,256]{2,1,0:T(8,128)} %collective-permute-done.19.refs_2_.refs_5_), channel_id=1, source_target_pairs={{0,1},{1,0},{4,5},{5,4},{8,9},{9,8},{12,13},{13,12},{18,19},{19,18... | collective-permute-start | bytes 6291464 | tf_op jit(solution)/shard_map/ppermute | solution.py:248
  378.8 104.0 %collective-permute-start.31 = (f32[2,512,1024]{2,1,0:T(8,128)}, f32[2,512,1024]{2,1,0:T(8,128)}, u32[]{:S(2)}, u32[]{:S(2)}) collective-permute-start(f32[2,512,1024]{2,1,0:T(8,128)} %get-tuple-element.175), channel_id=1, source_target_pairs={{0,4},{4,0},{9,13},{13,9},{18,22},{22,18},{27,31},{31,27}} | collective-permute-start | bytes 12582920 | tf_op jit(solution)/shard_map/ppermute | solution.py:248
  381.4 57.3 %collective-permute-start.26 = (f32[2,1024,256]{2,1,0:T(8,128)}, f32[2,1024,256]{2,1,0:T(8,128)S(1)}, u32[]{:S(2)}, u32[]{:S(2)}) collective-permute-start(f32[2,1024,256]{2,1,0:T(8,128)} %shard_map.22), channel_id=1, source_target_pairs={{0,2},{1,3},{4,6},{5,7},{8,10},{9,11},{12,14},{13,15},{18,16},{19,... | collective-permute-start | bytes 6291464 | tf_op jit(solution)/shard_map/ppermute | solution.py:248
  382.7 53.8 %collective-permute-start.27 = (f32[2,768,256]{2,1,0:T(8,128)S(1)}, f32[2,768,256]{2,1,0:T(8,128)S(1)}, u32[]{:S(2)}, u32[]{:S(2)}) collective-permute-start(f32[2,768,256]{2,1,0:T(8,128)S(1)} %collective-permute-done.21.refs_10_), channel_id=1, source_target_pairs={{10,2},{11,3},{14,6},{15,7},{16,24},{17,25},{20,28},{21,29}} | collective-permute-start | bytes 4718600 | tf_op jit(solution)/shard_map/ppermute | solution.py:248
  407.9 30.8 %collective-permute-start.28 = (f32[2,512,256]{2,1,0:T(8,128)}, f32[2,512,256]{2,1,0:T(8,128)}, u32[]{:S(2)}, u32[]{:S(2)}) collective-permute-start(f32[2,512,256]{2,1,0:T(8,128)} %get-tuple-element.169), channel_id=1, source_target_pairs={{2,6},{3,7},{6,2},{7,3},{10,14},{11,15},{14,10},{15,11},{16,20},{1... | collective-permute-start | bytes 3145736 | tf_op jit(solution)/shard_map/ppermute | solution.py:248
  430.6 52.2 %collective-permute-start.29 = (f32[2,1024,256]{2,1,0:T(8,128)}, f32[2,1024,256]{2,1,0:T(8,128)}, u32[]{:S(2)}, u32[]{:S(2)}) collective-permute-start(f32[2,1024,256]{2,1,0:T(8,128)} %shard_map.24), channel_id=1, source_target_pairs={{0,2},{1,3},{4,6},{5,7},{8,10},{9,11},{12,14},{13,15},{18,16},{19,... | collective-permute-start | bytes 6291464 | tf_op jit(solution)/shard_map/ppermute | solution.py:248
  436.5 7.0 %copy-start.10 = (f32[2,768,256]{2,1,0:T(8,128)}, f32[2,768,256]{2,1,0:T(8,128)S(1)}, u32[]{:S(2)}) copy-start(f32[2,768,256]{2,1,0:T(8,128)S(1)} %collective-permute-done.27.refs_8_) | copy-start | bytes 4718596
  438.8 1.3 copy-start.12
  440.1 96.1 %collective-permute-start.32 = (f32[2,512,1024]{2,1,0:T(8,128)}, f32[2,512,1024]{2,1,0:T(8,128)S(1)}, u32[]{:S(2)}, u32[]{:S(2)}) collective-permute-start(f32[2,512,1024]{2,1,0:T(8,128)} %get-tuple-element.177), channel_id=1, source_target_pairs={{1,5},{5,1},{8,12},{12,8},{19,23},{23,19},{26,30},{30,26}} | collective-permute-start | bytes 12582920 | tf_op jit(solution)/shard_map/ppermute | solution.py:248
  441.0 26.1 %collective-permute-start.30 = (f32[2,512,256]{2,1,0:T(8,128)}, f32[2,512,256]{2,1,0:T(8,128)}, u32[]{:S(2)}, u32[]{:S(2)}) collective-permute-start(f32[2,512,256]{2,1,0:T(8,128)} %get-tuple-element.174), channel_id=1, source_target_pairs={{2,6},{3,7},{6,2},{7,3},{10,14},{11,15},{14,10},{15,11},{16,20},{1... | collective-permute-start | bytes 3145736 | tf_op jit(solution)/shard_map/ppermute | solution.py:248
  482.8 27.0 %collective-permute-start.33 = (f32[2,512,256]{2,1,0:T(8,128)}, f32[2,512,256]{2,1,0:T(8,128)S(1)}, u32[]{:S(2)}, u32[]{:S(2)}) collective-permute-start(f32[2,512,256]{2,1,0:T(8,128)} %get-tuple-element.186), channel_id=1, source_target_pairs={{2,6},{3,7},{6,2},{7,3},{10,14},{11,15},{14,10},{15,11},{16,20},{1... | collective-permute-start | bytes 3145736 | tf_op jit(solution)/shard_map/ppermute | solution.py:248
  509.8 26.4 %copy-start.13 = (f32[2,512,256]{2,1,0:T(8,128)}, f32[2,512,256]{2,1,0:T(8,128)S(1)}, u32[]{:S(2)}) copy-start(f32[2,512,256]{2,1,0:T(8,128)S(1)} %collective-permute-done.33.refs_10_) | copy-start | bytes 3145732
  509.8 26.4 %collective-permute-start.34 = (f32[2,512,256]{2,1,0:T(8,128)}, f32[2,512,256]{2,1,0:T(8,128)S(1)}, u32[]{:S(2)}, u32[]{:S(2)}) collective-permute-start(f32[2,512,256]{2,1,0:T(8,128)} %get-tuple-element.188), channel_id=1, source_target_pairs={{2,6},{3,7},{6,2},{7,3},{10,14},{11,15},{14,10},{15,11},{16,20},{1... | collective-permute-start | bytes 3145736 | tf_op jit(solution)/shard_map/ppermute | solution.py:248
  536.2 1.0 copy-start.14
  536.2 2.3 copy-start.11

commit v3 on v2

--- a/solution.py
+++ b/solution.py
@@ -40,7 +40,7 @@
         out[2 * c, rows, at : at + k], out[2 * c + 1, rows, at : at + k] = split(v)
 
 
-def product_kernel(role_ref, *refs, picks, lefts, rights, more, halves, fetch, depth, keep):
+def product_kernel(role_ref, *refs, picks, lefts, rights, more, halves, fetch, depth, keep, negate):
     left, candidates, rest = refs[:lefts], refs[lefts : lefts + rights], refs[lefts + rights :]
     base, rest = (rest[0], rest[1:]) if more else (None, rest)
     outs, rest = rest[:halves], rest[halves:]
@@ -95,10 +95,11 @@
             parts = multiply_split(rest[1], slice(None), scratch)
         for h, out in enumerate(outs):
 
-            @pl.when(i * halves // pl.num_programs(1) == h)
+            @pl.when(i * min(halves, 2) // pl.num_programs(1) == min(h, 1))
             def _():
-                for c in range(2):
-                    out[c] = parts[c] if base is None else parts[c] + base[c]
+                for at, c in enumerate((h - 1,) if halves == 3 and h else (0, 1)):
+                    value = parts[c] if base is None else parts[c] + base[c]
+                    out[at] = -value if negate else value
 
 
 def multiply_split(left, columns, right):
@@ -113,7 +114,7 @@
     return rr - ii, ss - rr - ii
 
 
-def product(role, left, rights, picks, columns, base=None, half=None, halves=1, fetch=False, keep=False):
+def product(role, left, rights, picks, columns, base=None, half=None, halves=1, fetch=False, keep=False, negate=False):
     split_left = not isinstance(left, list)
     lefts = [left] if split_left else left
     rows = lefts[0].shape[1]
@@ -157,14 +158,18 @@
         scratch.append(pltpu.SemaphoreType.DMA((max(len(v) for v in every),)))
     body = functools.partial(
         product_kernel, picks=picks, lefts=len(lefts), rights=len(rights), more=base is not None, halves=halves, fetch=fetch,
-        depth=depth, keep=keep,
-    )
-    steps = rows // mb // halves
+        depth=depth, keep=keep, negate=negate,
+    )
+    steps = rows // mb // min(halves, 2)
+    counts = (2, 1, 1) if halves == 3 else (2,) * halves
     out_specs = [
-        pl.BlockSpec((2, mb, nb), lambda j, i, r, h=h: (0, jnp.clip(i - h * steps, 0, steps - 1) * on(r), j * on(r)))
-        for h in range(halves)
+        pl.BlockSpec(
+            (c, mb, nb),
+            lambda j, i, r, h=min(h, 1): (0, jnp.clip(i - h * steps, 0, steps - 1) * on(r), j * on(r)),
+        )
+        for h, c in enumerate(counts)
     ]
-    out_shape = [jax.ShapeDtypeStruct((2, rows // halves, columns), jnp.float32)] * halves
+    out_shape = [jax.ShapeDtypeStruct((c, steps * mb, columns), jnp.float32) for c in counts]
     if keep:
         out_specs.append(pl.BlockSpec((6, mb, total), lambda j, i, r: (0, i, 0)))
         out_shape.append(jax.ShapeDtypeStruct((6, rows, total), jnp.bfloat16))
@@ -185,40 +190,63 @@
 
 
 def place_kernel(role_ref, *refs):
-    (totals, gots, tops, crossed), out = (refs[:2], refs[2:4], refs[4:8], refs[8:12]), refs[12]
+    totals, gots, tops, crossed, out = refs[:2], refs[2:5], refs[5:9], refs[9:13], refs[13]
     f, j = pl.program_id(0), pl.program_id(1)
     kept = role_ref[1] == f
-    for sources, flag in ((totals, kept), (gots, jnp.logical_not(kept))):
-        for role, ref in enumerate(sources):
-
-            @pl.when(flag & (role_ref[0] == role))
-            def _():
-                out[:, 0] = -ref[...]
+    for role, ref in enumerate(totals):
+
+        @pl.when(kept & (role_ref[0] == role))
+        def _():
+            out[:, 0] = ref[...]
+
+    @pl.when(jnp.logical_not(kept) & (role_ref[0] == 0))
+    def _():
+        out[:, 0] = gots[0][...]
+
+    @pl.when(jnp.logical_not(kept) & (role_ref[0] == 1))
+    def _():
+        out[0, 0], out[1, 0] = gots[1][0], gots[2][0]
 
     for sources, flag in ((tops, kept), (crossed, jnp.logical_not(kept))):
         for step, ref in enumerate(sources):
 
             @pl.when(flag & (role_ref[0] >= 2) & (j == step))
             def _():
-                out[:, 0] = -ref[...]
+                out[:, 0] = ref[...]
 
 
 def place(role, totals, gots, tops, crossed):
     _, rows, columns = totals[0].shape
-    w = columns // CHUNKS
-    in_specs = [
-        pl.BlockSpec((2, rows, w), lambda f, j, r, k=k: (0, 0, j * jnp.where(r[0] == k, 1, 0))) for k in (0, 1, 0, 1)
-    ] + [pl.BlockSpec((2, rows, w), lambda f, j, r: (0, 0, 0))] * 8
+    w, steps = columns // CHUNKS, 2
+    block = rows // steps
+
+    def wide(role_, first, count):
+        def at(f, j, i, r):
+            used = jnp.where((r[0] == role_) & ((r[1] == f) == first), 1, 0)
+            return (0, i * used, j * used)
+
+        return pl.BlockSpec((count, block, w), at)
+
+    def narrow(step, first):
+        def at(f, j, i, r):
+            used = jnp.where((r[0] >= 2) & ((r[1] == f) == first) & (j == step), 1, 0)
+            return (0, i * used, 0)
+
+        return pl.BlockSpec((2, block, w), at)
+
+    uses = ((0, True, 2), (1, True, 2), (0, False, 2), (1, False, 1), (1, False, 1))
+    in_specs = [wide(*use) for use in uses]
+    in_specs += [narrow(step, first) for first in (True, False) for step in range(CHUNKS)]
     return pl.pallas_call(
         place_kernel,
         grid_spec=pltpu.PrefetchScalarGridSpec(
             num_scalar_prefetch=1,
-            grid=(2, CHUNKS),
+            grid=(2, CHUNKS, steps),
             in_specs=in_specs,
-            out_specs=pl.BlockSpec((2, 1, rows, w), lambda f, j, r: (0, f, 0, (j + 2 * f) % CHUNKS)),
+            out_specs=pl.BlockSpec((2, 1, block, w), lambda f, j, i, r: (0, f, i, (j + 2 * f) % CHUNKS)),
         ),
         out_shape=jax.ShapeDtypeStruct((2, 2, rows, columns), jnp.float32),
-        compiler_params=pltpu.CompilerParams(vmem_limit_bytes=56 * 2**20),
+        compiler_params=pltpu.CompilerParams(vmem_limit_bytes=40 * 2**20),
         cost_estimate=pl.CostEstimate(flops=1000, bytes_accessed=1000, transcendentals=0),
     )(role, *totals, *gots, *tops, *crossed)
 
@@ -339,7 +367,7 @@
         rights = (these if 0 in active else []) + (others if 1 in active else [])
         first_of = {0: 0, 1: len(rights) - k}
         picks = {v: [[whole(first_of[v] + i, n, i * w, True) for i in range(k)]] for v in active}
-        return product(roles, these, rights, picks, n, base=total, halves=halves, fetch=True)
+        return product(roles, these, rights, picks, n, base=total, halves=halves, fetch=True, negate=halves > 1)
 
     shares, shared = [None] * 4, [None] * 4
     there[1] = send(right[1], swap_slab, outward)
@@ -389,9 +417,9 @@
     shares[2], total, swapped = sync(shares[2], total, swapped)
     cores[3] = swapped
     keep_first, to_first = add_rights(total, (2, 3), (0,), 2)
-    there[3], shared[1], near4, far3, swapped, shares[2], keep_first, to_first, total = sync(
-        there[3], shared[1], near4, far3, swapped, shares[2], keep_first, to_first, total
-    )
+    to_first, swapped, far3, near3 = sync(to_first, swapped, far3, near3)
+
+    far4 = near4
 
     def rest(j, base):
         rights = seen[:3] + seen_cores[:2] + [swapped, far3, far4, near3, near4]
@@ -404,35 +432,40 @@
             picks[k + 1] += [(v, j * w, w, True, n + i * w, 0) for i, v in enumerate((3, 4, 5, 2))]
         used = sorted({entry[0] for pieces in picks.values() for entry in pieces})
         picks = {r: [[(used.index(e[0]),) + e[1:] for e in v]] for r, v in picks.items()}
-        return product(roles, left, [rights[i] for i in used], picks, w, base=base, halves=2, fetch=True)
+        return product(roles, left, [rights[i] for i in used], picks, w, base=base, halves=2, fetch=True, negate=True)
 
     tops, downs, crossed = [None] * 4, [None] * 4, [None] * 4
+    tops[0], downs[0] = rest(0, shared[0])
+    there[3], shared[1], near4, far3, swapped, shares[2], keep_first, to_first, total, downs[0] = sync(
+        there[3], shared[1], near4, far3, swapped, shares[2], keep_first, to_first, total, downs[0]
+    )
+
+    far4 = send(near4, outward)
     shared[2] = send(shares[2], to_off)
-    far4 = send(near4, outward)
     seen_cores[2] = send(there[2], swap_core_diag)
+    got_first = send(to_first, x_first)
     seen_cores[3] = send(there[3], swap_core_diag)
-    got_first = send(to_first, x_first)
+    crossed[0] = send(downs[0], x_off)
     shares[3] = share(3)
-    shares[3], shared[0], seen_cores[2], seen_cores[3] = sync(shares[3], shared[0], seen_cores[2], seen_cores[3])
+    shares[3], shared[1], seen_cores[2], seen_cores[3] = sync(shares[3], shared[1], seen_cores[2], seen_cores[3])
     shared[3] = send(shares[3], to_off)
-    tops[0], downs[0] = rest(0, shared[0])
-    downs[0], shared[1] = sync(downs[0], shared[1])
-    crossed[0] = send(downs[0], x_off)
     tops[1], downs[1] = rest(1, shared[1])
-    downs[1], total = sync(downs[1], total)
+    downs[1], total, crossed[0] = sync(downs[1], total, crossed[0])
     crossed[1] = send(downs[1], x_off)
-    keep_second, to_second = add_rights(total, (2, 3), (1,), 2)
-    to_second, shared[2], far4, crossed[0] = sync(to_second, shared[2], far4, crossed[0])
-    got_second = send(to_second, x_second)
+    keep_second, *to_second = add_rights(total, (2, 3), (1,), 3)
+    to_second[0], to_second[1], shared[2], far4 = sync(*to_second, shared[2], far4)
+    got_second = [send(v, x_second) for v in to_second]
     tops[2], downs[2] = rest(2, shared[2])
-    downs[2], shared[3], crossed[1], got_first = sync(downs[2], shared[3], crossed[1], got_first)
+    downs[2], crossed[1], got_first, far3 = sync(downs[2], crossed[1], got_first, far3)
     crossed[2] = send(downs[2], x_off)
-    tops[3], downs[3] = rest(3, shared[3])
-    downs[3], crossed[2] = sync(downs[3], crossed[2])
+    tops[3], downs[3] = rest(3, None)
+    tops[3], downs[3], shared[3], crossed[2] = sync(tops[3], downs[3], shared[3], crossed[2])
+    downs[3] = downs[3] - shared[3][:, part:]
     crossed[3] = send(downs[3], x_off)
+    tops[3] = tops[3] - shared[3][:, :part]
 
     flags = jnp.stack([role, x.astype(jnp.int32)])
-    return place(flags, [keep_first, keep_second], [got_first, got_second], tops, crossed)
+    return place(flags, [keep_first, keep_second], [got_first] + got_second, tops, crossed)
 
 
 def solution(mesh):

time: 559 us -> 537 us (0.961)
  waiting for transfers between devices: 267 us -> 247 us
    ppermute x35 -> x36, waiting for transfers between devices: 267 us -> 247 us  [send(): return lax.ppermute(value, AXES, pairs)]
    ppermute x35 -> x36, starting transfers between devices: 90.8 us -> 91.8 us  [send(): return lax.ppermute(value, AXES, pairs)]
  transfers between devices with their start and end apart: 35 -> 36, of which waited for: 15 -> 13; matrix products, arithmetic and copies ran while one was open for 6% -> 7% of each run, Pallas kernels for 23% -> 24%
where the time goes in v3:
time: 537 us; the launch traced here: 532 us
  waiting for transfers between devices  247 us (46%)
  Pallas kernels  136 us (25%)
  starting transfers between devices  91.8 us (17%)
  other arithmetic  39.6 us (7%)
  local copies, waits for them, and re-layouts  15.9 us (3%)
    ppermute x36, waiting for transfers between devices, send(): return lax.ppermute(value, AXES, pairs)  247 us
    pallas_call x13, Pallas kernels, product(): pl.pallas_call(body, grid_spec=pltpu.PrefetchScalarGridSpec(num_scalar_pr...  125 us
    ppermute x36, starting transfers between devices, send(): return lax.ppermute(value, AXES, pairs)  91.8 us
    pallas_call x1, Pallas kernels, place(): pl.pallas_call(place_kernel, grid_spec=pltpu.PrefetchScalarGridSpec(num_s...  11.2 us
  transfers between devices with their start and end apart: 36, of which 13 were waited for; matrix products, arithmetic and copies ran while one was open for 7% of the time, Pallas kernels for 24%

profile of v3, /device:TPU:16, one launch (start us, length us, event | category | flops | bytes accessed | tf_op | source)
XLA Modules:
  0.0 531.6 jit_solution(15117278076759037920)
XLA Ops:
  0.0 6.8 %dynamic-slice_bitcast_fusion.3 = (f32[2,512,512]{2,1,0:T(8,128)}, f32[2,512,512]{2,1,0:T(8,128)S(1)}, f32[2,512,512]{2,1,0:T(8,128)}, f32[2,512,512]{2,1,0:T(8,128)S(1)}) fusion(f32[2,2,512,1024]{3,2,1,0:T(8,128)} %param.1, s32[]{:T(128)S(6)} %select_n.129, s32[]{:T(128)S(6)} %select_n.131, s32[]{:T(128)S(6)} %select_n.133, s32[]{:T(128)S(6)} %select_n.134, ...), kind=kLoop, calls=%fused_computation.22 | loop fusion | bytes 16777240 | tf_op jit(solution)/shard_map/squeeze | solution.py:303
  6.8 1.5 collective-permute-start
  8.3 45.9 %collective-permute-done = f32[2,512,512]{2,1,0:T(8,128)S(1)} collective-permute-done((f32[2,512,512]{2,1,0:T(8,128)S(1)}, f32[2,512,512]{2,1,0:T(8,128)S(1)}, u32[]{:S(2)}, u32[]{:S(2)}) %collective-permute-start) | collective-permute-done | bytes 2097184 | tf_op jit(solution)/shard_map/ppermute | solution.py:276
  54.4 2.3 fusion.3
  56.7 3.7 pad_maximum_fusion.2
  60.4 2.6 pad_maximum_fusion.refs_0_.refs_6_.refs_1_
  63.0 2.4 collective-permute-start.3
  65.5 1.5 collective-permute-start.1
  66.9 6.2 %collective-permute-start.2 = (f32[2,1024,256]{2,1,0:T(8,128)}, f32[2,1024,256]{2,1,0:T(8,128)S(1)}, u32[]{:S(2)}, u32[]{:S(2)}) collective-permute-start(f32[2,1024,256]{2,1,0:T(8,128)} %get-tuple-element.106), channel_id=1, source_target_pairs={{2,0},{3,1},{6,4},{7,5},{8,16},{9,17},{10,8},{11,9},{12,20},{13,21... | collective-permute-start | bytes 6291464 | tf_op jit(solution)/shard_map/ppermute | solution.py:276
  73.3 1.5 slice.46
  74.8 39.0 %collective-permute-done.1 = f32[2,512,512]{2,1,0:T(8,128)} collective-permute-done((f32[2,512,512]{2,1,0:T(8,128)}, f32[2,512,512]{2,1,0:T(8,128)}, u32[]{:S(2)}, u32[]{:S(2)}) %collective-permute-start.1) | collective-permute-done | bytes 2097184 | tf_op jit(solution)/shard_map/ppermute | solution.py:276
  117.6 4.2 pad_maximum_fusion.1.refs_1_.refs_7_.refs_2_
  121.8 4.4 fusion.1
  126.3 4.8 collective-permute-start.5
  131.1 1.9 collective-permute-start.6
  133.0 2.0 collective-permute-start.9
  135.1 2.0 collective-permute-start.8
  137.1 16.9 %shard_map.17 = (f32[2,1024,1024]{2,1,0:T(8,128)}, bf16[6,1024,2048]{2,1,0:T(8,128)(2,1)}) custom-call(s32[1]{0:T(128)} %bitcast.role_ref, f32[2,1024,512]{2,1,0:T(8,128)} %pad_maximum_fusion.refs_0_.refs_6_.refs_1_, f32[2,1024,512]{2,1,0:T(8,128)} %pad_maximum_fusion.1.refs_1_.refs_7_.refs_2_, f32[2,1024,512]{2,1,0:T(8,128)} %collective-permute-done.4.refs_2_.refs_4_, ...), custom_call_target="tpu_custom_call" | custom-call | flops 1000 | bytes 1000 | tf_op jit(solution)/shard_map/pallas_call | solution.py:176
  154.0 21.3 %collective-permute-done.5.refs_2_.refs_8_ = f32[2,1024,256]{2,1,0:T(8,128)} collective-permute-done((f32[2,1024,256]{2,1,0:T(8,128)S(1)}, f32[2,1024,256]{2,1,0:T(8,128)}, u32[]{:S(2)}, u32[]{:S(2)}) %collective-permute-start.5) | collective-permute-done | bytes 2097184 | tf_op jit(solution)/shard_map/ppermute | solution.py:276
  175.3 5.7 %collective-permute-done.6.refs_1_.refs_5_ = f32[2,1024,256]{2,1,0:T(8,128)} collective-permute-done((f32[2,1024,256]{2,1,0:T(8,128)}, f32[2,1024,256]{2,1,0:T(8,128)}, u32[]{:S(2)}, u32[]{:S(2)}) %collective-permute-start.6) | collective-permute-done | bytes 2097184 | tf_op jit(solution)/shard_map/ppermute | solution.py:276
  182.7 3.9 slice_select_fusion
  186.6 2.6 collective-permute-start.10
  189.2 2.0 collective-permute-start.12
  191.2 10.1 %collective-permute-start.11 = (f32[2,1024,256]{2,1,0:T(8,128)}, f32[2,1024,256]{2,1,0:T(8,128)}, u32[]{:S(2)}, u32[]{:S(2)}) collective-permute-start(f32[2,1024,256]{2,1,0:T(8,128)} %slice_select_fusion), channel_id=1, source_target_pairs={{2,0},{3,1},{6,4},{7,5},{8,16},{9,17},{10,8},{11,9},{12,20},{13,21... | collective-permute-start | bytes 6291464 | tf_op jit(solution)/shard_map/ppermute | solution.py:276
  201.7 3.6 shard_map.19
  205.3 4.0 shard_map.18.refs_12_
  209.3 3.3 broadcast_select_fusion.1
  212.6 20.3 %collective-permute-done.10.refs_2_.refs_9_ = f32[2,1024,256]{2,1,0:T(8,128)} collective-permute-done((f32[2,1024,256]{2,1,0:T(8,128)}, f32[2,1024,256]{2,1,0:T(8,128)}, u32[]{:S(2)}, u32[]{:S(2)}) %collective-permute-start.10) | collective-permute-done | bytes 2097184 | tf_op jit(solution)/shard_map/ppermute | solution.py:276
  232.9 3.2 broadcast_select_fusion.3.refs_2_
  236.1 10.7 %collective-permute-done.11.refs_1_.refs_0_.refs_4_ = f32[2,1024,256]{2,1,0:T(8,128)} collective-permute-done((f32[2,1024,256]{2,1,0:T(8,128)}, f32[2,1024,256]{2,1,0:T(8,128)}, u32[]{:S(2)}, u32[]{:S(2)}) %collective-permute-start.11) | collective-permute-done | bytes 2097184 | tf_op jit(solution)/shard_map/ppermute | solution.py:276
  249.0 3.5 collective-permute-start.14
  252.5 10.5 %collective-permute-start.15 = (f32[2,1024,256]{2,1,0:T(8,128)}, f32[2,1024,256]{2,1,0:T(8,128)S(1)}, u32[]{:S(2)}, u32[]{:S(2)}) collective-permute-start(f32[2,1024,256]{2,1,0:T(8,128)} %broadcast_select_fusion.1), channel_id=1, source_target_pairs={{0,2},{1,3},{2,0},{3,1},{4,6},{5,7},{6,4},{7,5},{8,10},{9,11},{10,... | collective-permute-start | bytes 6291464 | tf_op jit(solution)/shard_map/ppermute | solution.py:276
  263.0 2.0 collective-permute-start.17
  265.0 3.8 shard_map.20
  268.7 2.8 broadcast_select_fusion.5
  272.8 3.6 shard_map.21.refs_8_
  276.5 20.6 %collective-permute-done.14.refs_2_.refs_4_ = f32[2,1024,256]{2,1,0:T(8,128)} collective-permute-done((f32[2,1024,256]{2,1,0:T(8,128)}, f32[2,1024,256]{2,1,0:T(8,128)}, u32[]{:S(2)}, u32[]{:S(2)}) %collective-permute-start.14) | collective-permute-done | bytes 2097184 | tf_op jit(solution)/shard_map/ppermute | solution.py:276
  297.0 12.4 %collective-permute-done.15.refs_1_.refs_5_.refs_8_ = f32[2,1024,256]{2,1,0:T(8,128)S(1)} collective-permute-done((f32[2,1024,256]{2,1,0:T(8,128)}, f32[2,1024,256]{2,1,0:T(8,128)S(1)}, u32[]{:S(2)}, u32[]{:S(2)}) %collective-permute-start.15) | collective-permute-done | bytes 2097184 | tf_op jit(solution)/shard_map/ppermute | solution.py:276
  309.5 4.8 broadcast_select_fusion
  314.2 5.4 %collective-permute-start.23 = (f32[2,1792,256]{2,1,0:T(8,128)}, f32[2,1792,256]{2,1,0:T(8,128)}, u32[]{:S(2)}, u32[]{:S(2)}) collective-permute-start(f32[2,1792,256]{2,1,0:T(8,128)} %collective-permute-done.16.refs_7_.refs_8_.refs_9_), channel_id=1, source_target_pairs={{11,3},{15,7},{16,24},{20,28}} | collective-permute-start | bytes 11010056 | tf_op jit(solution)/shard_map/ppermute | solution.py:276
  319.7 2.1 collective-permute-start.19
  324.3 3.9 shard_map.22
  328.2 1.3 copy-done.5
  329.5 4.3 shard_map.23
  333.8 24.7 %collective-permute-done.23.refs_6_.refs_7_ = f32[2,1792,256]{2,1,0:T(8,128)} collective-permute-done((f32[2,1792,256]{2,1,0:T(8,128)}, f32[2,1792,256]{2,1,0:T(8,128)}, u32[]{:S(2)}, u32[]{:S(2)}) %collective-permute-start.23) | collective-permute-done | bytes 3670048 | tf_op jit(solution)/shard_map/ppermute | solution.py:276
  358.6 19.4 %shard_map.24 = (f32[2,512,256]{2,1,0:T(8,128)}, f32[2,512,256]{2,1,0:T(8,128)}) custom-call(s32[1]{0:T(128)} %bitcast.role_ref, bf16[6,1024,2048]{2,1,0:T(8,128)(2,1)} %get-tuple-element.128.refs_0_, f32[2,1024,256]{2,1,0:T(8,128)} %copy-done.7, f32[2,1024,256]{2,1,0:T(8,128)} %get-tuple-element.204.refs_2_.refs_3_, f32[2,1024,256]{2,1,0:T(8,128)} %copy-done.8, ...), custom_call_target="tpu_custom_call" | custom-call | flops 1000 | bytes 1000 | tf_op jit(solution)/shard_map/pallas_call | solution.py:176
  378.1 2.6 collective-permute-start.30
  380.7 2.0 collective-permute-start.24
  382.7 2.0 collective-permute-start.25
  386.0 3.4 collective-permute-start.26
  389.4 4.5 collective-permute-start.28
  393.9 3.8 shard_map.25
  397.7 19.1 %shard_map.26 = (f32[2,512,256]{2,1,0:T(8,128)}, f32[2,512,256]{2,1,0:T(8,128)}) custom-call(s32[1]{0:T(128)} %bitcast.role_ref, bf16[6,1024,2048]{2,1,0:T(8,128)(2,1)} %get-tuple-element.128.refs_0_, f32[2,1024,256]{2,1,0:T(8,128)} %copy-done.7, f32[2,1024,256]{2,1,0:T(8,128)} %broadcast_select_fusion.3.refs_2_, ...), custom_call_target="tpu_custom_call" | custom-call | flops 1000 | bytes 1000 | tf_op jit(solution)/shard_map/pallas_call | solution.py:176
  416.9 2.4 collective-permute-start.29
  420.6 4.6 shard_map.27
  425.2 20.7 %collective-permute-done.27.refs_11_ = f32[2,1024,256]{2,1,0:T(8,128)} collective-permute-done((f32[2,1024,256]{2,1,0:T(8,128)}, f32[2,1024,256]{2,1,0:T(8,128)}, u32[]{:S(2)}, u32[]{:S(2)}) %collective-permute-start.27) | collective-permute-done | bytes 2097184 | tf_op jit(solution)/shard_map/ppermute | solution.py:276
  445.9 19.3 %shard_map.28 = (f32[2,512,256]{2,1,0:T(8,128)}, f32[2,512,256]{2,1,0:T(8,128)}) custom-call(s32[1]{0:T(128)} %bitcast.role_ref, bf16[6,1024,2048]{2,1,0:T(8,128)(2,1)} %get-tuple-element.128.refs_0_, f32[2,1024,256]{2,1,0:T(8,128)} %copy-done.7, f32[2,1024,256]{2,1,0:T(8,128)} %broadcast_select_fusion.3.refs_2_, ...), custom_call_target="tpu_custom_call" | custom-call | flops 1000 | bytes 1000 | tf_op jit(solution)/shard_map/pallas_call | solution.py:176
  466.3 2.4 collective-permute-start.34
  470.4 19.0 %shard_map.29 = (f32[2,512,256]{2,1,0:T(8,128)}, f32[2,512,256]{2,1,0:T(8,128)}) custom-call(s32[1]{0:T(128)} %bitcast.role_ref, bf16[6,1024,2048]{2,1,0:T(8,128)(2,1)} %get-tuple-element.128.refs_0_, f32[2,1024,256]{2,1,0:T(8,128)} %copy-done.7, f32[2,1024,256]{2,1,0:T(8,128)} %broadcast_select_fusion.3.refs_2_, ...), custom_call_target="tpu_custom_call" | custom-call | flops 1000 | bytes 1000 | tf_op jit(solution)/shard_map/pallas_call | solution.py:176
  490.3 2.2 collective-permute-done.34.refs_11_
  492.4 2.6 slice_subtract_fusion
  495.0 2.4 collective-permute-start.35
  497.6 22.3 %collective-permute-done.35.refs_12_ = f32[2,512,256]{2,1,0:T(8,128)S(1)} collective-permute-done((f32[2,512,256]{2,1,0:T(8,128)S(1)}, f32[2,512,256]{2,1,0:T(8,128)S(1)}, u32[]{:S(2)}, u32[]{:S(2)}) %collective-permute-start.35) | collective-permute-done | bytes 1048608 | tf_op jit(solution)/shard_map/ppermute | solution.py:276
  519.9 11.2 %shard_map.30 = f32[2,2,512,1024]{3,2,1,0:T(8,128)} custom-call(s32[2]{0:T(128)S(1)} %pad_add_fusion.role_ref, f32[2,512,1024]{2,1,0:T(8,128)} %get-tuple-element.164.refs_0_, f32[2,512,1024]{2,1,0:T(8,128)} %get-tuple-element.176.refs_1_, f32[2,512,1024]{2,1,0:T(8,128)} %collective-permute-done.30.refs_2_, ...), custom_call_target="tpu_custom_call" | custom-call | flops 1000 | bytes 1000 | tf_op jit(solution)/shard_map/pallas_call | solution.py:240
  (71 shorter events, 18.3 us)
Async XLA Ops:
  6.8 47.4 %collective-permute-start = (f32[2,512,512]{2,1,0:T(8,128)S(1)}, f32[2,512,512]{2,1,0:T(8,128)S(1)}, u32[]{:S(2)}, u32[]{:S(2)}) collective-permute-start(f32[2,512,512]{2,1,0:T(8,128)S(1)} %get-tuple-element.208), channel_id=1, source_target_pairs={{0,4},{1,5},{2,6},{3,7},{4,0},{5,1},{6,2},{7,3},{8,12},{9,13},{10,... | collective-permute-start | bytes 6291464 | tf_op jit(solution)/shard_map/ppermute | solution.py:276
  63.0 63.2 %collective-permute-start.4 = (f32[2,1024,512]{2,1,0:T(8,128)}, f32[2,1024,512]{2,1,0:T(8,128)}, u32[]{:S(2)}, u32[]{:S(2)}) collective-permute-start(f32[2,1024,512]{2,1,0:T(8,128)} %pad_maximum_fusion.refs_0_.refs_6_.refs_1_), channel_id=1, source_target_pairs={{0,1},{1,0},{2,3},{3,2},{4,5},{5,4},{6,7},{7,6},{8,9},{9,8},{10,11... | collective-permute-start | bytes 12582920 | tf_op jit(solution)/shard_map/ppermute | solution.py:276
  63.0 63.2 %collective-permute-start.3 = (f32[2,1792,256]{2,1,0:T(8,128)}, f32[2,1792,256]{2,1,0:T(8,128)}, u32[]{:S(2)}, u32[]{:S(2)}) collective-permute-start(f32[2,1792,256]{2,1,0:T(8,128)} %pad_maximum_fusion.2), channel_id=1, source_target_pairs={{0,8},{4,12},{9,1},{13,5},{18,26},{22,30},{27,19},{31,23}} | collective-permute-start | bytes 11010056 | tf_op jit(solution)/shard_map/ppermute | solution.py:276
  65.5 48.4 %collective-permute-start.1 = (f32[2,512,512]{2,1,0:T(8,128)}, f32[2,512,512]{2,1,0:T(8,128)}, u32[]{:S(2)}, u32[]{:S(2)}) collective-permute-start(f32[2,512,512]{2,1,0:T(8,128)} %get-tuple-element.104), channel_id=1, source_target_pairs={{0,4},{1,5},{2,6},{3,7},{4,0},{5,1},{6,2},{7,3},{8,12},{9,13},{10,... | collective-permute-start | bytes 6291464 | tf_op jit(solution)/shard_map/ppermute | solution.py:276
  66.9 59.3 %collective-permute-start.2 = (f32[2,1024,256]{2,1,0:T(8,128)}, f32[2,1024,256]{2,1,0:T(8,128)S(1)}, u32[]{:S(2)}, u32[]{:S(2)}) collective-permute-start(f32[2,1024,256]{2,1,0:T(8,128)} %get-tuple-element.106), channel_id=1, source_target_pairs={{2,0},{3,1},{6,4},{7,5},{8,16},{9,17},{10,8},{11,9},{12,20},{13,21... | collective-permute-start | bytes 6291464 | tf_op jit(solution)/shard_map/ppermute | solution.py:276
  115.1 2.5 copy-start.11
  117.6 4.2 copy-start.12
  126.2 54.9 %copy-start.10 = (f32[2,1024,256]{2,1,0:T(8,128)}, f32[2,1024,256]{2,1,0:T(8,128)S(1)}, u32[]{:S(2)}) copy-start(f32[2,1024,256]{2,1,0:T(8,128)S(1)} %collective-permute-done.2.refs_1_.refs_0_.refs_4_) | copy-start | bytes 6291460
  126.2 10.9 %collective-permute-start.7 = (f32[2,1024,512]{2,1,0:T(8,128)}, f32[2,1024,512]{2,1,0:T(8,128)}, u32[]{:S(2)}, u32[]{:S(2)}) collective-permute-start(f32[2,1024,512]{2,1,0:T(8,128)} %pad_maximum_fusion.1.refs_1_.refs_7_.refs_2_), channel_id=1, source_target_pairs={{0,1},{1,0},{2,3},{3,2},{4,5},{5,4},{6,7},{7,6},{8,9},{9,8},{10,11... | collective-permute-start | bytes 12582920 | tf_op jit(solution)/shard_map/ppermute | solution.py:276
  126.3 49.0 %collective-permute-start.5 = (f32[2,1024,256]{2,1,0:T(8,128)S(1)}, f32[2,1024,256]{2,1,0:T(8,128)}, u32[]{:S(2)}, u32[]{:S(2)}) collective-permute-start(f32[2,1024,256]{2,1,0:T(8,128)S(1)} %collective-permute-done.2.refs_1_.refs_0_.refs_4_), channel_id=1, source_target_pairs={{0,8},{1,9},{4,12},{5,13},{8,0},{9,1},{10,2},{11,3},{12,4},{13,5},... | collective-permute-start | bytes 6291464 | tf_op jit(solution)/shard_map/ppermute | solution.py:276
  131.1 49.9 %collective-permute-start.6 = (f32[2,1024,256]{2,1,0:T(8,128)}, f32[2,1024,256]{2,1,0:T(8,128)}, u32[]{:S(2)}, u32[]{:S(2)}) collective-permute-start(f32[2,1024,256]{2,1,0:T(8,128)} %get-tuple-element.110), channel_id=1, source_target_pairs={{2,0},{3,1},{6,4},{7,5},{8,16},{9,17},{10,8},{11,9},{12,20},{13,21... | collective-permute-start | bytes 6291464 | tf_op jit(solution)/shard_map/ppermute | solution.py:276
  133.0 53.5 %collective-permute-start.9 = (f32[2,1024,256]{2,1,0:T(8,128)S(1)}, f32[2,1024,256]{2,1,0:T(8,128)}, u32[]{:S(2)}, u32[]{:S(2)}) collective-permute-start(f32[2,1024,256]{2,1,0:T(8,128)S(1)} %collective-permute-done.2.refs_1_.refs_0_.refs_4_), channel_id=1, source_target_pairs={{0,1},{1,0},{4,5},{5,4},{8,9},{9,8},{12,13},{13,12},{18,19},{19,18... | collective-permute-start | bytes 6291464 | tf_op jit(solution)/shard_map/ppermute | solution.py:276
  135.1 51.5 %collective-permute-start.8 = (f32[2,768,256]{2,1,0:T(8,128)}, f32[2,768,256]{2,1,0:T(8,128)}, u32[]{:S(2)}, u32[]{:S(2)}) collective-permute-start(f32[2,768,256]{2,1,0:T(8,128)} %pad_maximum_fusion.3), channel_id=1, source_target_pairs={{0,8},{4,12},{9,1},{13,5},{18,26},{22,30},{27,19},{31,23}} | collective-permute-start | bytes 4718600 | tf_op jit(solution)/shard_map/ppermute | solution.py:276
  181.1 1.6 copy-start.13
  182.7 18.7 %copy-start.7 = (f32[2,1024,256]{2,1,0:T(8,128)}, f32[2,1024,256]{2,1,0:T(8,128)S(1)}, u32[]{:S(2)}) copy-start(f32[2,1024,256]{2,1,0:T(8,128)S(1)} %broadcast_select_fusion.4.refs_1_) | copy-start | bytes 6291460
  186.6 46.3 %collective-permute-start.10 = (f32[2,1024,256]{2,1,0:T(8,128)}, f32[2,1024,256]{2,1,0:T(8,128)}, u32[]{:S(2)}, u32[]{:S(2)}) collective-permute-start(f32[2,1024,256]{2,1,0:T(8,128)} %collective-permute-done.6.refs_1_.refs_5_), channel_id=1, source_target_pairs={{0,8},{1,9},{4,12},{5,13},{8,0},{9,1},{10,2},{11,3},{12,4},{13,5},... | collective-permute-start | bytes 6291464 | tf_op jit(solution)/shard_map/ppermute | solution.py:276
  189.2 57.6 %collective-permute-start.12 = (f32[2,1024,256]{2,1,0:T(8,128)}, f32[2,1024,256]{2,1,0:T(8,128)}, u32[]{:S(2)}, u32[]{:S(2)}) collective-permute-start(f32[2,1024,256]{2,1,0:T(8,128)} %collective-permute-done.6.refs_1_.refs_5_), channel_id=1, source_target_pairs={{0,1},{1,0},{4,5},{5,4},{8,9},{9,8},{12,13},{13,12},{18,19},{19,18... | collective-permute-start | bytes 6291464 | tf_op jit(solution)/shard_map/ppermute | solution.py:276
  191.2 55.5 %collective-permute-start.11 = (f32[2,1024,256]{2,1,0:T(8,128)}, f32[2,1024,256]{2,1,0:T(8,128)}, u32[]{:S(2)}, u32[]{:S(2)}) collective-permute-start(f32[2,1024,256]{2,1,0:T(8,128)} %slice_select_fusion), channel_id=1, source_target_pairs={{2,0},{3,1},{6,4},{7,5},{8,16},{9,17},{10,8},{11,9},{12,20},{13,21... | collective-permute-start | bytes 6291464 | tf_op jit(solution)/shard_map/ppermute | solution.py:276
  201.4 45.4 %collective-permute-start.13 = (f32[2,1024,256]{2,1,0:T(8,128)S(1)}, f32[2,1024,256]{2,1,0:T(8,128)S(1)}, u32[]{:S(2)}, u32[]{:S(2)}) collective-permute-start(f32[2,1024,256]{2,1,0:T(8,128)S(1)} %broadcast_select_fusion.4.refs_1_), channel_id=1, source_target_pairs={{0,1},{1,0},{2,3},{3,2},{4,5},{5,4},{6,7},{7,6},{8,9},{9,8},{10,11... | collective-permute-start | bytes 6291464 | tf_op jit(solution)/shard_map/ppermute | solution.py:276
  246.8 2.2 copy-start.8
  246.8 67.5 %collective-permute-start.16 = (f32[2,1792,256]{2,1,0:T(8,128)}, f32[2,1792,256]{2,1,0:T(8,128)}, u32[]{:S(2)}, u32[]{:S(2)}) collective-permute-start(f32[2,1792,256]{2,1,0:T(8,128)} %collective-permute-done.3.refs_3_), channel_id=1, source_target_pairs={{8,16},{12,20},{19,11},{23,15}} | collective-permute-start | bytes 11010056 | tf_op jit(solution)/shard_map/ppermute | solution.py:276
  248.1 23.5 %collective-permute-start.18 = (f32[2,1024,256]{2,1,0:T(8,128)}, f32[2,1024,256]{2,1,0:T(8,128)S(1)}, u32[]{:S(2)}, u32[]{:S(2)}) collective-permute-start(f32[2,1024,256]{2,1,0:T(8,128)} %broadcast_select_fusion.3.refs_2_), channel_id=1, source_target_pairs={{0,1},{1,0},{2,3},{3,2},{4,5},{5,4},{6,7},{7,6},{8,9},{9,8},{10,11... | collective-permute-start | bytes 6291464 | tf_op jit(solution)/shard_map/ppermute | solution.py:276
  249.0 48.1 %collective-permute-start.14 = (f32[2,1024,256]{2,1,0:T(8,128)}, f32[2,1024,256]{2,1,0:T(8,128)}, u32[]{:S(2)}, u32[]{:S(2)}) collective-permute-start(f32[2,1024,256]{2,1,0:T(8,128)} %collective-permute-done.11.refs_1_.refs_0_.refs_4_), channel_id=1, source_target_pairs={{0,8},{1,9},{4,12},{5,13},{8,0},{9,1},{10,2},{11,3},{12,4},{13,5},... | collective-permute-start | bytes 6291464 | tf_op jit(solution)/shard_map/ppermute | solution.py:276
  252.5 57.0 %collective-permute-start.15 = (f32[2,1024,256]{2,1,0:T(8,128)}, f32[2,1024,256]{2,1,0:T(8,128)S(1)}, u32[]{:S(2)}, u32[]{:S(2)}) collective-permute-start(f32[2,1024,256]{2,1,0:T(8,128)} %broadcast_select_fusion.1), channel_id=1, source_target_pairs={{0,2},{1,3},{2,0},{3,1},{4,6},{5,7},{6,4},{7,5},{8,10},{9,11},{10,... | collective-permute-start | bytes 6291464 | tf_op jit(solution)/shard_map/ppermute | solution.py:276
  263.0 51.3 %collective-permute-start.17 = (f32[2,1024,256]{2,1,0:T(8,128)}, f32[2,1024,256]{2,1,0:T(8,128)}, u32[]{:S(2)}, u32[]{:S(2)}) collective-permute-start(f32[2,1024,256]{2,1,0:T(8,128)} %collective-permute-done.11.refs_1_.refs_0_.refs_4_), channel_id=1, source_target_pairs={{0,1},{1,0},{4,5},{5,4},{8,9},{9,8},{12,13},{13,12},{18,19},{19,18... | collective-permute-start | bytes 6291464 | tf_op jit(solution)/shard_map/ppermute | solution.py:276
  271.5 1.3 copy-start.9
  309.5 10.2 %copy-start.6 = (f32[2,1024,256]{2,1,0:T(8,128)}, f32[2,1024,256]{2,1,0:T(8,128)S(1)}, u32[]{:S(2)}) copy-start(f32[2,1024,256]{2,1,0:T(8,128)S(1)} %collective-permute-done.15.refs_1_.refs_5_.refs_8_) | copy-start | bytes 6291460
  314.2 44.3 %collective-permute-start.23 = (f32[2,1792,256]{2,1,0:T(8,128)}, f32[2,1792,256]{2,1,0:T(8,128)}, u32[]{:S(2)}, u32[]{:S(2)}) collective-permute-start(f32[2,1792,256]{2,1,0:T(8,128)} %collective-permute-done.16.refs_7_.refs_8_.refs_9_), channel_id=1, source_target_pairs={{11,3},{15,7},{16,24},{20,28}} | collective-permute-start | bytes 11010056 | tf_op jit(solution)/shard_map/ppermute | solution.py:276
  319.7 8.5 %collective-permute-start.22 = (f32[2,1024,256]{2,1,0:T(8,128)}, f32[2,1024,256]{2,1,0:T(8,128)S(1)}, u32[]{:S(2)}, u32[]{:S(2)}) collective-permute-start(f32[2,1024,256]{2,1,0:T(8,128)} %get-tuple-element.152), channel_id=1, source_target_pairs={{0,1},{1,0},{2,3},{3,2},{4,5},{5,4},{6,7},{7,6},{8,9},{9,8},{10,11... | collective-permute-start | bytes 6291464 | tf_op jit(solution)/shard_map/ppermute | solution.py:276
  319.7 58.4 %collective-permute-start.19 = (f32[2,1024,256]{2,1,0:T(8,128)S(1)}, f32[2,1024,256]{2,1,0:T(8,128)}, u32[]{:S(2)}, u32[]{:S(2)}) collective-permute-start(f32[2,1024,256]{2,1,0:T(8,128)S(1)} %collective-permute-done.15.refs_1_.refs_5_.refs_8_), channel_id=1, source_target_pairs={{0,8},{1,9},{4,12},{5,13},{8,0},{9,1},{12,4},{13,5},{18,26},{19,27... | collective-permute-start | bytes 6291464 | tf_op jit(solution)/shard_map/ppermute | solution.py:276
  321.7 56.3 %collective-permute-start.20 = (f32[2,1024,256]{2,1,0:T(8,128)}, f32[2,1024,256]{2,1,0:T(8,128)}, u32[]{:S(2)}, u32[]{:S(2)}) collective-permute-start(f32[2,1024,256]{2,1,0:T(8,128)} %shard_map.20), channel_id=1, source_target_pairs={{0,2},{1,3},{4,6},{5,7},{8,10},{9,11},{12,14},{13,15},{18,16},{19,... | collective-permute-start | bytes 6291464 | tf_op jit(solution)/shard_map/ppermute | solution.py:276
  323.0 55.0 %collective-permute-start.21 = (f32[2,768,256]{2,1,0:T(8,128)}, f32[2,768,256]{2,1,0:T(8,128)}, u32[]{:S(2)}, u32[]{:S(2)}) collective-permute-start(f32[2,768,256]{2,1,0:T(8,128)} %broadcast_select_fusion.5), channel_id=1, source_target_pairs={{8,16},{9,17},{12,20},{13,21},{18,10},{19,11},{22,14},{23,15}} | collective-permute-start | bytes 4718600 | tf_op jit(solution)/shard_map/ppermute | solution.py:276
  328.2 1.3 copy-start.5
  378.1 88.3 %collective-permute-start.30 = (f32[2,512,1024]{2,1,0:T(8,128)}, f32[2,512,1024]{2,1,0:T(8,128)}, u32[]{:S(2)}, u32[]{:S(2)}) collective-permute-start(f32[2,512,1024]{2,1,0:T(8,128)} %get-tuple-element.185), channel_id=1, source_target_pairs={{0,4},{4,0},{9,13},{13,9},{18,22},{22,18},{27,31},{31,27}} | collective-permute-start | bytes 12582920 | tf_op jit(solution)/shard_map/ppermute | solution.py:276
  380.7 8.7 %collective-permute-start.24 = (f32[2,1024,256]{2,1,0:T(8,128)}, f32[2,1024,256]{2,1,0:T(8,128)}, u32[]{:S(2)}, u32[]{:S(2)}) collective-permute-start(f32[2,1024,256]{2,1,0:T(8,128)} %collective-permute-done.14.refs_2_.refs_4_), channel_id=1, source_target_pairs={{0,1},{1,0},{4,5},{5,4},{8,9},{9,8},{12,13},{13,12},{18,19},{19,18... | collective-permute-start | bytes 6291464 | tf_op jit(solution)/shard_map/ppermute | solution.py:276
  382.7 15.1 %collective-permute-start.25 = (f32[2,1024,256]{2,1,0:T(8,128)}, f32[2,1024,256]{2,1,0:T(8,128)}, u32[]{:S(2)}, u32[]{:S(2)}) collective-permute-start(f32[2,1024,256]{2,1,0:T(8,128)} %collective-permute-done.19.refs_2_.refs_5_), channel_id=1, source_target_pairs={{0,1},{1,0},{4,5},{5,4},{8,9},{9,8},{12,13},{13,12},{18,19},{19,18... | collective-permute-start | bytes 6291464 | tf_op jit(solution)/shard_map/ppermute | solution.py:276
  384.7 61.2 %collective-permute-start.27 = (f32[2,1024,256]{2,1,0:T(8,128)}, f32[2,1024,256]{2,1,0:T(8,128)}, u32[]{:S(2)}, u32[]{:S(2)}) collective-permute-start(f32[2,1024,256]{2,1,0:T(8,128)} %shard_map.22), channel_id=1, source_target_pairs={{0,2},{1,3},{4,6},{5,7},{8,10},{9,11},{12,14},{13,15},{18,16},{19,... | collective-permute-start | bytes 6291464 | tf_op jit(solution)/shard_map/ppermute | solution.py:276
  386.0 30.9 %collective-permute-start.26 = (f32[2,512,256]{2,1,0:T(8,128)}, f32[2,512,256]{2,1,0:T(8,128)S(1)}, u32[]{:S(2)}, u32[]{:S(2)}) collective-permute-start(f32[2,512,256]{2,1,0:T(8,128)} %get-tuple-element.174), channel_id=1, source_target_pairs={{2,6},{3,7},{6,2},{7,3},{10,14},{11,15},{14,10},{15,11},{16,20},{1... | collective-permute-start | bytes 3145736 | tf_op jit(solution)/shard_map/ppermute | solution.py:276
  389.4 35.8 %collective-permute-start.28 = (f32[2,768,256]{2,1,0:T(8,128)}, f32[2,768,256]{2,1,0:T(8,128)S(1)}, u32[]{:S(2)}, u32[]{:S(2)}) collective-permute-start(f32[2,768,256]{2,1,0:T(8,128)} %collective-permute-done.21.refs_10_), channel_id=1, source_target_pairs={{10,2},{11,3},{14,6},{15,7},{16,24},{17,25},{20,28},{21,29}} | collective-permute-start | bytes 4718600 | tf_op jit(solution)/shard_map/ppermute | solution.py:276
  416.9 48.4 %collective-permute-start.29 = (f32[2,512,256]{2,1,0:T(8,128)}, f32[2,512,256]{2,1,0:T(8,128)S(1)}, u32[]{:S(2)}, u32[]{:S(2)}) collective-permute-start(f32[2,512,256]{2,1,0:T(8,128)} %get-tuple-element.184), channel_id=1, source_target_pairs={{2,6},{3,7},{6,2},{7,3},{10,14},{11,15},{14,10},{15,11},{16,20},{1... | collective-permute-start | bytes 3145736 | tf_op jit(solution)/shard_map/ppermute | solution.py:276
  419.3 71.0 %collective-permute-start.33 = (f32[2,1024,256]{2,1,0:T(8,128)}, f32[2,1024,256]{2,1,0:T(8,128)}, u32[]{:S(2)}, u32[]{:S(2)}) collective-permute-start(f32[2,1024,256]{2,1,0:T(8,128)} %shard_map.25), channel_id=1, source_target_pairs={{0,2},{1,3},{4,6},{5,7},{8,10},{9,11},{12,14},{13,15},{18,16},{19,... | collective-permute-start | bytes 6291464 | tf_op jit(solution)/shard_map/ppermute | solution.py:276
  425.2 20.7 %copy-start.14 = (f32[2,768,256]{2,1,0:T(8,128)}, f32[2,768,256]{2,1,0:T(8,128)S(1)}, u32[]{:S(2)}) copy-start(f32[2,768,256]{2,1,0:T(8,128)S(1)} %collective-permute-done.28.refs_8_) | copy-start | bytes 4718596
  465.3 1.1 copy-start.2
  466.3 26.1 %collective-permute-start.34 = (f32[2,512,256]{2,1,0:T(8,128)}, f32[2,512,256]{2,1,0:T(8,128)}, u32[]{:S(2)}, u32[]{:S(2)}) collective-permute-start(f32[2,512,256]{2,1,0:T(8,128)} %get-tuple-element.196), channel_id=1, source_target_pairs={{2,6},{3,7},{6,2},{7,3},{10,14},{11,15},{14,10},{15,11},{16,20},{1... | collective-permute-start | bytes 3145736 | tf_op jit(solution)/shard_map/ppermute | solution.py:276
  468.8 28.8 %collective-permute-start.31 = (f32[1,512,1024]{2,1,0:T(8,128)}, f32[1,512,1024]{2,1,0:T(8,128)S(1)}, u32[]{:S(2)}, u32[]{:S(2)}) collective-permute-start(f32[1,512,1024]{2,1,0:T(8,128)} %get-tuple-element.187), channel_id=1, source_target_pairs={{1,5},{5,1},{8,12},{12,8},{19,23},{23,19},{26,30},{30,26}} | collective-permute-start | bytes 6291464 | tf_op jit(solution)/shard_map/ppermute | solution.py:276
  469.6 28.0 %collective-permute-start.32 = (f32[1,512,1024]{2,1,0:T(8,128)}, f32[1,512,1024]{2,1,0:T(8,128)S(1)}, u32[]{:S(2)}, u32[]{:S(2)}) collective-permute-start(f32[1,512,1024]{2,1,0:T(8,128)} %get-tuple-element.188), channel_id=1, source_target_pairs={{1,5},{5,1},{8,12},{12,8},{19,23},{23,19},{26,30},{30,26}} | collective-permute-start | bytes 6291464 | tf_op jit(solution)/shard_map/ppermute | solution.py:276
  492.4 27.5 %copy-start = (f32[2,512,256]{2,1,0:T(8,128)S(1)}, f32[2,512,256]{2,1,0:T(8,128)}, u32[]{:S(2)}) copy-start(f32[2,512,256]{2,1,0:T(8,128)} %get-tuple-element.189.refs_5_) | copy-start | bytes 3145732
  492.4 27.5 %copy-start.1 = (f32[2,512,256]{2,1,0:T(8,128)S(1)}, f32[2,512,256]{2,1,0:T(8,128)}, u32[]{:S(2)}) copy-start(f32[2,512,256]{2,1,0:T(8,128)} %get-tuple-element.190.refs_6_) | copy-start | bytes 3145732
  492.4 27.5 %copy-start.3 = (f32[2,512,256]{2,1,0:T(8,128)S(1)}, f32[2,512,256]{2,1,0:T(8,128)}, u32[]{:S(2)}) copy-start(f32[2,512,256]{2,1,0:T(8,128)} %copy-done.2) | copy-start | bytes 3145732
  492.4 27.5 %copy-start.4 = (f32[2,512,256]{2,1,0:T(8,128)S(1)}, f32[2,512,256]{2,1,0:T(8,128)}, u32[]{:S(2)}) copy-start(f32[2,512,256]{2,1,0:T(8,128)} %get-tuple-element.191.refs_7_) | copy-start | bytes 3145732
  495.0 24.9 %collective-permute-start.35 = (f32[2,512,256]{2,1,0:T(8,128)S(1)}, f32[2,512,256]{2,1,0:T(8,128)S(1)}, u32[]{:S(2)}, u32[]{:S(2)}) collective-permute-start(f32[2,512,256]{2,1,0:T(8,128)S(1)} %get-tuple-element.213), channel_id=1, source_target_pairs={{2,6},{3,7},{6,2},{7,3},{10,14},{11,15},{14,10},{15,11},{16,20},{1... | collective-permute-start | bytes 3145736 | tf_op jit(solution)/shard_map/ppermute | solution.py:276

commit v4 on v3

--- a/solution.py
+++ b/solution.py
@@ -15,7 +15,7 @@
     return jnp.dot(left, right, precision=lax.Precision.HIGH, preferred_element_type=jnp.float32)
 
 
-def multiply(left, right):
+def multiply_complex(left, right):
     rr, ii = dot(left[0], right[0]), dot(left[1], right[1])
     ss = dot(left[0] + left[1], right[0] + right[1])
     return jnp.stack([rr - ii, ss - rr - ii])
@@ -24,7 +24,7 @@
 def gathered(recorded):
     rows = lax.all_gather(recorded, "col", axis=3, tiled=True)
     columns = lax.all_gather(recorded, "row", axis=2, tiled=True)
-    out = [multiply(rows[:, f], columns[:, f]) for f in range(recorded.shape[1])]
+    out = [multiply_complex(rows[:, f], columns[:, f]) for f in range(recorded.shape[1])]
     return -jnp.stack(out, axis=1)
 
 
@@ -40,7 +40,7 @@
         out[2 * c, rows, at : at + k], out[2 * c + 1, rows, at : at + k] = split(v)
 
 
-def product_kernel(role_ref, *refs, picks, lefts, rights, more, halves, fetch, depth, keep, negate):
+def product_kernel(role_ref, *refs, picks, lefts, rights, more, halves, fetch, depth, keep, negate, by_rows):
     left, candidates, rest = refs[:lefts], refs[lefts : lefts + rights], refs[lefts + rights :]
     base, rest = (rest[0], rest[1:]) if more else (None, rest)
     outs, rest = rest[:halves], rest[halves:]
@@ -87,12 +87,12 @@
     @pl.when(functools.reduce(jnp.logical_or, [role_ref[0] == role for role in picks]))
     def _():
         if keep:
-            parts = multiply_split(kept, slice(kept.shape[2] - depth, None), scratch)
+            parts = multiply_split(kept, slice(kept.shape[2] - depth, None), scratch, by_rows)
         elif lefts == 1:
-            parts = multiply_split(left[0], slice(None), scratch)
+            parts = multiply_split(left[0], slice(None), scratch, by_rows)
         else:
             split_left(rest[1])
-            parts = multiply_split(rest[1], slice(None), scratch)
+            parts = multiply_split(rest[1], slice(None), scratch, by_rows)
         for h, out in enumerate(outs):
 
             @pl.when(i * min(halves, 2) // pl.num_programs(1) == min(h, 1))
@@ -102,19 +102,24 @@
                     out[at] = -value if negate else value
 
 
-def multiply_split(left, columns, right):
+def multiply(left, right, by_rows):
+    dims = (((1,), (1 if by_rows else 0,)), ((), ()))
+    return lax.dot_general(left, right, dims, preferred_element_type=jnp.float32)
+
+
+def multiply_split(left, columns, right, by_rows):
     parts = []
     for c in range(3):
         high, low = left[2 * c, :, columns], left[2 * c + 1, :, columns]
-        total = jnp.dot(high, right[2 * c], preferred_element_type=jnp.float32)
-        total += jnp.dot(high, right[2 * c + 1], preferred_element_type=jnp.float32)
-        total += jnp.dot(low, right[2 * c], preferred_element_type=jnp.float32)
+        total = multiply(high, right[2 * c], by_rows)
+        total += multiply(high, right[2 * c + 1], by_rows)
+        total += multiply(low, right[2 * c], by_rows)
         parts.append(total)
     rr, ii, ss = parts
     return rr - ii, ss - rr - ii
 
 
-def product(role, left, rights, picks, columns, base=None, half=None, halves=1, fetch=False, keep=False, negate=False):
+def product(role, left, rights, picks, columns, base=None, half=None, halves=1, fetch=False, keep=False, negate=False, by_rows=False):
     split_left = not isinstance(left, list)
     lefts = [left] if split_left else left
     rows = lefts[0].shape[1]
@@ -148,7 +153,7 @@
     if base is not None:
         in_specs.append(pl.BlockSpec((2, mb, nb), lambda j, i, r: (0, i * on(r), j * on(r))))
         args.append(base)
-    scratch = [pltpu.VMEM((6, depth, nb), jnp.bfloat16)]
+    scratch = [pltpu.VMEM((6, nb, depth) if by_rows else (6, depth, nb), jnp.bfloat16)]
     if not split_left and not keep:
         scratch.append(pltpu.VMEM((6, mb, depth), jnp.bfloat16))
     if fetch:
@@ -158,7 +163,7 @@
         scratch.append(pltpu.SemaphoreType.DMA((max(len(v) for v in every),)))
     body = functools.partial(
         product_kernel, picks=picks, lefts=len(lefts), rights=len(rights), more=base is not None, halves=halves, fetch=fetch,
-        depth=depth, keep=keep, negate=negate,
+        depth=depth, keep=keep, negate=negate, by_rows=by_rows,
     )
     steps = rows // mb // min(halves, 2)
     counts = (2, 1, 1) if halves == 3 else (2,) * halves
@@ -190,65 +195,61 @@
 
 
 def place_kernel(role_ref, *refs):
-    totals, gots, tops, crossed, out = refs[:2], refs[2:5], refs[5:9], refs[9:13], refs[13]
-    f, j = pl.program_id(0), pl.program_id(1)
-    kept = role_ref[1] == f
-    for role, ref in enumerate(totals):
-
-        @pl.when(kept & (role_ref[0] == role))
+    blocks, out = refs[: 4 + CHUNKS], refs[-1]
+    for role, sources in ((0, blocks[:1]), (1, blocks[1:4])):
+
+        @pl.when(role_ref[0] == role)
+        def _():
+            if sources[-1].shape[0] == 2:
+                out[:, 0] = sources[0][...]
+            else:
+                out[0, 0], out[1, 0] = sources[1][0], sources[2][0]
+
+    for step, ref in enumerate(blocks[4:]):
+
+        @pl.when((role_ref[0] >= 2) & (pl.program_id(0) == step))
         def _():
             out[:, 0] = ref[...]
 
-    @pl.when(jnp.logical_not(kept) & (role_ref[0] == 0))
-    def _():
-        out[:, 0] = gots[0][...]
-
-    @pl.when(jnp.logical_not(kept) & (role_ref[0] == 1))
-    def _():
-        out[0, 0], out[1, 0] = gots[1][0], gots[2][0]
-
-    for sources, flag in ((tops, kept), (crossed, jnp.logical_not(kept))):
-        for step, ref in enumerate(sources):
-
-            @pl.when(flag & (role_ref[0] >= 2) & (j == step))
-            def _():
-                out[:, 0] = ref[...]
-
-
-def place(role, totals, gots, tops, crossed):
-    _, rows, columns = totals[0].shape
+
+def place(role, first, second, chunks, other, onto=None):
+    _, rows, columns = first.shape
     w, steps = columns // CHUNKS, 2
     block = rows // steps
-
-    def wide(role_, first, count):
-        def at(f, j, i, r):
-            used = jnp.where((r[0] == role_) & ((r[1] == f) == first), 1, 0)
+    second = [second] * 3 if not isinstance(second, list) else [second[0]] + second
+
+    def wide(role_, count):
+        def at(j, i, r):
+            used = jnp.where(r[0] == role_, 1, 0)
             return (0, i * used, j * used)
 
         return pl.BlockSpec((count, block, w), at)
 
-    def narrow(step, first):
-        def at(f, j, i, r):
-            used = jnp.where((r[0] >= 2) & ((r[1] == f) == first) & (j == step), 1, 0)
-            return (0, i * used, 0)
-
-        return pl.BlockSpec((2, block, w), at)
-
-    uses = ((0, True, 2), (1, True, 2), (0, False, 2), (1, False, 1), (1, False, 1))
-    in_specs = [wide(*use) for use in uses]
-    in_specs += [narrow(step, first) for first in (True, False) for step in range(CHUNKS)]
+    def narrow(step):
+        return pl.BlockSpec((2, block, w), lambda j, i, r: (0, i * jnp.where((r[0] >= 2) & (j == step), 1, 0), 0))
+
+    def to(j, i, r):
+        f = 1 - r[1] if other else r[1]
+        return (0, f, i, (j + 2 * f) % CHUNKS)
+
+    in_specs = [wide(0, 2)] + [wide(1, v.shape[0]) for v in second] + [narrow(step) for step in range(CHUNKS)]
+    args = [role, first, *second, *chunks]
+    if other:
+        in_specs.append(pl.BlockSpec(memory_space=pl.ANY))
+        args.append(onto)
     return pl.pallas_call(
         place_kernel,
         grid_spec=pltpu.PrefetchScalarGridSpec(
             num_scalar_prefetch=1,
-            grid=(2, CHUNKS, steps),
+            grid=(CHUNKS, steps),
             in_specs=in_specs,
-            out_specs=pl.BlockSpec((2, 1, block, w), lambda f, j, i, r: (0, f, i, (j + 2 * f) % CHUNKS)),
+            out_specs=pl.BlockSpec((2, 1, block, w), to),
         ),
         out_shape=jax.ShapeDtypeStruct((2, 2, rows, columns), jnp.float32),
+        input_output_aliases={len(args) - 1: 0} if other else {},
         compiler_params=pltpu.CompilerParams(vmem_limit_bytes=40 * 2**20),
         cost_estimate=pl.CostEstimate(flops=1000, bytes_accessed=1000, transcendentals=0),
-    )(role, *totals, *gots, *tops, *crossed)
+    )(*args)
 
 
 def blocked(recorded):
@@ -348,6 +349,7 @@
         keep=True,
     )
     there[0], right[1], total, left = sync(there[0], right[1], total, left)
+    there[1] = send(right[1], swap_slab, outward)
     mixed = pick(diag & first, chunk(core23, 1), own[2])
     seen[0] = pick(mid_off, right[0], there[0])
     there[0], right[1], low01, low23, cores[0], left, total, mixed, seen[0], own[3] = sync(
@@ -357,7 +359,7 @@
     def share(j):
         r, t = right[j], there[j]
         return product(
-            roles, left, [r, t], {0: [[whole(0, n, 0), whole(1, n, n)]], 1: [[whole(1, n, 0), whole(0, n, n)]]}, w, fetch=True
+            roles, left, [r, t], {0: [[whole(0, n, 0), whole(1, n, n)]], 1: [[whole(1, n, 0), whole(0, n, n)]]}, w
         )
 
     def add_rights(total, js, active, halves=1):
@@ -366,11 +368,10 @@
         k = len(these)
         rights = (these if 0 in active else []) + (others if 1 in active else [])
         first_of = {0: 0, 1: len(rights) - k}
-        picks = {v: [[whole(first_of[v] + i, n, i * w, True) for i in range(k)]] for v in active}
-        return product(roles, these, rights, picks, n, base=total, halves=halves, fetch=True, negate=halves > 1)
+        picks = {v: [[(first_of[v] + i, 0, n, False, 0, i * w) for i in range(k)]] for v in active}
+        return product(roles, these, rights, picks, n, base=total, halves=halves, fetch=True, negate=halves > 1, by_rows=True)
 
     shares, shared = [None] * 4, [None] * 4
-    there[1] = send(right[1], swap_slab, outward)
     right[2] = send(mixed, to_diag, over_middle)
     cores[1] = send(right[1], swap_core_diag)
     seen_cores[0] = send(seen[0], swap_core)
@@ -380,19 +381,24 @@
         roles,
         left,
         [own01, own23, low01, low23],
-        {0: [both], 1: [sum([lower(low_sources, j, 0, j * w) for j in range(4)], [])]},
+        {
+            0: [[(0, 0, n, False, 0, 0), (1, 0, n, False, 0, n // 2)]],
+            1: [sum([lower(low_sources, j, 0, j * w) for j in range(4)], [])],
+        },
         n,
         base=total,
         half=0,
         fetch=True,
-    )
+        by_rows=True,
+    )
+    right[2], total = sync(right[2], total)
+    there[2] = send(right[2], swap_slab, outward)
     mixed = pick(diag, shares[0], own[3])
     seen[1] = pick(mid_off, right[1], there[1])
     there[1], right[2], low01, low23, cores[1], seen_cores[0], total, mixed, seen[1] = sync(
         there[1], right[2], low01, low23, cores[1], seen_cores[0], total, mixed, seen[1]
     )
 
-    there[2] = send(right[2], swap_slab, outward)
     right[3] = send(mixed, swap_y)
     near3 = send(low01, middle_second)
     cores[2] = send(right[2], swap_core_diag)
@@ -400,6 +406,8 @@
     shares[1] = share(1)
     shares[1], seen_cores[1], cores[1], total = sync(shares[1], seen_cores[1], cores[1], total)
     total = add_rights(total, (0, 1), (0, 1))
+    right[3], total = sync(right[3], total)
+    there[3] = send(right[3], swap_slab)
     seen[2] = pick(mid_off, right[2], there[2])
     mixed = pick(diag & first, lows23, low23)
     swapped = pick(diag, right[3], seen[2])
@@ -408,7 +416,6 @@
     )
     shared[0] = right[3]
 
-    there[3] = send(right[3], swap_slab)
     shared[1] = send(shares[1], to_off)
     near4 = send(mixed, over_middle)
     far3 = send(near3, outward_second)
@@ -465,7 +472,8 @@
     tops[3] = tops[3] - shared[3][:, :part]
 
     flags = jnp.stack([role, x.astype(jnp.int32)])
-    return place(flags, [keep_first, keep_second], [got_first] + got_second, tops, crossed)
+    out = place(flags, keep_first, keep_second, tops, False)
+    return place(flags, got_first, got_second, crossed, True, out)
 
 
 def solution(mesh):

time: 537 us -> 528 us (0.983)
  waiting for transfers between devices: 247 us -> 226 us
  Pallas kernels: 136 us -> 142 us
    ppermute x36, waiting for transfers between devices: 247 us -> 226 us  [send(): return lax.ppermute(value, AXES, pairs)]
    pallas_call x1 -> x2, Pallas kernels: 11.2 us -> 12 us  [place(): pl.pallas_call(place_kernel, grid_spec=pltpu.PrefetchScalarGridSpec(num_s...]
  transfers between devices with their start and end apart: 36 -> 36, of which waited for: 13 -> 12; matrix products, arithmetic and copies ran while one was open for 7% -> 7% of each run, Pallas kernels for 24% -> 26%
where the time goes in v4:
time: 528 us; the launch traced here: 522 us
  waiting for transfers between devices  226 us (43%)
  Pallas kernels  142 us (27%)
  starting transfers between devices  93.3 us (18%)
  other arithmetic  39.6 us (8%)
  local copies, waits for them, and re-layouts  20.4 us (4%)
    ppermute x36, waiting for transfers between devices, send(): return lax.ppermute(value, AXES, pairs)  226 us
    pallas_call x13, Pallas kernels, product(): pl.pallas_call(body, grid_spec=pltpu.PrefetchScalarGridSpec(num_scalar_pr...  130 us
    ppermute x36, starting transfers between devices, send(): return lax.ppermute(value, AXES, pairs)  93.3 us
    pallas_call x2, Pallas kernels, place(): pl.pallas_call(place_kernel, grid_spec=pltpu.PrefetchScalarGridSpec(num_s...  12 us
  transfers between devices with their start and end apart: 36, of which 12 were waited for; matrix products, arithmetic and copies ran while one was open for 7% of the time, Pallas kernels for 26%

profile of v4, /device:TPU:16, one launch (start us, length us, event | category | flops | bytes accessed | tf_op | source)
XLA Modules:
  0.0 522.1 jit_solution(10233615838644832482)
XLA Ops:
  0.0 6.8 %dynamic-slice_bitcast_fusion.3 = (f32[2,512,512]{2,1,0:T(8,128)}, f32[2,512,512]{2,1,0:T(8,128)S(1)}, f32[2,512,512]{2,1,0:T(8,128)}, f32[2,512,512]{2,1,0:T(8,128)S(1)}) fusion(f32[2,2,512,1024]{3,2,1,0:T(8,128)} %param.1, s32[]{:T(128)S(6)} %select_n.129, s32[]{:T(128)S(6)} %select_n.131, s32[]{:T(128)S(6)} %select_n.133, s32[]{:T(128)S(6)} %select_n.134, ...), kind=kLoop, calls=%fused_computation.22 | loop fusion | bytes 16777240 | tf_op jit(solution)/shard_map/squeeze | solution.py:304
  6.8 1.5 collective-permute-start
  8.3 45.9 %collective-permute-done = f32[2,512,512]{2,1,0:T(8,128)S(1)} collective-permute-done((f32[2,512,512]{2,1,0:T(8,128)S(1)}, f32[2,512,512]{2,1,0:T(8,128)S(1)}, u32[]{:S(2)}, u32[]{:S(2)}) %collective-permute-start) | collective-permute-done | bytes 2097184 | tf_op jit(solution)/shard_map/ppermute | solution.py:277
  54.4 2.3 fusion.3
  56.7 3.7 pad_maximum_fusion.2
  60.4 2.6 pad_maximum_fusion.refs_0_.refs_6_.refs_1_
  63.0 2.5 collective-permute-start.3
  65.5 1.5 collective-permute-start.1
  66.9 6.2 %collective-permute-start.2 = (f32[2,1024,256]{2,1,0:T(8,128)}, f32[2,1024,256]{2,1,0:T(8,128)S(1)}, u32[]{:S(2)}, u32[]{:S(2)}) collective-permute-start(f32[2,1024,256]{2,1,0:T(8,128)} %get-tuple-element.110), channel_id=1, source_target_pairs={{2,0},{3,1},{6,4},{7,5},{8,16},{9,17},{10,8},{11,9},{12,20},{13,21... | collective-permute-start | bytes 6291464 | tf_op jit(solution)/shard_map/ppermute | solution.py:277
  73.3 1.5 slice.46
  74.8 39.0 %collective-permute-done.1 = f32[2,512,512]{2,1,0:T(8,128)} collective-permute-done((f32[2,512,512]{2,1,0:T(8,128)}, f32[2,512,512]{2,1,0:T(8,128)}, u32[]{:S(2)}, u32[]{:S(2)}) %collective-permute-start.1) | collective-permute-done | bytes 2097184 | tf_op jit(solution)/shard_map/ppermute | solution.py:277
  117.7 4.2 pad_maximum_fusion.1.refs_1_.refs_7_.refs_2_
  121.8 4.4 fusion.1
  126.3 4.8 collective-permute-start.5
  131.2 1.9 collective-permute-start.6
  133.1 2.0 collective-permute-start.9
  135.1 2.0 collective-permute-start.8
  137.2 16.9 %shard_map.17 = (f32[2,1024,1024]{2,1,0:T(8,128)}, bf16[6,1024,2048]{2,1,0:T(8,128)(2,1)}) custom-call(s32[1]{0:T(128)} %bitcast.role_ref, f32[2,1024,512]{2,1,0:T(8,128)} %pad_maximum_fusion.refs_0_.refs_6_.refs_1_, f32[2,1024,512]{2,1,0:T(8,128)} %pad_maximum_fusion.1.refs_1_.refs_7_.refs_2_, f32[2,1024,512]{2,1,0:T(8,128)} %collective-permute-done.4.refs_2_.refs_4_, ...), custom_call_target="tpu_custom_call" | custom-call | flops 1000 | bytes 1000 | tf_op jit(solution)/shard_map/pallas_call | solution.py:181
  154.1 21.3 %collective-permute-done.5.refs_2_.refs_8_ = f32[2,1024,256]{2,1,0:T(8,128)} collective-permute-done((f32[2,1024,256]{2,1,0:T(8,128)S(1)}, f32[2,1024,256]{2,1,0:T(8,128)}, u32[]{:S(2)}, u32[]{:S(2)}) %collective-permute-start.5) | collective-permute-done | bytes 2097184 | tf_op jit(solution)/shard_map/ppermute | solution.py:277
  175.3 5.8 %collective-permute-done.6.refs_1_.refs_5_ = f32[2,1024,256]{2,1,0:T(8,128)} collective-permute-done((f32[2,1024,256]{2,1,0:T(8,128)}, f32[2,1024,256]{2,1,0:T(8,128)}, u32[]{:S(2)}, u32[]{:S(2)}) %collective-permute-start.6) | collective-permute-done | bytes 2097184 | tf_op jit(solution)/shard_map/ppermute | solution.py:277
  182.7 4.0 slice_select_fusion
  186.6 7.9 %collective-permute-start.11 = (f32[2,1024,256]{2,1,0:T(8,128)}, f32[2,1024,256]{2,1,0:T(8,128)}, u32[]{:S(2)}, u32[]{:S(2)}) collective-permute-start(f32[2,1024,256]{2,1,0:T(8,128)} %slice_select_fusion), channel_id=1, source_target_pairs={{2,0},{3,1},{6,4},{7,5},{8,16},{9,17},{10,8},{11,9},{12,20},{13,21... | collective-permute-start | bytes 6291464 | tf_op jit(solution)/shard_map/ppermute | solution.py:277
  194.6 7.1 %collective-permute-start.10 = (f32[2,1024,256]{2,1,0:T(8,128)}, f32[2,1024,256]{2,1,0:T(8,128)}, u32[]{:S(2)}, u32[]{:S(2)}) collective-permute-start(f32[2,1024,256]{2,1,0:T(8,128)} %collective-permute-done.6.refs_1_.refs_5_), channel_id=1, source_target_pairs={{0,8},{1,9},{4,12},{5,13},{8,0},{9,1},{10,2},{11,3},{12,4},{13,5},... | collective-permute-start | bytes 6291464 | tf_op jit(solution)/shard_map/ppermute | solution.py:277
  201.7 2.5 collective-permute-start.12
  204.2 4.9 shard_map.19
  209.1 3.9 shard_map.18.refs_12_
  213.0 3.2 broadcast_select_fusion.1
  216.2 24.5 %collective-permute-done.11.refs_1_.refs_0_.refs_4_ = f32[2,1024,256]{2,1,0:T(8,128)} collective-permute-done((f32[2,1024,256]{2,1,0:T(8,128)}, f32[2,1024,256]{2,1,0:T(8,128)}, u32[]{:S(2)}, u32[]{:S(2)}) %collective-permute-start.11) | collective-permute-done | bytes 2097184 | tf_op jit(solution)/shard_map/ppermute | solution.py:277
  240.7 2.8 collective-permute-done.10.refs_2_.refs_9_
  243.4 3.2 broadcast_select_fusion.3.refs_2_
  248.0 10.7 %collective-permute-start.16 = (f32[2,1024,256]{2,1,0:T(8,128)}, f32[2,1024,256]{2,1,0:T(8,128)S(1)}, u32[]{:S(2)}, u32[]{:S(2)}) collective-permute-start(f32[2,1024,256]{2,1,0:T(8,128)} %broadcast_select_fusion.1), channel_id=1, source_target_pairs={{0,2},{1,3},{2,0},{3,1},{4,6},{5,7},{6,4},{7,5},{8,10},{9,11},{10,... | collective-permute-start | bytes 6291464 | tf_op jit(solution)/shard_map/ppermute | solution.py:277
  258.7 2.9 collective-permute-start.14
  261.7 2.0 collective-permute-start.19
  263.7 5.0 shard_map.20
  268.7 2.8 broadcast_select_fusion.5
  272.9 3.6 shard_map.21.refs_8_
  276.5 28.3 %collective-permute-done.16.refs_1_.refs_5_.refs_8_ = f32[2,1024,256]{2,1,0:T(8,128)S(1)} collective-permute-done((f32[2,1024,256]{2,1,0:T(8,128)}, f32[2,1024,256]{2,1,0:T(8,128)S(1)}, u32[]{:S(2)}, u32[]{:S(2)}) %collective-permute-start.16) | collective-permute-done | bytes 2097184 | tf_op jit(solution)/shard_map/ppermute | solution.py:277
  305.7 4.0 broadcast_select_fusion
  309.7 6.2 %collective-permute-start.23 = (f32[2,1792,256]{2,1,0:T(8,128)}, f32[2,1792,256]{2,1,0:T(8,128)}, u32[]{:S(2)}, u32[]{:S(2)}) collective-permute-start(f32[2,1792,256]{2,1,0:T(8,128)} %collective-permute-done.18.refs_7_.refs_8_.refs_9_), channel_id=1, source_target_pairs={{11,3},{15,7},{16,24},{20,28}} | collective-permute-start | bytes 11010056 | tf_op jit(solution)/shard_map/ppermute | solution.py:277
  315.8 2.0 collective-permute-start.17
  320.5 5.1 shard_map.22
  326.9 4.3 shard_map.23
  331.2 23.5 %collective-permute-done.23.refs_6_.refs_7_ = f32[2,1792,256]{2,1,0:T(8,128)} collective-permute-done((f32[2,1792,256]{2,1,0:T(8,128)}, f32[2,1792,256]{2,1,0:T(8,128)}, u32[]{:S(2)}, u32[]{:S(2)}) %collective-permute-start.23) | collective-permute-done | bytes 3670048 | tf_op jit(solution)/shard_map/ppermute | solution.py:277
  354.8 19.5 %shard_map.24 = (f32[2,512,256]{2,1,0:T(8,128)}, f32[2,512,256]{2,1,0:T(8,128)}) custom-call(s32[1]{0:T(128)} %bitcast.role_ref, bf16[6,1024,2048]{2,1,0:T(8,128)(2,1)} %get-tuple-element.127.refs_0_, f32[2,1024,256]{2,1,0:T(8,128)} %copy-done.9, f32[2,1024,256]{2,1,0:T(8,128)} %get-tuple-element.212.refs_2_.refs_3_, f32[2,1024,256]{2,1,0:T(8,128)} %copy-done.10, ...), custom_call_target="tpu_custom_call" | custom-call | flops 1000 | bytes 1000 | tf_op jit(solution)/shard_map/pallas_call | solution.py:181
  375.2 2.0 collective-permute-start.24
  377.2 2.0 collective-permute-start.25
  380.5 3.4 collective-permute-start.26
  384.0 5.6 %collective-permute-start.28 = (f32[2,768,256]{2,1,0:T(8,128)}, f32[2,768,256]{2,1,0:T(8,128)}, u32[]{:S(2)}, u32[]{:S(2)}) collective-permute-start(f32[2,768,256]{2,1,0:T(8,128)} %copy-done.16), channel_id=1, source_target_pairs={{10,2},{11,3},{14,6},{15,7},{16,24},{17,25},{20,28},{21,29}} | collective-permute-start | bytes 4718600 | tf_op jit(solution)/shard_map/ppermute | solution.py:277
  389.5 5.0 shard_map.25
  394.5 19.0 %shard_map.26 = (f32[2,512,256]{2,1,0:T(8,128)}, f32[2,512,256]{2,1,0:T(8,128)}) custom-call(s32[1]{0:T(128)} %bitcast.role_ref, bf16[6,1024,2048]{2,1,0:T(8,128)(2,1)} %get-tuple-element.127.refs_0_, f32[2,1024,256]{2,1,0:T(8,128)} %copy-done.9, f32[2,1024,256]{2,1,0:T(8,128)} %broadcast_select_fusion.3.refs_2_, ...), custom_call_target="tpu_custom_call" | custom-call | flops 1000 | bytes 1000 | tf_op jit(solution)/shard_map/pallas_call | solution.py:181
  413.6 2.4 collective-permute-start.29
  417.4 4.6 shard_map.27
  422.0 16.3 %collective-permute-done.27.refs_11_ = f32[2,1024,256]{2,1,0:T(8,128)} collective-permute-done((f32[2,1024,256]{2,1,0:T(8,128)}, f32[2,1024,256]{2,1,0:T(8,128)}, u32[]{:S(2)}, u32[]{:S(2)}) %collective-permute-start.27) | collective-permute-done | bytes 2097184 | tf_op jit(solution)/shard_map/ppermute | solution.py:277
  438.3 19.3 %shard_map.28 = (f32[2,512,256]{2,1,0:T(8,128)}, f32[2,512,256]{2,1,0:T(8,128)}) custom-call(s32[1]{0:T(128)} %bitcast.role_ref, bf16[6,1024,2048]{2,1,0:T(8,128)(2,1)} %get-tuple-element.127.refs_0_, f32[2,1024,256]{2,1,0:T(8,128)} %copy-done.9, f32[2,1024,256]{2,1,0:T(8,128)} %broadcast_select_fusion.3.refs_2_, ...), custom_call_target="tpu_custom_call" | custom-call | flops 1000 | bytes 1000 | tf_op jit(solution)/shard_map/pallas_call | solution.py:181
  457.6 2.1 copy-done.1
  459.7 2.4 collective-permute-start.34
  463.7 19.0 %shard_map.29 = (f32[2,512,256]{2,1,0:T(8,128)}, f32[2,512,256]{2,1,0:T(8,128)}) custom-call(s32[1]{0:T(128)} %bitcast.role_ref, bf16[6,1024,2048]{2,1,0:T(8,128)(2,1)} %get-tuple-element.127.refs_0_, f32[2,1024,256]{2,1,0:T(8,128)} %copy-done.9, f32[2,1024,256]{2,1,0:T(8,128)} %broadcast_select_fusion.3.refs_2_, ...), custom_call_target="tpu_custom_call" | custom-call | flops 1000 | bytes 1000 | tf_op jit(solution)/shard_map/pallas_call | solution.py:181
  482.7 3.0 collective-permute-done.34.refs_6_
  485.8 3.6 slice_subtract_fusion
  489.3 2.4 collective-permute-start.35
  491.9 2.2 copy-done.3
  495.3 4.8 shard_map.30.refs_8_
  500.1 14.3 %collective-permute-done.35.refs_7_ = f32[2,512,256]{2,1,0:T(8,128)S(1)} collective-permute-done((f32[2,512,256]{2,1,0:T(8,128)}, f32[2,512,256]{2,1,0:T(8,128)S(1)}, u32[]{:S(2)}, u32[]{:S(2)}) %collective-permute-start.35) | collective-permute-done | bytes 1048608 | tf_op jit(solution)/shard_map/ppermute | solution.py:277
  514.4 7.2 %shard_map.31 = f32[2,2,512,1024]{3,2,1,0:T(8,128)} custom-call(s32[2]{0:T(128)S(1)} %pad_add_fusion.role_ref, f32[2,512,1024]{2,1,0:T(8,128)S(1)} %copy-done.2, f32[1,512,1024]{2,1,0:T(8,128)S(1)} %collective-permute-done.31.refs_1_.refs_2_, f32[1,512,1024]{2,1,0:T(8,128)S(1)} %collective-permute-done.31.refs_1_.refs_2_, ...), custom_call_target="tpu_custom_call", output_to_operand_aliasing={{}: (9, {})} | custom-call | flops 1000 | bytes 1000 | tf_op jit(solution)/shard_map/pallas_call | solution.py:240
  (76 shorter events, 19.9 us)
Async XLA Ops:
  6.8 47.4 %collective-permute-start = (f32[2,512,512]{2,1,0:T(8,128)S(1)}, f32[2,512,512]{2,1,0:T(8,128)S(1)}, u32[]{:S(2)}, u32[]{:S(2)}) collective-permute-start(f32[2,512,512]{2,1,0:T(8,128)S(1)} %get-tuple-element.216), channel_id=1, source_target_pairs={{0,4},{1,5},{2,6},{3,7},{4,0},{5,1},{6,2},{7,3},{8,12},{9,13},{10,... | collective-permute-start | bytes 6291464 | tf_op jit(solution)/shard_map/ppermute | solution.py:277
  63.0 63.2 %collective-permute-start.4 = (f32[2,1024,512]{2,1,0:T(8,128)}, f32[2,1024,512]{2,1,0:T(8,128)}, u32[]{:S(2)}, u32[]{:S(2)}) collective-permute-start(f32[2,1024,512]{2,1,0:T(8,128)} %pad_maximum_fusion.refs_0_.refs_6_.refs_1_), channel_id=1, source_target_pairs={{0,1},{1,0},{2,3},{3,2},{4,5},{5,4},{6,7},{7,6},{8,9},{9,8},{10,11... | collective-permute-start | bytes 12582920 | tf_op jit(solution)/shard_map/ppermute | solution.py:277
  63.0 63.2 %collective-permute-start.3 = (f32[2,1792,256]{2,1,0:T(8,128)}, f32[2,1792,256]{2,1,0:T(8,128)}, u32[]{:S(2)}, u32[]{:S(2)}) collective-permute-start(f32[2,1792,256]{2,1,0:T(8,128)} %pad_maximum_fusion.2), channel_id=1, source_target_pairs={{0,8},{4,12},{9,1},{13,5},{18,26},{22,30},{27,19},{31,23}} | collective-permute-start | bytes 11010056 | tf_op jit(solution)/shard_map/ppermute | solution.py:277
  65.5 48.4 %collective-permute-start.1 = (f32[2,512,512]{2,1,0:T(8,128)}, f32[2,512,512]{2,1,0:T(8,128)}, u32[]{:S(2)}, u32[]{:S(2)}) collective-permute-start(f32[2,512,512]{2,1,0:T(8,128)} %get-tuple-element.108), channel_id=1, source_target_pairs={{0,4},{1,5},{2,6},{3,7},{4,0},{5,1},{6,2},{7,3},{8,12},{9,13},{10,... | collective-permute-start | bytes 6291464 | tf_op jit(solution)/shard_map/ppermute | solution.py:277
  66.9 59.3 %collective-permute-start.2 = (f32[2,1024,256]{2,1,0:T(8,128)}, f32[2,1024,256]{2,1,0:T(8,128)S(1)}, u32[]{:S(2)}, u32[]{:S(2)}) collective-permute-start(f32[2,1024,256]{2,1,0:T(8,128)} %get-tuple-element.110), channel_id=1, source_target_pairs={{2,0},{3,1},{6,4},{7,5},{8,16},{9,17},{10,8},{11,9},{12,20},{13,21... | collective-permute-start | bytes 6291464 | tf_op jit(solution)/shard_map/ppermute | solution.py:277
  115.1 2.5 copy-start.13
  117.7 4.2 copy-start.14
  126.2 54.9 %copy-start.12 = (f32[2,1024,256]{2,1,0:T(8,128)}, f32[2,1024,256]{2,1,0:T(8,128)S(1)}, u32[]{:S(2)}) copy-start(f32[2,1024,256]{2,1,0:T(8,128)S(1)} %collective-permute-done.2.refs_1_.refs_0_.refs_4_) | copy-start | bytes 6291460
  126.2 10.9 %collective-permute-start.7 = (f32[2,1024,512]{2,1,0:T(8,128)}, f32[2,1024,512]{2,1,0:T(8,128)}, u32[]{:S(2)}, u32[]{:S(2)}) collective-permute-start(f32[2,1024,512]{2,1,0:T(8,128)} %pad_maximum_fusion.1.refs_1_.refs_7_.refs_2_), channel_id=1, source_target_pairs={{0,1},{1,0},{2,3},{3,2},{4,5},{5,4},{6,7},{7,6},{8,9},{9,8},{10,11... | collective-permute-start | bytes 12582920 | tf_op jit(solution)/shard_map/ppermute | solution.py:277
  126.3 49.0 %collective-permute-start.5 = (f32[2,1024,256]{2,1,0:T(8,128)S(1)}, f32[2,1024,256]{2,1,0:T(8,128)}, u32[]{:S(2)}, u32[]{:S(2)}) collective-permute-start(f32[2,1024,256]{2,1,0:T(8,128)S(1)} %collective-permute-done.2.refs_1_.refs_0_.refs_4_), channel_id=1, source_target_pairs={{0,8},{1,9},{4,12},{5,13},{8,0},{9,1},{10,2},{11,3},{12,4},{13,5},... | collective-permute-start | bytes 6291464 | tf_op jit(solution)/shard_map/ppermute | solution.py:277
  131.2 49.9 %collective-permute-start.6 = (f32[2,1024,256]{2,1,0:T(8,128)}, f32[2,1024,256]{2,1,0:T(8,128)}, u32[]{:S(2)}, u32[]{:S(2)}) collective-permute-start(f32[2,1024,256]{2,1,0:T(8,128)} %get-tuple-element.114), channel_id=1, source_target_pairs={{2,0},{3,1},{6,4},{7,5},{8,16},{9,17},{10,8},{11,9},{12,20},{13,21... | collective-permute-start | bytes 6291464 | tf_op jit(solution)/shard_map/ppermute | solution.py:277
  133.1 53.6 %collective-permute-start.9 = (f32[2,1024,256]{2,1,0:T(8,128)S(1)}, f32[2,1024,256]{2,1,0:T(8,128)}, u32[]{:S(2)}, u32[]{:S(2)}) collective-permute-start(f32[2,1024,256]{2,1,0:T(8,128)S(1)} %collective-permute-done.2.refs_1_.refs_0_.refs_4_), channel_id=1, source_target_pairs={{0,1},{1,0},{4,5},{5,4},{8,9},{9,8},{12,13},{13,12},{18,19},{19,18... | collective-permute-start | bytes 6291464 | tf_op jit(solution)/shard_map/ppermute | solution.py:277
  135.1 51.5 %collective-permute-start.8 = (f32[2,768,256]{2,1,0:T(8,128)}, f32[2,768,256]{2,1,0:T(8,128)}, u32[]{:S(2)}, u32[]{:S(2)}) collective-permute-start(f32[2,768,256]{2,1,0:T(8,128)} %pad_maximum_fusion.3), channel_id=1, source_target_pairs={{0,8},{4,12},{9,1},{13,5},{18,26},{22,30},{27,19},{31,23}} | collective-permute-start | bytes 4718600 | tf_op jit(solution)/shard_map/ppermute | solution.py:277
  181.1 1.6 copy-start.15
  182.7 21.4 %copy-start.9 = (f32[2,1024,256]{2,1,0:T(8,128)}, f32[2,1024,256]{2,1,0:T(8,128)S(1)}, u32[]{:S(2)}) copy-start(f32[2,1024,256]{2,1,0:T(8,128)S(1)} %broadcast_select_fusion.4.refs_1_) | copy-start | bytes 6291460
  186.6 54.0 %collective-permute-start.11 = (f32[2,1024,256]{2,1,0:T(8,128)}, f32[2,1024,256]{2,1,0:T(8,128)}, u32[]{:S(2)}, u32[]{:S(2)}) collective-permute-start(f32[2,1024,256]{2,1,0:T(8,128)} %slice_select_fusion), channel_id=1, source_target_pairs={{2,0},{3,1},{6,4},{7,5},{8,16},{9,17},{10,8},{11,9},{12,20},{13,21... | collective-permute-start | bytes 6291464 | tf_op jit(solution)/shard_map/ppermute | solution.py:277
  194.6 48.9 %collective-permute-start.10 = (f32[2,1024,256]{2,1,0:T(8,128)}, f32[2,1024,256]{2,1,0:T(8,128)}, u32[]{:S(2)}, u32[]{:S(2)}) collective-permute-start(f32[2,1024,256]{2,1,0:T(8,128)} %collective-permute-done.6.refs_1_.refs_5_), channel_id=1, source_target_pairs={{0,8},{1,9},{4,12},{5,13},{8,0},{9,1},{10,2},{11,3},{12,4},{13,5},... | collective-permute-start | bytes 6291464 | tf_op jit(solution)/shard_map/ppermute | solution.py:277
  201.7 45.0 %collective-permute-start.12 = (f32[2,1024,256]{2,1,0:T(8,128)}, f32[2,1024,256]{2,1,0:T(8,128)}, u32[]{:S(2)}, u32[]{:S(2)}) collective-permute-start(f32[2,1024,256]{2,1,0:T(8,128)} %collective-permute-done.6.refs_1_.refs_5_), channel_id=1, source_target_pairs={{0,1},{1,0},{4,5},{5,4},{8,9},{9,8},{12,13},{13,12},{18,19},{19,18... | collective-permute-start | bytes 6291464 | tf_op jit(solution)/shard_map/ppermute | solution.py:277
  204.1 42.5 %collective-permute-start.13 = (f32[2,1024,256]{2,1,0:T(8,128)S(1)}, f32[2,1024,256]{2,1,0:T(8,128)S(1)}, u32[]{:S(2)}, u32[]{:S(2)}) collective-permute-start(f32[2,1024,256]{2,1,0:T(8,128)S(1)} %broadcast_select_fusion.4.refs_1_), channel_id=1, source_target_pairs={{0,1},{1,0},{2,3},{3,2},{4,5},{5,4},{6,7},{7,6},{8,9},{9,8},{10,11... | collective-permute-start | bytes 6291464 | tf_op jit(solution)/shard_map/ppermute | solution.py:277
  246.6 1.3 copy-start.10
  246.6 63.1 %collective-permute-start.18 = (f32[2,1792,256]{2,1,0:T(8,128)}, f32[2,1792,256]{2,1,0:T(8,128)}, u32[]{:S(2)}, u32[]{:S(2)}) collective-permute-start(f32[2,1792,256]{2,1,0:T(8,128)} %collective-permute-done.3.refs_3_), channel_id=1, source_target_pairs={{8,16},{12,20},{19,11},{23,15}} | collective-permute-start | bytes 11010056 | tf_op jit(solution)/shard_map/ppermute | solution.py:277
  248.0 23.6 %collective-permute-start.15 = (f32[2,1024,256]{2,1,0:T(8,128)}, f32[2,1024,256]{2,1,0:T(8,128)S(1)}, u32[]{:S(2)}, u32[]{:S(2)}) collective-permute-start(f32[2,1024,256]{2,1,0:T(8,128)} %broadcast_select_fusion.3.refs_2_), channel_id=1, source_target_pairs={{0,1},{1,0},{2,3},{3,2},{4,5},{5,4},{6,7},{7,6},{8,9},{9,8},{10,11... | collective-permute-start | bytes 6291464 | tf_op jit(solution)/shard_map/ppermute | solution.py:277
  248.0 56.7 %collective-permute-start.16 = (f32[2,1024,256]{2,1,0:T(8,128)}, f32[2,1024,256]{2,1,0:T(8,128)S(1)}, u32[]{:S(2)}, u32[]{:S(2)}) collective-permute-start(f32[2,1024,256]{2,1,0:T(8,128)} %broadcast_select_fusion.1), channel_id=1, source_target_pairs={{0,2},{1,3},{2,0},{3,1},{4,6},{5,7},{6,4},{7,5},{8,10},{9,11},{10,... | collective-permute-start | bytes 6291464 | tf_op jit(solution)/shard_map/ppermute | solution.py:277
  258.7 47.0 %collective-permute-start.14 = (f32[2,1024,256]{2,1,0:T(8,128)}, f32[2,1024,256]{2,1,0:T(8,128)}, u32[]{:S(2)}, u32[]{:S(2)}) collective-permute-start(f32[2,1024,256]{2,1,0:T(8,128)} %collective-permute-done.11.refs_1_.refs_0_.refs_4_), channel_id=1, source_target_pairs={{0,8},{1,9},{4,12},{5,13},{8,0},{9,1},{10,2},{11,3},{12,4},{13,5},... | collective-permute-start | bytes 6291464 | tf_op jit(solution)/shard_map/ppermute | solution.py:277
  261.7 48.0 %collective-permute-start.19 = (f32[2,1024,256]{2,1,0:T(8,128)}, f32[2,1024,256]{2,1,0:T(8,128)}, u32[]{:S(2)}, u32[]{:S(2)}) collective-permute-start(f32[2,1024,256]{2,1,0:T(8,128)} %collective-permute-done.11.refs_1_.refs_0_.refs_4_), channel_id=1, source_target_pairs={{0,1},{1,0},{4,5},{5,4},{8,9},{9,8},{12,13},{13,12},{18,19},{19,18... | collective-permute-start | bytes 6291464 | tf_op jit(solution)/shard_map/ppermute | solution.py:277
  271.5 1.4 copy-start.11
  304.7 11.1 %copy-start.8 = (f32[2,1024,256]{2,1,0:T(8,128)}, f32[2,1024,256]{2,1,0:T(8,128)S(1)}, u32[]{:S(2)}) copy-start(f32[2,1024,256]{2,1,0:T(8,128)S(1)} %collective-permute-done.16.refs_1_.refs_5_.refs_8_) | copy-start | bytes 6291460
  309.7 45.1 %collective-permute-start.23 = (f32[2,1792,256]{2,1,0:T(8,128)}, f32[2,1792,256]{2,1,0:T(8,128)}, u32[]{:S(2)}, u32[]{:S(2)}) collective-permute-start(f32[2,1792,256]{2,1,0:T(8,128)} %collective-permute-done.18.refs_7_.refs_8_.refs_9_), channel_id=1, source_target_pairs={{11,3},{15,7},{16,24},{20,28}} | collective-permute-start | bytes 11010056 | tf_op jit(solution)/shard_map/ppermute | solution.py:277
  315.8 9.7 %collective-permute-start.22 = (f32[2,1024,256]{2,1,0:T(8,128)}, f32[2,1024,256]{2,1,0:T(8,128)S(1)}, u32[]{:S(2)}, u32[]{:S(2)}) collective-permute-start(f32[2,1024,256]{2,1,0:T(8,128)} %get-tuple-element.160), channel_id=1, source_target_pairs={{0,1},{1,0},{2,3},{3,2},{4,5},{5,4},{6,7},{7,6},{8,9},{9,8},{10,11... | collective-permute-start | bytes 6291464 | tf_op jit(solution)/shard_map/ppermute | solution.py:277
  315.8 58.4 %collective-permute-start.17 = (f32[2,1024,256]{2,1,0:T(8,128)S(1)}, f32[2,1024,256]{2,1,0:T(8,128)}, u32[]{:S(2)}, u32[]{:S(2)}) collective-permute-start(f32[2,1024,256]{2,1,0:T(8,128)S(1)} %collective-permute-done.16.refs_1_.refs_5_.refs_8_), channel_id=1, source_target_pairs={{0,8},{1,9},{4,12},{5,13},{8,0},{9,1},{12,4},{13,5},{18,26},{19,27... | collective-permute-start | bytes 6291464 | tf_op jit(solution)/shard_map/ppermute | solution.py:277
  317.9 56.4 %collective-permute-start.20 = (f32[2,1024,256]{2,1,0:T(8,128)}, f32[2,1024,256]{2,1,0:T(8,128)}, u32[]{:S(2)}, u32[]{:S(2)}) collective-permute-start(f32[2,1024,256]{2,1,0:T(8,128)} %shard_map.20), channel_id=1, source_target_pairs={{0,2},{1,3},{4,6},{5,7},{8,10},{9,11},{12,14},{13,15},{18,16},{19,... | collective-permute-start | bytes 6291464 | tf_op jit(solution)/shard_map/ppermute | solution.py:277
  319.2 55.1 %collective-permute-start.21 = (f32[2,768,256]{2,1,0:T(8,128)}, f32[2,768,256]{2,1,0:T(8,128)S(1)}, u32[]{:S(2)}, u32[]{:S(2)}) collective-permute-start(f32[2,768,256]{2,1,0:T(8,128)} %broadcast_select_fusion.5), channel_id=1, source_target_pairs={{8,16},{9,17},{12,20},{13,21},{18,10},{19,11},{22,14},{23,15}} | collective-permute-start | bytes 4718600 | tf_op jit(solution)/shard_map/ppermute | solution.py:277
  325.5 1.4 copy-start.7
  374.3 5.0 copy-start.16
  374.3 83.3 %collective-permute-start.30 = (f32[2,512,1024]{2,1,0:T(8,128)}, f32[2,512,1024]{2,1,0:T(8,128)S(1)}, u32[]{:S(2)}, u32[]{:S(2)}) collective-permute-start(f32[2,512,1024]{2,1,0:T(8,128)} %get-tuple-element.191), channel_id=1, source_target_pairs={{0,4},{4,0},{9,13},{13,9},{18,22},{22,18},{27,31},{31,27}} | collective-permute-start | bytes 12582920 | tf_op jit(solution)/shard_map/ppermute | solution.py:277
  375.2 8.7 %collective-permute-start.24 = (f32[2,1024,256]{2,1,0:T(8,128)}, f32[2,1024,256]{2,1,0:T(8,128)}, u32[]{:S(2)}, u32[]{:S(2)}) collective-permute-start(f32[2,1024,256]{2,1,0:T(8,128)} %collective-permute-done.14.refs_2_.refs_4_), channel_id=1, source_target_pairs={{0,1},{1,0},{4,5},{5,4},{8,9},{9,8},{12,13},{13,12},{18,19},{19,18... | collective-permute-start | bytes 6291464 | tf_op jit(solution)/shard_map/ppermute | solution.py:277
  377.2 17.3 %collective-permute-start.25 = (f32[2,1024,256]{2,1,0:T(8,128)}, f32[2,1024,256]{2,1,0:T(8,128)}, u32[]{:S(2)}, u32[]{:S(2)}) collective-permute-start(f32[2,1024,256]{2,1,0:T(8,128)} %collective-permute-done.17.refs_2_.refs_5_), channel_id=1, source_target_pairs={{0,1},{1,0},{4,5},{5,4},{8,9},{9,8},{12,13},{13,12},{18,19},{19,18... | collective-permute-start | bytes 6291464 | tf_op jit(solution)/shard_map/ppermute | solution.py:277
  379.2 59.0 %collective-permute-start.27 = (f32[2,1024,256]{2,1,0:T(8,128)}, f32[2,1024,256]{2,1,0:T(8,128)}, u32[]{:S(2)}, u32[]{:S(2)}) collective-permute-start(f32[2,1024,256]{2,1,0:T(8,128)} %shard_map.22), channel_id=1, source_target_pairs={{0,2},{1,3},{4,6},{5,7},{8,10},{9,11},{12,14},{13,15},{18,16},{19,... | collective-permute-start | bytes 6291464 | tf_op jit(solution)/shard_map/ppermute | solution.py:277
  380.5 33.1 %collective-permute-start.26 = (f32[2,512,256]{2,1,0:T(8,128)}, f32[2,512,256]{2,1,0:T(8,128)S(1)}, u32[]{:S(2)}, u32[]{:S(2)}) collective-permute-start(f32[2,512,256]{2,1,0:T(8,128)} %get-tuple-element.181), channel_id=1, source_target_pairs={{2,6},{3,7},{6,2},{7,3},{10,14},{11,15},{14,10},{15,11},{16,20},{1... | collective-permute-start | bytes 3145736 | tf_op jit(solution)/shard_map/ppermute | solution.py:277
  384.0 38.0 %collective-permute-start.28 = (f32[2,768,256]{2,1,0:T(8,128)}, f32[2,768,256]{2,1,0:T(8,128)}, u32[]{:S(2)}, u32[]{:S(2)}) collective-permute-start(f32[2,768,256]{2,1,0:T(8,128)} %copy-done.16), channel_id=1, source_target_pairs={{10,2},{11,3},{14,6},{15,7},{16,24},{17,25},{20,28},{21,29}} | collective-permute-start | bytes 4718600 | tf_op jit(solution)/shard_map/ppermute | solution.py:277
  413.6 44.0 %collective-permute-start.29 = (f32[2,512,256]{2,1,0:T(8,128)}, f32[2,512,256]{2,1,0:T(8,128)}, u32[]{:S(2)}, u32[]{:S(2)}) collective-permute-start(f32[2,512,256]{2,1,0:T(8,128)} %get-tuple-element.190), channel_id=1, source_target_pairs={{2,6},{3,7},{6,2},{7,3},{10,14},{11,15},{14,10},{15,11},{16,20},{1... | collective-permute-start | bytes 3145736 | tf_op jit(solution)/shard_map/ppermute | solution.py:277
  416.1 66.7 %collective-permute-start.33 = (f32[2,1024,256]{2,1,0:T(8,128)}, f32[2,1024,256]{2,1,0:T(8,128)}, u32[]{:S(2)}, u32[]{:S(2)}) collective-permute-start(f32[2,1024,256]{2,1,0:T(8,128)} %shard_map.25), channel_id=1, source_target_pairs={{0,2},{1,3},{4,6},{5,7},{8,10},{9,11},{12,14},{13,15},{18,16},{19,... | collective-permute-start | bytes 6291464 | tf_op jit(solution)/shard_map/ppermute | solution.py:277
  457.6 2.1 copy-start.1
  459.7 26.1 %collective-permute-start.34 = (f32[2,512,256]{2,1,0:T(8,128)}, f32[2,512,256]{2,1,0:T(8,128)}, u32[]{:S(2)}, u32[]{:S(2)}) collective-permute-start(f32[2,512,256]{2,1,0:T(8,128)} %get-tuple-element.201), channel_id=1, source_target_pairs={{2,6},{3,7},{6,2},{7,3},{10,14},{11,15},{14,10},{15,11},{16,20},{1... | collective-permute-start | bytes 3145736 | tf_op jit(solution)/shard_map/ppermute | solution.py:277
  462.1 38.0 %collective-permute-start.31 = (f32[1,512,1024]{2,1,0:T(8,128)}, f32[1,512,1024]{2,1,0:T(8,128)S(1)}, u32[]{:S(2)}, u32[]{:S(2)}) collective-permute-start(f32[1,512,1024]{2,1,0:T(8,128)} %get-tuple-element.193), channel_id=1, source_target_pairs={{1,5},{5,1},{8,12},{12,8},{19,23},{23,19},{26,30},{30,26}} | collective-permute-start | bytes 6291464 | tf_op jit(solution)/shard_map/ppermute | solution.py:277
  462.9 37.2 %collective-permute-start.32 = (f32[1,512,1024]{2,1,0:T(8,128)}, f32[1,512,1024]{2,1,0:T(8,128)S(1)}, u32[]{:S(2)}, u32[]{:S(2)}) collective-permute-start(f32[1,512,1024]{2,1,0:T(8,128)} %get-tuple-element.194), channel_id=1, source_target_pairs={{1,5},{5,1},{8,12},{12,8},{19,23},{23,19},{26,30},{30,26}} | collective-permute-start | bytes 6291464 | tf_op jit(solution)/shard_map/ppermute | solution.py:277
  485.8 6.1 %copy-start = (f32[2,512,1024]{2,1,0:T(8,128)S(1)}, f32[2,512,1024]{2,1,0:T(8,128)}, u32[]{:S(2)}) copy-start(f32[2,512,1024]{2,1,0:T(8,128)} %get-tuple-element.206.refs_1_.refs_2_.refs_3_) | copy-start | bytes 12582916
  485.8 6.1 %copy-start.4 = (f32[2,512,256]{2,1,0:T(8,128)S(1)}, f32[2,512,256]{2,1,0:T(8,128)}, u32[]{:S(2)}) copy-start(f32[2,512,256]{2,1,0:T(8,128)} %get-tuple-element.207.refs_4_) | copy-start | bytes 3145732
  485.8 6.1 %copy-start.5 = (f32[2,512,256]{2,1,0:T(8,128)S(1)}, f32[2,512,256]{2,1,0:T(8,128)}, u32[]{:S(2)}) copy-start(f32[2,512,256]{2,1,0:T(8,128)} %get-tuple-element.208.refs_5_) | copy-start | bytes 3145732
  489.3 25.0 %collective-permute-start.35 = (f32[2,512,256]{2,1,0:T(8,128)}, f32[2,512,256]{2,1,0:T(8,128)S(1)}, u32[]{:S(2)}, u32[]{:S(2)}) collective-permute-start(f32[2,512,256]{2,1,0:T(8,128)} %get-tuple-element.222), channel_id=1, source_target_pairs={{2,6},{3,7},{6,2},{7,3},{10,14},{11,15},{14,10},{15,11},{16,20},{1... | collective-permute-start | bytes 3145736 | tf_op jit(solution)/shard_map/ppermute | solution.py:277
  491.9 2.2 copy-start.3
  494.1 1.2 copy-start.6
  495.3 19.1 %copy-start.2 = (f32[2,512,1024]{2,1,0:T(8,128)S(1)}, f32[2,512,1024]{2,1,0:T(8,128)}, u32[]{:S(2)}) copy-start(f32[2,512,1024]{2,1,0:T(8,128)} %copy-done.1) | copy-start | bytes 12582916

commit v5 on v4

--- a/solution.py
+++ b/solution.py
@@ -408,9 +408,8 @@
     total = add_rights(total, (0, 1), (0, 1))
     right[3], total = sync(right[3], total)
     there[3] = send(right[3], swap_slab)
-    seen[2] = pick(mid_off, right[2], there[2])
     mixed = pick(diag & first, lows23, low23)
-    swapped = pick(diag, right[3], seen[2])
+    swapped = pick(diag, right[3], pick(mid_off, right[2], there[2]))
     there[2], right[3], near3, cores[2], shares[1], total, swapped, mixed = sync(
         there[2], right[3], near3, cores[2], shares[1], total, swapped, mixed
     )
@@ -429,14 +428,14 @@
     far4 = near4
 
     def rest(j, base):
-        rights = seen[:3] + seen_cores[:2] + [swapped, far3, far4, near3, near4]
+        rights = seen[:2] + [there[2]] + seen_cores[:2] + [swapped, far3, far4, near3, near4, right[2]]
         picks = {}
-        for k, last in ((2, 6), (4, 8)):
+        for k, last, third in ((2, 6, 2), (4, 8, 10)):
             lane_low = [(0, 0), (1, 0), (last + 1, 0), (1, 3 * w)]
             other_low = [(last, 0), (last, n), (last + 1, 0), (last + 1, 2 * w)]
-            picks[k] = lower(other_low, j, 0, 0) + [whole((0, 1, 2, 5)[j], n, n)]
+            picks[k] = lower(other_low, j, 0, 0) + [whole((0, 1, third, 5)[j], n, n)]
             picks[k + 1] = lower(lane_low, j, 0, 0)
-            picks[k + 1] += [(v, j * w, w, True, n + i * w, 0) for i, v in enumerate((3, 4, 5, 2))]
+            picks[k + 1] += [(v, j * w, w, True, n + i * w, 0) for i, v in enumerate((3, 4, 5, third))]
         used = sorted({entry[0] for pieces in picks.values() for entry in pieces})
         picks = {r: [[(used.index(e[0]),) + e[1:] for e in v]] for r, v in picks.items()}
         return product(roles, left, [rights[i] for i in used], picks, w, base=base, halves=2, fetch=True, negate=True)

time: 528 us -> 528 us (level)
  no operation moved by 1% of the time
where the time goes in v5:
time: 528 us; the launch traced here: 522 us
  waiting for transfers between devices  228 us (43%)
  Pallas kernels  142 us (27%)
  starting transfers between devices  91.8 us (17%)
  other arithmetic  39.7 us (8%)
  local copies, waits for them, and re-layouts  19.2 us (4%)
    ppermute x36, waiting for transfers between devices, send(): return lax.ppermute(value, AXES, pairs)  228 us
    pallas_call x13, Pallas kernels, product(): pl.pallas_call(body, grid_spec=pltpu.PrefetchScalarGridSpec(num_scalar_pr...  130 us
    ppermute x36, starting transfers between devices, send(): return lax.ppermute(value, AXES, pairs)  91.8 us
    pallas_call x2, Pallas kernels, place(): pl.pallas_call(place_kernel, grid_spec=pltpu.PrefetchScalarGridSpec(num_s...  12 us
  transfers between devices with their start and end apart: 36, of which 12 were waited for; matrix products, arithmetic and copies ran while one was open for 7% of the time, Pallas kernels for 26%

profile of v5, /device:TPU:16, one launch (start us, length us, event | category | flops | bytes accessed | tf_op | source)
XLA Modules:
  0.0 522.2 jit_solution(9977679334989827646)
XLA Ops:
  0.0 6.4 %dynamic-slice_bitcast_fusion.3 = (f32[2,512,512]{2,1,0:T(8,128)S(1)}, f32[2,512,512]{2,1,0:T(8,128)S(1)}, f32[2,512,512]{2,1,0:T(8,128)}, f32[2,512,512]{2,1,0:T(8,128)S(1)}) fusion(f32[2,2,512,1024]{3,2,1,0:T(8,128)} %param.1, s32[]{:T(128)S(6)} %select_n.129, s32[]{:T(128)S(6)} %select_n.131, s32[]{:T(128)S(6)} %select_n.133, s32[]{:T(128)S(6)} %select_n.134, ...), kind=kLoop, calls=%fused_computation.23 | loop fusion | bytes 16777240 | tf_op jit(solution)/shard_map/squeeze | solution.py:304
  7.9 45.9 %collective-permute-done = f32[2,512,512]{2,1,0:T(8,128)S(1)} collective-permute-done((f32[2,512,512]{2,1,0:T(8,128)S(1)}, f32[2,512,512]{2,1,0:T(8,128)S(1)}, u32[]{:S(2)}, u32[]{:S(2)}) %collective-permute-start) | collective-permute-done | bytes 2097184 | tf_op jit(solution)/shard_map/ppermute | solution.py:277
  54.0 2.4 fusion.3
  56.4 3.7 pad_maximum_fusion.2
  60.0 2.6 pad_maximum_fusion.refs_0_.refs_6_.refs_1_
  62.7 2.4 collective-permute-start.3
  66.6 6.2 %collective-permute-start.2 = (f32[2,1024,256]{2,1,0:T(8,128)}, f32[2,1024,256]{2,1,0:T(8,128)}, u32[]{:S(2)}, u32[]{:S(2)}) collective-permute-start(f32[2,1024,256]{2,1,0:T(8,128)} %get-tuple-element.110), channel_id=1, source_target_pairs={{2,0},{3,1},{6,4},{7,5},{8,16},{9,17},{10,8},{11,9},{12,20},{13,21... | collective-permute-start | bytes 6291464 | tf_op jit(solution)/shard_map/ppermute | solution.py:277
  72.9 1.5 slice.46
  74.4 39.0 %collective-permute-done.1 = f32[2,512,512]{2,1,0:T(8,128)} collective-permute-done((f32[2,512,512]{2,1,0:T(8,128)}, f32[2,512,512]{2,1,0:T(8,128)}, u32[]{:S(2)}, u32[]{:S(2)}) %collective-permute-start.1) | collective-permute-done | bytes 2097184 | tf_op jit(solution)/shard_map/ppermute | solution.py:277
  117.1 4.2 pad_maximum_fusion.1.refs_1_.refs_7_.refs_2_
  121.3 4.6 fusion.1
  126.0 3.6 collective-permute-start.5
  129.6 2.8 collective-permute-start.6
  132.4 2.0 collective-permute-start.9
  134.3 2.1 collective-permute-start.8
  136.5 16.9 %shard_map.17 = (f32[2,1024,1024]{2,1,0:T(8,128)}, bf16[6,1024,2048]{2,1,0:T(8,128)(2,1)}) custom-call(s32[1]{0:T(128)} %bitcast.role_ref, f32[2,1024,512]{2,1,0:T(8,128)} %pad_maximum_fusion.refs_0_.refs_6_.refs_1_, f32[2,1024,512]{2,1,0:T(8,128)} %pad_maximum_fusion.1.refs_1_.refs_7_.refs_2_, f32[2,1024,512]{2,1,0:T(8,128)} %collective-permute-done.4.refs_2_.refs_4_, ...), custom_call_target="tpu_custom_call" | custom-call | flops 1000 | bytes 1000 | tf_op jit(solution)/shard_map/pallas_call | solution.py:181
  153.4 21.9 %collective-permute-done.5.refs_2_.refs_8_ = f32[2,1024,256]{2,1,0:T(8,128)S(1)} collective-permute-done((f32[2,1024,256]{2,1,0:T(8,128)}, f32[2,1024,256]{2,1,0:T(8,128)S(1)}, u32[]{:S(2)}, u32[]{:S(2)}) %collective-permute-start.5) | collective-permute-done | bytes 2097184 | tf_op jit(solution)/shard_map/ppermute | solution.py:277
  175.3 4.2 collective-permute-done.6.refs_1_.refs_5_
  179.5 2.0 broadcast_select_fusion.2.refs_1_
  181.8 4.0 slice_select_fusion
  185.7 8.8 %collective-permute-start.11 = (f32[2,1024,256]{2,1,0:T(8,128)}, f32[2,1024,256]{2,1,0:T(8,128)S(1)}, u32[]{:S(2)}, u32[]{:S(2)}) collective-permute-start(f32[2,1024,256]{2,1,0:T(8,128)} %slice_select_fusion), channel_id=1, source_target_pairs={{2,0},{3,1},{6,4},{7,5},{8,16},{9,17},{10,8},{11,9},{12,20},{13,21... | collective-permute-start | bytes 6291464 | tf_op jit(solution)/shard_map/ppermute | solution.py:277
  194.6 5.9 %collective-permute-start.10 = (f32[2,1024,256]{2,1,0:T(8,128)}, f32[2,1024,256]{2,1,0:T(8,128)}, u32[]{:S(2)}, u32[]{:S(2)}) collective-permute-start(f32[2,1024,256]{2,1,0:T(8,128)} %collective-permute-done.6.refs_1_.refs_5_), channel_id=1, source_target_pairs={{0,8},{1,9},{4,12},{5,13},{8,0},{9,1},{10,2},{11,3},{12,4},{13,5},... | collective-permute-start | bytes 6291464 | tf_op jit(solution)/shard_map/ppermute | solution.py:277
  200.5 2.4 collective-permute-start.12
  203.0 4.9 shard_map.19
  207.9 3.9 shard_map.18.refs_12_
  211.8 3.2 broadcast_select_fusion
  215.0 25.6 %collective-permute-done.11.refs_1_.refs_0_.refs_4_.refs_8_.refs_9_.refs_11_ = f32[2,1024,256]{2,1,0:T(8,128)S(1)} collective-permute-done((f32[2,1024,256]{2,1,0:T(8,128)}, f32[2,1024,256]{2,1,0:T(8,128)S(1)}, u32[]{:S(2)}, u32[]{:S(2)}) %collective-permute-start.11) | collective-permute-done | bytes 2097184 | tf_op jit(solution)/shard_map/ppermute | solution.py:277
  240.6 1.6 collective-permute-done.10.refs_2_.refs_9_
  242.2 3.2 broadcast_select_fusion.1.refs_2_
  246.8 12.7 %collective-permute-start.15 = (f32[2,1024,256]{2,1,0:T(8,128)}, f32[2,1024,256]{2,1,0:T(8,128)}, u32[]{:S(2)}, u32[]{:S(2)}) collective-permute-start(f32[2,1024,256]{2,1,0:T(8,128)} %broadcast_select_fusion), channel_id=1, source_target_pairs={{0,2},{1,3},{2,0},{3,1},{4,6},{5,7},{6,4},{7,5},{8,10},{9,11},{10,... | collective-permute-start | bytes 6291464 | tf_op jit(solution)/shard_map/ppermute | solution.py:277
  259.5 1.7 collective-permute-start.14
  261.2 2.0 collective-permute-start.18
  263.2 5.0 shard_map.20
  268.2 2.8 broadcast_select_fusion.3
  271.0 3.7 shard_map.21.refs_8_
  274.6 31.0 %collective-permute-done.15.refs_1_.refs_5_.refs_9_ = f32[2,1024,256]{2,1,0:T(8,128)} collective-permute-done((f32[2,1024,256]{2,1,0:T(8,128)}, f32[2,1024,256]{2,1,0:T(8,128)}, u32[]{:S(2)}, u32[]{:S(2)}) %collective-permute-start.15) | collective-permute-done | bytes 2097184 | tf_op jit(solution)/shard_map/ppermute | solution.py:277
  306.2 2.0 select_select_fusion
  308.2 4.6 collective-permute-start.23
  312.9 2.0 collective-permute-start.19
  317.5 5.1 shard_map.22
  324.0 4.3 shard_map.23
  328.3 25.0 %collective-permute-done.23.refs_6_.refs_7_ = f32[2,1792,256]{2,1,0:T(8,128)S(1)} collective-permute-done((f32[2,1792,256]{2,1,0:T(8,128)}, f32[2,1792,256]{2,1,0:T(8,128)S(1)}, u32[]{:S(2)}, u32[]{:S(2)}) %collective-permute-start.23) | collective-permute-done | bytes 3670048 | tf_op jit(solution)/shard_map/ppermute | solution.py:277
  353.3 1.8 copy-done.10
  355.0 19.4 %shard_map.24 = (f32[2,512,256]{2,1,0:T(8,128)}, f32[2,512,256]{2,1,0:T(8,128)}) custom-call(s32[1]{0:T(128)} %bitcast.role_ref, bf16[6,1024,2048]{2,1,0:T(8,128)(2,1)} %get-tuple-element.127.refs_0_, f32[2,1024,256]{2,1,0:T(8,128)} %copy-done.11, f32[2,1024,256]{2,1,0:T(8,128)} %copy-done.8, ...), custom_call_target="tpu_custom_call" | custom-call | flops 1000 | bytes 1000 | tf_op jit(solution)/shard_map/pallas_call | solution.py:181
  375.5 2.0 collective-permute-start.24
  377.5 2.0 collective-permute-start.25
  380.8 3.4 collective-permute-start.26
  384.2 5.5 %collective-permute-start.28 = (f32[2,768,256]{2,1,0:T(8,128)}, f32[2,768,256]{2,1,0:T(8,128)}, u32[]{:S(2)}, u32[]{:S(2)}) collective-permute-start(f32[2,768,256]{2,1,0:T(8,128)} %collective-permute-done.21.refs_10_), channel_id=1, source_target_pairs={{10,2},{11,3},{14,6},{15,7},{16,24},{17,25},{20,28},{21,29}} | collective-permute-start | bytes 4718600 | tf_op jit(solution)/shard_map/ppermute | solution.py:277
  389.6 5.0 shard_map.25
  394.6 19.0 %shard_map.26 = (f32[2,512,256]{2,1,0:T(8,128)}, f32[2,512,256]{2,1,0:T(8,128)}) custom-call(s32[1]{0:T(128)} %bitcast.role_ref, bf16[6,1024,2048]{2,1,0:T(8,128)(2,1)} %get-tuple-element.127.refs_0_, f32[2,1024,256]{2,1,0:T(8,128)} %copy-done.11, f32[2,1024,256]{2,1,0:T(8,128)} %broadcast_select_fusion.1.refs_2_, f32[2,1024,256]{2,1,0:T(8,128)} %copy-done.8, ...), custom_call_target="tpu_custom_call" | custom-call | flops 1000 | bytes 1000 | tf_op jit(solution)/shard_map/pallas_call | solution.py:181
  413.7 2.4 collective-permute-start.29
  417.4 4.6 shard_map.27
  422.1 16.2 %collective-permute-done.27.refs_12_ = f32[2,1024,256]{2,1,0:T(8,128)} collective-permute-done((f32[2,1024,256]{2,1,0:T(8,128)}, f32[2,1024,256]{2,1,0:T(8,128)}, u32[]{:S(2)}, u32[]{:S(2)}) %collective-permute-start.27) | collective-permute-done | bytes 2097184 | tf_op jit(solution)/shard_map/ppermute | solution.py:277
  438.3 19.3 %shard_map.28 = (f32[2,512,256]{2,1,0:T(8,128)}, f32[2,512,256]{2,1,0:T(8,128)}) custom-call(s32[1]{0:T(128)} %bitcast.role_ref, bf16[6,1024,2048]{2,1,0:T(8,128)(2,1)} %get-tuple-element.127.refs_0_, f32[2,1024,256]{2,1,0:T(8,128)} %copy-done.11, f32[2,1024,256]{2,1,0:T(8,128)} %broadcast_select_fusion.1.refs_2_, f32[2,1024,256]{2,1,0:T(8,128)} %copy-done.8, ...), custom_call_target="tpu_custom_call" | custom-call | flops 1000 | bytes 1000 | tf_op jit(solution)/shard_map/pallas_call | solution.py:181
  457.6 2.1 copy-done.1
  459.7 2.4 collective-permute-start.34
  463.8 19.0 %shard_map.29 = (f32[2,512,256]{2,1,0:T(8,128)}, f32[2,512,256]{2,1,0:T(8,128)}) custom-call(s32[1]{0:T(128)} %bitcast.role_ref, bf16[6,1024,2048]{2,1,0:T(8,128)(2,1)} %get-tuple-element.127.refs_0_, f32[2,1024,256]{2,1,0:T(8,128)} %copy-done.11, f32[2,1024,256]{2,1,0:T(8,128)} %broadcast_select_fusion.1.refs_2_, f32[2,1024,256]{2,1,0:T(8,128)} %copy-done.8, ...), custom_call_target="tpu_custom_call" | custom-call | flops 1000 | bytes 1000 | tf_op jit(solution)/shard_map/pallas_call | solution.py:181
  482.7 3.1 collective-permute-done.34.refs_6_
  485.8 3.6 slice_subtract_fusion
  489.4 2.4 collective-permute-start.35
  491.9 2.2 copy-done.3
  495.3 4.8 shard_map.30.refs_8_
  500.2 14.3 %collective-permute-done.35.refs_7_ = f32[2,512,256]{2,1,0:T(8,128)S(1)} collective-permute-done((f32[2,512,256]{2,1,0:T(8,128)}, f32[2,512,256]{2,1,0:T(8,128)S(1)}, u32[]{:S(2)}, u32[]{:S(2)}) %collective-permute-start.35) | collective-permute-done | bytes 1048608 | tf_op jit(solution)/shard_map/ppermute | solution.py:277
  514.4 7.2 %shard_map.31 = f32[2,2,512,1024]{3,2,1,0:T(8,128)} custom-call(s32[2]{0:T(128)S(1)} %pad_add_fusion.role_ref, f32[2,512,1024]{2,1,0:T(8,128)S(1)} %copy-done.2, f32[1,512,1024]{2,1,0:T(8,128)S(1)} %collective-permute-done.31.refs_1_.refs_2_, f32[1,512,1024]{2,1,0:T(8,128)S(1)} %collective-permute-done.31.refs_1_.refs_2_, ...), custom_call_target="tpu_custom_call", output_to_operand_aliasing={{}: (9, {})} | custom-call | flops 1000 | bytes 1000 | tf_op jit(solution)/shard_map/pallas_call | solution.py:240
  (72 shorter events, 19.7 us)
Async XLA Ops:
  6.4 47.4 %collective-permute-start = (f32[2,512,512]{2,1,0:T(8,128)S(1)}, f32[2,512,512]{2,1,0:T(8,128)S(1)}, u32[]{:S(2)}, u32[]{:S(2)}) collective-permute-start(f32[2,512,512]{2,1,0:T(8,128)S(1)} %get-tuple-element.214), channel_id=1, source_target_pairs={{0,4},{1,5},{2,6},{3,7},{4,0},{5,1},{6,2},{7,3},{8,12},{9,13},{10,... | collective-permute-start | bytes 6291464 | tf_op jit(solution)/shard_map/ppermute | solution.py:277
  62.7 63.2 %collective-permute-start.4 = (f32[2,1024,512]{2,1,0:T(8,128)}, f32[2,1024,512]{2,1,0:T(8,128)}, u32[]{:S(2)}, u32[]{:S(2)}) collective-permute-start(f32[2,1024,512]{2,1,0:T(8,128)} %pad_maximum_fusion.refs_0_.refs_6_.refs_1_), channel_id=1, source_target_pairs={{0,1},{1,0},{2,3},{3,2},{4,5},{5,4},{6,7},{7,6},{8,9},{9,8},{10,11... | collective-permute-start | bytes 12582920 | tf_op jit(solution)/shard_map/ppermute | solution.py:277
  62.7 63.2 %collective-permute-start.3 = (f32[2,1792,256]{2,1,0:T(8,128)}, f32[2,1792,256]{2,1,0:T(8,128)}, u32[]{:S(2)}, u32[]{:S(2)}) collective-permute-start(f32[2,1792,256]{2,1,0:T(8,128)} %pad_maximum_fusion.2), channel_id=1, source_target_pairs={{0,8},{4,12},{9,1},{13,5},{18,26},{22,30},{27,19},{31,23}} | collective-permute-start | bytes 11010056 | tf_op jit(solution)/shard_map/ppermute | solution.py:277
  65.1 48.4 %collective-permute-start.1 = (f32[2,512,512]{2,1,0:T(8,128)}, f32[2,512,512]{2,1,0:T(8,128)}, u32[]{:S(2)}, u32[]{:S(2)}) collective-permute-start(f32[2,512,512]{2,1,0:T(8,128)} %get-tuple-element.108), channel_id=1, source_target_pairs={{0,4},{1,5},{2,6},{3,7},{4,0},{5,1},{6,2},{7,3},{8,12},{9,13},{10,... | collective-permute-start | bytes 6291464 | tf_op jit(solution)/shard_map/ppermute | solution.py:277
  66.6 59.3 %collective-permute-start.2 = (f32[2,1024,256]{2,1,0:T(8,128)}, f32[2,1024,256]{2,1,0:T(8,128)}, u32[]{:S(2)}, u32[]{:S(2)}) collective-permute-start(f32[2,1024,256]{2,1,0:T(8,128)} %get-tuple-element.110), channel_id=1, source_target_pairs={{2,0},{3,1},{6,4},{7,5},{8,16},{9,17},{10,8},{11,9},{12,20},{13,21... | collective-permute-start | bytes 6291464 | tf_op jit(solution)/shard_map/ppermute | solution.py:277
  117.1 4.2 copy-start.13
  125.9 10.6 %collective-permute-start.7 = (f32[2,1024,512]{2,1,0:T(8,128)}, f32[2,1024,512]{2,1,0:T(8,128)}, u32[]{:S(2)}, u32[]{:S(2)}) collective-permute-start(f32[2,1024,512]{2,1,0:T(8,128)} %pad_maximum_fusion.1.refs_1_.refs_7_.refs_2_), channel_id=1, source_target_pairs={{0,1},{1,0},{2,3},{3,2},{4,5},{5,4},{6,7},{7,6},{8,9},{9,8},{10,11... | collective-permute-start | bytes 12582920 | tf_op jit(solution)/shard_map/ppermute | solution.py:277
  126.0 49.3 %collective-permute-start.5 = (f32[2,1024,256]{2,1,0:T(8,128)}, f32[2,1024,256]{2,1,0:T(8,128)S(1)}, u32[]{:S(2)}, u32[]{:S(2)}) collective-permute-start(f32[2,1024,256]{2,1,0:T(8,128)} %collective-permute-done.2.refs_1_.refs_0_.refs_4_), channel_id=1, source_target_pairs={{0,8},{1,9},{4,12},{5,13},{8,0},{9,1},{10,2},{11,3},{12,4},{13,5},... | collective-permute-start | bytes 6291464 | tf_op jit(solution)/shard_map/ppermute | solution.py:277
  129.6 49.9 %collective-permute-start.6 = (f32[2,1024,256]{2,1,0:T(8,128)}, f32[2,1024,256]{2,1,0:T(8,128)}, u32[]{:S(2)}, u32[]{:S(2)}) collective-permute-start(f32[2,1024,256]{2,1,0:T(8,128)} %get-tuple-element.114), channel_id=1, source_target_pairs={{2,0},{3,1},{6,4},{7,5},{8,16},{9,17},{10,8},{11,9},{12,20},{13,21... | collective-permute-start | bytes 6291464 | tf_op jit(solution)/shard_map/ppermute | solution.py:277
  132.4 53.4 %collective-permute-start.9 = (f32[2,1024,256]{2,1,0:T(8,128)}, f32[2,1024,256]{2,1,0:T(8,128)}, u32[]{:S(2)}, u32[]{:S(2)}) collective-permute-start(f32[2,1024,256]{2,1,0:T(8,128)} %collective-permute-done.2.refs_1_.refs_0_.refs_4_), channel_id=1, source_target_pairs={{0,1},{1,0},{4,5},{5,4},{8,9},{9,8},{12,13},{13,12},{18,19},{19,18... | collective-permute-start | bytes 6291464 | tf_op jit(solution)/shard_map/ppermute | solution.py:277
  134.3 51.4 %collective-permute-start.8 = (f32[2,768,256]{2,1,0:T(8,128)}, f32[2,768,256]{2,1,0:T(8,128)}, u32[]{:S(2)}, u32[]{:S(2)}) collective-permute-start(f32[2,768,256]{2,1,0:T(8,128)} %pad_maximum_fusion.3), channel_id=1, source_target_pairs={{0,8},{4,12},{9,1},{13,5},{18,26},{22,30},{27,19},{31,23}} | collective-permute-start | bytes 4718600 | tf_op jit(solution)/shard_map/ppermute | solution.py:277
  175.3 4.2 copy-start.12
  179.5 2.2 copy-start.14
  181.8 21.2 %copy-start.11 = (f32[2,1024,256]{2,1,0:T(8,128)}, f32[2,1024,256]{2,1,0:T(8,128)S(1)}, u32[]{:S(2)}) copy-start(f32[2,1024,256]{2,1,0:T(8,128)S(1)} %broadcast_select_fusion.2.refs_1_) | copy-start | bytes 6291460
  185.7 54.8 %collective-permute-start.11 = (f32[2,1024,256]{2,1,0:T(8,128)}, f32[2,1024,256]{2,1,0:T(8,128)S(1)}, u32[]{:S(2)}, u32[]{:S(2)}) collective-permute-start(f32[2,1024,256]{2,1,0:T(8,128)} %slice_select_fusion), channel_id=1, source_target_pairs={{2,0},{3,1},{6,4},{7,5},{8,16},{9,17},{10,8},{11,9},{12,20},{13,21... | collective-permute-start | bytes 6291464 | tf_op jit(solution)/shard_map/ppermute | solution.py:277
  194.6 47.6 %collective-permute-start.10 = (f32[2,1024,256]{2,1,0:T(8,128)}, f32[2,1024,256]{2,1,0:T(8,128)}, u32[]{:S(2)}, u32[]{:S(2)}) collective-permute-start(f32[2,1024,256]{2,1,0:T(8,128)} %collective-permute-done.6.refs_1_.refs_5_), channel_id=1, source_target_pairs={{0,8},{1,9},{4,12},{5,13},{8,0},{9,1},{10,2},{11,3},{12,4},{13,5},... | collective-permute-start | bytes 6291464 | tf_op jit(solution)/shard_map/ppermute | solution.py:277
  200.5 44.9 %collective-permute-start.12 = (f32[2,1024,256]{2,1,0:T(8,128)}, f32[2,1024,256]{2,1,0:T(8,128)}, u32[]{:S(2)}, u32[]{:S(2)}) collective-permute-start(f32[2,1024,256]{2,1,0:T(8,128)} %collective-permute-done.6.refs_1_.refs_5_), channel_id=1, source_target_pairs={{0,1},{1,0},{4,5},{5,4},{8,9},{9,8},{12,13},{13,12},{18,19},{19,18... | collective-permute-start | bytes 6291464 | tf_op jit(solution)/shard_map/ppermute | solution.py:277
  202.9 42.5 %collective-permute-start.13 = (f32[2,1024,256]{2,1,0:T(8,128)S(1)}, f32[2,1024,256]{2,1,0:T(8,128)}, u32[]{:S(2)}, u32[]{:S(2)}) collective-permute-start(f32[2,1024,256]{2,1,0:T(8,128)S(1)} %broadcast_select_fusion.2.refs_1_), channel_id=1, source_target_pairs={{0,1},{1,0},{2,3},{3,2},{4,5},{5,4},{6,7},{7,6},{8,9},{9,8},{10,11... | collective-permute-start | bytes 6291464 | tf_op jit(solution)/shard_map/ppermute | solution.py:277
  240.6 65.6 %copy-start.7 = (f32[2,1024,256]{2,1,0:T(8,128)}, f32[2,1024,256]{2,1,0:T(8,128)S(1)}, u32[]{:S(2)}) copy-start(f32[2,1024,256]{2,1,0:T(8,128)S(1)} %collective-permute-done.11.refs_1_.refs_0_.refs_4_.refs_8_.refs_9_.refs_11_) | copy-start | bytes 6291460
  245.4 62.8 %collective-permute-start.17 = (f32[2,1792,256]{2,1,0:T(8,128)}, f32[2,1792,256]{2,1,0:T(8,128)}, u32[]{:S(2)}, u32[]{:S(2)}) collective-permute-start(f32[2,1792,256]{2,1,0:T(8,128)} %collective-permute-done.3.refs_3_), channel_id=1, source_target_pairs={{8,16},{12,20},{19,11},{23,15}} | collective-permute-start | bytes 11010056 | tf_op jit(solution)/shard_map/ppermute | solution.py:277
  246.7 24.3 %collective-permute-start.16 = (f32[2,1024,256]{2,1,0:T(8,128)}, f32[2,1024,256]{2,1,0:T(8,128)}, u32[]{:S(2)}, u32[]{:S(2)}) collective-permute-start(f32[2,1024,256]{2,1,0:T(8,128)} %broadcast_select_fusion.1.refs_2_), channel_id=1, source_target_pairs={{0,1},{1,0},{2,3},{3,2},{4,5},{5,4},{6,7},{7,6},{8,9},{9,8},{10,11... | collective-permute-start | bytes 6291464 | tf_op jit(solution)/shard_map/ppermute | solution.py:277
  246.8 58.8 %collective-permute-start.15 = (f32[2,1024,256]{2,1,0:T(8,128)}, f32[2,1024,256]{2,1,0:T(8,128)}, u32[]{:S(2)}, u32[]{:S(2)}) collective-permute-start(f32[2,1024,256]{2,1,0:T(8,128)} %broadcast_select_fusion), channel_id=1, source_target_pairs={{0,2},{1,3},{2,0},{3,1},{4,6},{5,7},{6,4},{7,5},{8,10},{9,11},{10,... | collective-permute-start | bytes 6291464 | tf_op jit(solution)/shard_map/ppermute | solution.py:277
  259.5 46.6 %collective-permute-start.14 = (f32[2,1024,256]{2,1,0:T(8,128)S(1)}, f32[2,1024,256]{2,1,0:T(8,128)S(1)}, u32[]{:S(2)}, u32[]{:S(2)}) collective-permute-start(f32[2,1024,256]{2,1,0:T(8,128)S(1)} %collective-permute-done.11.refs_1_.refs_0_.refs_4_.refs_8_.refs_9_.refs_11_), channel_id=1, source_target_pairs={{0,8},{1,9},{4,12},{5,13},{8,0},{9,1},{10,2},{11,3},{12,4},{13,5},... | collective-permute-start | bytes 6291464 | tf_op jit(solution)/shard_map/ppermute | solution.py:277
  261.2 47.0 %collective-permute-start.18 = (f32[2,1024,256]{2,1,0:T(8,128)S(1)}, f32[2,1024,256]{2,1,0:T(8,128)}, u32[]{:S(2)}, u32[]{:S(2)}) collective-permute-start(f32[2,1024,256]{2,1,0:T(8,128)S(1)} %collective-permute-done.11.refs_1_.refs_0_.refs_4_.refs_8_.refs_9_.refs_11_), channel_id=1, source_target_pairs={{0,1},{1,0},{4,5},{5,4},{8,9},{9,8},{12,13},{13,12},{18,19},{19,18... | collective-permute-start | bytes 6291464 | tf_op jit(solution)/shard_map/ppermute | solution.py:277
  306.2 2.0 copy-start.8
  308.2 45.1 %collective-permute-start.23 = (f32[2,1792,256]{2,1,0:T(8,128)}, f32[2,1792,256]{2,1,0:T(8,128)S(1)}, u32[]{:S(2)}, u32[]{:S(2)}) collective-permute-start(f32[2,1792,256]{2,1,0:T(8,128)} %collective-permute-done.17.refs_7_.refs_8_.refs_9_), channel_id=1, source_target_pairs={{11,3},{15,7},{16,24},{20,28}} | collective-permute-start | bytes 11010056 | tf_op jit(solution)/shard_map/ppermute | solution.py:277
  312.8 9.8 %collective-permute-start.22 = (f32[2,1024,256]{2,1,0:T(8,128)}, f32[2,1024,256]{2,1,0:T(8,128)S(1)}, u32[]{:S(2)}, u32[]{:S(2)}) collective-permute-start(f32[2,1024,256]{2,1,0:T(8,128)} %select_select_fusion), channel_id=1, source_target_pairs={{0,1},{1,0},{2,3},{3,2},{4,5},{5,4},{6,7},{7,6},{8,9},{9,8},{10,11... | collective-permute-start | bytes 6291464 | tf_op jit(solution)/shard_map/ppermute | solution.py:277
  312.9 61.6 %collective-permute-start.19 = (f32[2,1024,256]{2,1,0:T(8,128)}, f32[2,1024,256]{2,1,0:T(8,128)}, u32[]{:S(2)}, u32[]{:S(2)}) collective-permute-start(f32[2,1024,256]{2,1,0:T(8,128)} %collective-permute-done.15.refs_1_.refs_5_.refs_9_), channel_id=1, source_target_pairs={{0,8},{1,9},{4,12},{5,13},{8,0},{9,1},{12,4},{13,5},{18,26},{19,27... | collective-permute-start | bytes 6291464 | tf_op jit(solution)/shard_map/ppermute | solution.py:277
  314.9 59.6 %collective-permute-start.20 = (f32[2,1024,256]{2,1,0:T(8,128)}, f32[2,1024,256]{2,1,0:T(8,128)}, u32[]{:S(2)}, u32[]{:S(2)}) collective-permute-start(f32[2,1024,256]{2,1,0:T(8,128)} %shard_map.20), channel_id=1, source_target_pairs={{0,2},{1,3},{4,6},{5,7},{8,10},{9,11},{12,14},{13,15},{18,16},{19,... | collective-permute-start | bytes 6291464 | tf_op jit(solution)/shard_map/ppermute | solution.py:277
  316.2 58.3 %collective-permute-start.21 = (f32[2,768,256]{2,1,0:T(8,128)}, f32[2,768,256]{2,1,0:T(8,128)}, u32[]{:S(2)}, u32[]{:S(2)}) collective-permute-start(f32[2,768,256]{2,1,0:T(8,128)} %broadcast_select_fusion.3), channel_id=1, source_target_pairs={{8,16},{9,17},{12,20},{13,21},{18,10},{19,11},{22,14},{23,15}} | collective-permute-start | bytes 4718600 | tf_op jit(solution)/shard_map/ppermute | solution.py:277
  322.6 1.4 copy-start.9
  353.3 1.8 copy-start.10
  374.5 83.1 %collective-permute-start.30 = (f32[2,512,1024]{2,1,0:T(8,128)}, f32[2,512,1024]{2,1,0:T(8,128)S(1)}, u32[]{:S(2)}, u32[]{:S(2)}) collective-permute-start(f32[2,512,1024]{2,1,0:T(8,128)} %get-tuple-element.191), channel_id=1, source_target_pairs={{0,4},{4,0},{9,13},{13,9},{18,22},{22,18},{27,31},{31,27}} | collective-permute-start | bytes 12582920 | tf_op jit(solution)/shard_map/ppermute | solution.py:277
  375.5 8.7 %collective-permute-start.24 = (f32[2,1024,256]{2,1,0:T(8,128)}, f32[2,1024,256]{2,1,0:T(8,128)}, u32[]{:S(2)}, u32[]{:S(2)}) collective-permute-start(f32[2,1024,256]{2,1,0:T(8,128)} %copy-done.8), channel_id=1, source_target_pairs={{0,1},{1,0},{4,5},{5,4},{8,9},{9,8},{12,13},{13,12},{18,19},{19,18... | collective-permute-start | bytes 6291464 | tf_op jit(solution)/shard_map/ppermute | solution.py:277
  377.5 17.1 %collective-permute-start.25 = (f32[2,1024,256]{2,1,0:T(8,128)}, f32[2,1024,256]{2,1,0:T(8,128)}, u32[]{:S(2)}, u32[]{:S(2)}) collective-permute-start(f32[2,1024,256]{2,1,0:T(8,128)} %collective-permute-done.19.refs_2_.refs_5_), channel_id=1, source_target_pairs={{0,1},{1,0},{4,5},{5,4},{8,9},{9,8},{12,13},{13,12},{18,19},{19,18... | collective-permute-start | bytes 6291464 | tf_op jit(solution)/shard_map/ppermute | solution.py:277
  379.5 58.9 %collective-permute-start.27 = (f32[2,1024,256]{2,1,0:T(8,128)}, f32[2,1024,256]{2,1,0:T(8,128)}, u32[]{:S(2)}, u32[]{:S(2)}) collective-permute-start(f32[2,1024,256]{2,1,0:T(8,128)} %shard_map.22), channel_id=1, source_target_pairs={{0,2},{1,3},{4,6},{5,7},{8,10},{9,11},{12,14},{13,15},{18,16},{19,... | collective-permute-start | bytes 6291464 | tf_op jit(solution)/shard_map/ppermute | solution.py:277
  380.8 32.9 %collective-permute-start.26 = (f32[2,512,256]{2,1,0:T(8,128)}, f32[2,512,256]{2,1,0:T(8,128)S(1)}, u32[]{:S(2)}, u32[]{:S(2)}) collective-permute-start(f32[2,512,256]{2,1,0:T(8,128)} %get-tuple-element.181), channel_id=1, source_target_pairs={{2,6},{3,7},{6,2},{7,3},{10,14},{11,15},{14,10},{15,11},{16,20},{1... | collective-permute-start | bytes 3145736 | tf_op jit(solution)/shard_map/ppermute | solution.py:277
  384.2 37.9 %collective-permute-start.28 = (f32[2,768,256]{2,1,0:T(8,128)}, f32[2,768,256]{2,1,0:T(8,128)}, u32[]{:S(2)}, u32[]{:S(2)}) collective-permute-start(f32[2,768,256]{2,1,0:T(8,128)} %collective-permute-done.21.refs_10_), channel_id=1, source_target_pairs={{10,2},{11,3},{14,6},{15,7},{16,24},{17,25},{20,28},{21,29}} | collective-permute-start | bytes 4718600 | tf_op jit(solution)/shard_map/ppermute | solution.py:277
  413.7 43.9 %collective-permute-start.29 = (f32[2,512,256]{2,1,0:T(8,128)}, f32[2,512,256]{2,1,0:T(8,128)}, u32[]{:S(2)}, u32[]{:S(2)}) collective-permute-start(f32[2,512,256]{2,1,0:T(8,128)} %get-tuple-element.190), channel_id=1, source_target_pairs={{2,6},{3,7},{6,2},{7,3},{10,14},{11,15},{14,10},{15,11},{16,20},{1... | collective-permute-start | bytes 3145736 | tf_op jit(solution)/shard_map/ppermute | solution.py:277
  416.1 66.6 %collective-permute-start.33 = (f32[2,1024,256]{2,1,0:T(8,128)}, f32[2,1024,256]{2,1,0:T(8,128)}, u32[]{:S(2)}, u32[]{:S(2)}) collective-permute-start(f32[2,1024,256]{2,1,0:T(8,128)} %shard_map.25), channel_id=1, source_target_pairs={{0,2},{1,3},{4,6},{5,7},{8,10},{9,11},{12,14},{13,15},{18,16},{19,... | collective-permute-start | bytes 6291464 | tf_op jit(solution)/shard_map/ppermute | solution.py:277
  457.6 2.1 copy-start.1
  459.7 26.1 %collective-permute-start.34 = (f32[2,512,256]{2,1,0:T(8,128)}, f32[2,512,256]{2,1,0:T(8,128)}, u32[]{:S(2)}, u32[]{:S(2)}) collective-permute-start(f32[2,512,256]{2,1,0:T(8,128)} %get-tuple-element.201), channel_id=1, source_target_pairs={{2,6},{3,7},{6,2},{7,3},{10,14},{11,15},{14,10},{15,11},{16,20},{1... | collective-permute-start | bytes 3145736 | tf_op jit(solution)/shard_map/ppermute | solution.py:277
  462.1 38.0 %collective-permute-start.31 = (f32[1,512,1024]{2,1,0:T(8,128)}, f32[1,512,1024]{2,1,0:T(8,128)S(1)}, u32[]{:S(2)}, u32[]{:S(2)}) collective-permute-start(f32[1,512,1024]{2,1,0:T(8,128)} %get-tuple-element.193), channel_id=1, source_target_pairs={{1,5},{5,1},{8,12},{12,8},{19,23},{23,19},{26,30},{30,26}} | collective-permute-start | bytes 6291464 | tf_op jit(solution)/shard_map/ppermute | solution.py:277
  463.0 37.2 %collective-permute-start.32 = (f32[1,512,1024]{2,1,0:T(8,128)}, f32[1,512,1024]{2,1,0:T(8,128)S(1)}, u32[]{:S(2)}, u32[]{:S(2)}) collective-permute-start(f32[1,512,1024]{2,1,0:T(8,128)} %get-tuple-element.194), channel_id=1, source_target_pairs={{1,5},{5,1},{8,12},{12,8},{19,23},{23,19},{26,30},{30,26}} | collective-permute-start | bytes 6291464 | tf_op jit(solution)/shard_map/ppermute | solution.py:277
  485.8 6.1 %copy-start = (f32[2,512,1024]{2,1,0:T(8,128)S(1)}, f32[2,512,1024]{2,1,0:T(8,128)}, u32[]{:S(2)}) copy-start(f32[2,512,1024]{2,1,0:T(8,128)} %get-tuple-element.206.refs_1_.refs_2_.refs_3_) | copy-start | bytes 12582916
  485.8 6.1 %copy-start.4 = (f32[2,512,256]{2,1,0:T(8,128)S(1)}, f32[2,512,256]{2,1,0:T(8,128)}, u32[]{:S(2)}) copy-start(f32[2,512,256]{2,1,0:T(8,128)} %get-tuple-element.207.refs_4_) | copy-start | bytes 3145732
  485.8 6.1 %copy-start.5 = (f32[2,512,256]{2,1,0:T(8,128)S(1)}, f32[2,512,256]{2,1,0:T(8,128)}, u32[]{:S(2)}) copy-start(f32[2,512,256]{2,1,0:T(8,128)} %get-tuple-element.208.refs_5_) | copy-start | bytes 3145732
  489.4 25.0 %collective-permute-start.35 = (f32[2,512,256]{2,1,0:T(8,128)}, f32[2,512,256]{2,1,0:T(8,128)S(1)}, u32[]{:S(2)}, u32[]{:S(2)}) collective-permute-start(f32[2,512,256]{2,1,0:T(8,128)} %get-tuple-element.220), channel_id=1, source_target_pairs={{2,6},{3,7},{6,2},{7,3},{10,14},{11,15},{14,10},{15,11},{16,20},{1... | collective-permute-start | bytes 3145736 | tf_op jit(solution)/shard_map/ppermute | solution.py:277
  491.9 2.2 copy-start.3
  494.1 1.2 copy-start.6
  495.3 19.1 %copy-start.2 = (f32[2,512,1024]{2,1,0:T(8,128)S(1)}, f32[2,512,1024]{2,1,0:T(8,128)}, u32[]{:S(2)}) copy-start(f32[2,512,1024]{2,1,0:T(8,128)} %copy-done.1) | copy-start | bytes 12582916
